TPU v7x, 32 devices: a whole 2x2x4 slice. The times are simulated.
32 devices in a mesh: dp: 4 (over y, x), space: 8 (over z, core).
Axes of the slice: x: 2, y: 2, z: 4, core: 2. Of those that a mesh axis runs over, the one named last changes fastest.
Arguments:
- fields: bfloat16 [4, 32, 768, 128], P('dp', None, 'space'), may hold values from -6 to 6
- land_mask: int32 [768, 128], P('space'), may hold values from 0 to 1, as said below
- land_frac: float32 [768, 128], P('space'), may hold values from 0.05 to 1
- owner_map: int32 [1536], replicated, may hold values from 0 to 1535, as said below
- targets: float32 [4, 14, 1536], P('dp', None, 'space'), may hold values from -3 to 3
- conv_weight: bfloat16 [3, 3, 32, 128], replicated, may hold values from -0.375 to 0.375
- conv_bias: float32 [128], replicated, may hold values from -3 to 3
- mix_weight: bfloat16 [128, 128], replicated, may hold values from -0.5 to 0.5
- mix_bias: float32 [128], replicated, may hold values from -3 to 3
- out_weight: bfloat16 [128, 14], replicated, may hold values from -0.5 to 0.5
- out_bias: float32 [14], replicated, may hold values from -3 to 3
Outputs:
- coarse_pred: float32 [4, 14, 1536], P('dp', None, 'space')
- conv_grad: float32 [3, 3, 32, 128], replicated
- conv_bias_grad: float32 [128], replicated
- mix_grad: float32 [128, 128], replicated
- mix_bias_grad: float32 [128], replicated
- out_grad: float32 [128, 14], replicated
- out_bias_grad: float32 [14], replicated
- loss: float32 [], replicated
Inputs may be any that keep to these rules, and one draw needn't show every extreme that they name: A permutation. Coarse cell g is owned by index owner_map[g] // 192 of space, at local place owner_map[g] % 192; the 192 coarse cells of every strip go to every owner exactly 24 at a time. `land_mask`: 1 marks land.
All inputs are finite; a program needn't handle non-finite values.
Results may differ from a plain program's by a relative error of at most 0.00039.
Values may be sent and summed in bfloat16 or wider, within the bound.
No kernel may reach another device: no remote copies, remote signals or barrier semaphores. Data moves between devices by JAX's collectives and lax.ppermute only.
A program may use at most 128 MiB of HBM per device.

v0:
```python
import math

import jax
import jax.numpy as jnp
from jax import lax
from jax.sharding import PartitionSpec as P

SIDE = 8


CUBIC = 0.044715
ROOT_TWO_PI = math.sqrt(2.0 / math.pi)


def padded_2(block, sides, width):
    for axis, dim in sides:
        count = lax.axis_size(axis)
        forward = [(i, i + 1) for i in range(count - 1)]
        backward = [(target, source) for source, target in forward]
        low = lax.ppermute(
            lax.slice_in_dim(block, block.shape[dim] - width, None, axis=dim), axis, forward
        )
        high = lax.ppermute(lax.slice_in_dim(block, 0, width, axis=dim), axis, backward)
        block = jnp.concatenate([low, block, high], axis=dim)
    return block


def gelu_pair(pre):
    inner = ROOT_TWO_PI * (pre + CUBIC * pre * pre * pre)
    tanh_value = jnp.tanh(inner)
    value = 0.5 * pre * (1.0 + tanh_value)
    slope = 0.5 * (1.0 + tanh_value) + 0.5 * pre * (1.0 - tanh_value * tanh_value) * ROOT_TWO_PI * (
        1.0 + 3.0 * CUBIC * pre * pre
    )
    return (value, slope)


def product(form, left, right):
    return jnp.einsum(form, left, right, preferred_element_type=jnp.float32)


def block_sums(values, side):
    leading = values.shape[:-2]
    height, breadth = (values.shape[-2], values.shape[-1])
    shaped = values.reshape(leading + (height // side, side, breadth // side, side))
    return jnp.sum(shaped, axis=(-3, -1)).reshape(leading + (height // side * (breadth // side),))


def forward_tile(padded, conv_weight, conv_bias, mix_weight, mix_bias, out_weight, out_bias):
    height = padded.shape[2] - 2
    breadth = padded.shape[3] - 2
    pieces = [
        padded[:, :, row_shift : row_shift + height, col_shift : col_shift + breadth]
        for row_shift in range(3)
        for col_shift in range(3)
    ]
    stacked = jnp.concatenate(pieces, axis=1)
    flat_weight = conv_weight.reshape(-1, conv_weight.shape[3])
    pre_one = product("mkrc,kh->mrch", stacked, flat_weight) + conv_bias
    value_one, slope_one = gelu_pair(pre_one)
    hidden_one = value_one.astype(jnp.bfloat16)
    pre_two = product("mrch,hg->mrcg", hidden_one, mix_weight) + mix_bias
    value_two, slope_two = gelu_pair(pre_two)
    hidden_two = value_two.astype(jnp.bfloat16)
    raw = product("mrch,hp->mprc", hidden_two, out_weight) + out_bias[None, :, None, None]
    return (stacked, slope_one, hidden_one, slope_two, hidden_two, raw)


def backward_tile(
    stacked,
    slope_one,
    hidden_one,
    slope_two,
    hidden_two,
    raw,
    weight_map,
    d_block,
    mix_weight,
    out_weight,
    side,
):
    members, pools = (d_block.shape[0], d_block.shape[1])
    height, breadth = weight_map.shape
    d_cells = d_block.reshape(members, pools, height // side, breadth // side)
    d_cells = jnp.repeat(jnp.repeat(d_cells, side, axis=2), side, axis=3)
    d_raw = (d_cells * weight_map * jax.nn.sigmoid(raw)).astype(jnp.bfloat16)
    out_grad = product("mrch,mprc->hp", hidden_two, d_raw)
    out_bias_grad = jnp.sum(d_raw.astype(jnp.float32), axis=(0, 2, 3))
    d_two = (product("mprc,hp->mrch", d_raw, out_weight) * slope_two).astype(jnp.bfloat16)
    mix_grad = product("mrch,mrcg->hg", hidden_one, d_two)
    mix_bias_grad = jnp.sum(d_two.astype(jnp.float32), axis=(0, 1, 2))
    d_one = (product("mrcg,hg->mrch", d_two, mix_weight) * slope_one).astype(jnp.bfloat16)
    conv_grad = product("mkrc,mrch->kh", stacked, d_one)
    conv_bias_grad = jnp.sum(d_one.astype(jnp.float32), axis=(0, 1, 2))
    return (conv_grad, conv_bias_grad, mix_grad, mix_bias_grad, out_grad, out_bias_grad)


def route_tables(owner_map, position, peers, blocks):
    capacity = blocks // peers
    serial = jnp.arange(blocks, dtype=jnp.int32)
    owned = lax.dynamic_slice_in_dim(owner_map, position * blocks, blocks)
    target = owned // blocks
    earlier = serial[None, :] < serial[:, None]
    ranking = jnp.sum((target[None, :] == target[:, None]) & earlier, axis=1)
    send_slot = target * capacity + ranking
    slot_block = jnp.zeros((blocks,), jnp.int32).at[send_slot].set(serial)
    count_all = owner_map.shape[0]
    inverse = (
        jnp.zeros((count_all,), jnp.int32).at[owner_map].set(jnp.arange(count_all, dtype=jnp.int32))
    )
    mine_list = lax.dynamic_slice_in_dim(inverse, position * blocks, blocks)
    source = mine_list // blocks
    within = mine_list % blocks
    source_rows = owner_map.reshape(peers, blocks)[source] // blocks
    before = serial[None, :] < within[:, None]
    home_rank = jnp.sum((source_rows == position) & before, axis=1)
    home_slot = source * capacity + home_rank
    return (owned, send_slot, slot_block, home_slot, mine_list)


def on_device(
    fields,
    land_mask,
    land_frac,
    owner_map,
    targets,
    conv_weight,
    conv_bias,
    mix_weight,
    mix_bias,
    out_weight,
    out_bias,
):
    peers = lax.axis_size("space")
    position = lax.axis_index("space")
    members = fields.shape[0]
    pools = out_weight.shape[1]
    tile_rows = fields.shape[2]
    tile_cols = fields.shape[3]
    blocks = tile_rows // SIDE * (tile_cols // SIDE)
    capacity = blocks // peers
    extended = padded_2(fields, (("space", 2),), 1)
    padded = jnp.pad(extended, ((0, 0), (0, 0), (0, 0), (1, 1)))
    outputs = forward_tile(
        padded, conv_weight, conv_bias, mix_weight, mix_bias, out_weight, out_bias
    )
    weight_map = land_frac * land_mask.astype(jnp.float32)
    density = jax.nn.softplus(outputs[5]) * weight_map
    owned, send_slot, slot_block, home_slot, mine_list = route_tables(
        owner_map, position, peers, blocks
    )
    strip_values = block_sums(density, SIDE)
    strip_weights = block_sums(weight_map, SIDE)
    got_values, got_weights = (
        lax.all_to_all(
            strip_values[:, :, slot_block].reshape(members, pools, peers, capacity),
            "space",
            split_axis=2,
            concat_axis=2,
            tiled=True,
        ),
        lax.all_to_all(
            strip_weights[slot_block].reshape(1, 1, peers, capacity),
            "space",
            split_axis=2,
            concat_axis=2,
            tiled=True,
        ),
    )
    coarse_sum = got_values.reshape(members, pools, blocks)[:, :, home_slot]
    coarse_weight = got_weights.reshape(blocks)[home_slot]
    denom = jnp.maximum(coarse_weight, 1.0)
    coarse_pred = coarse_sum / denom
    residual = coarse_pred - targets
    count_all = members * lax.axis_size("dp") * pools * owner_map.shape[0]
    d_coarse = residual / (math.sqrt(count_all) * denom)
    serial = jnp.arange(blocks, dtype=jnp.int32)
    back_order = jnp.zeros((blocks,), jnp.int32).at[home_slot].set(serial)
    returned = lax.all_to_all(
        d_coarse[:, :, back_order].reshape(members, pools, peers, capacity),
        "space",
        split_axis=2,
        concat_axis=2,
        tiled=True,
    )
    d_block = returned.reshape(members, pools, blocks)[:, :, send_slot]
    grads = backward_tile(*outputs, weight_map, d_block, mix_weight, out_weight, SIDE)
    squares = jnp.sum(residual * residual)
    conv_grad, conv_bias_grad, mix_grad, mix_bias_grad, out_grad, out_bias_grad, total = lax.psum(
        (grads[0], grads[1], grads[2], grads[3], grads[4], grads[5], squares), ("dp", "space")
    )
    loss = 0.5 * total / count_all
    conv_grad = conv_grad.reshape(conv_weight.shape)
    return (
        coarse_pred,
        conv_grad,
        conv_bias_grad,
        mix_grad,
        mix_bias_grad,
        out_grad,
        out_bias_grad,
        loss,
    )


def solution(mesh):
    placed = (
        P("dp", None, "space", None),
        P("space", None),
        P("space", None),
        P(),
        P("dp", None, "space"),
        P(),
        P(),
        P(),
        P(),
        P(),
        P(),
    )
    return jax.shard_map(
        on_device,
        mesh=mesh,
        in_specs=placed,
        out_specs=(P("dp", None, "space"), P(), P(), P(), P(), P(), P(), P()),
        check_vma=False,
    )
```

profile of v0, /device:TPU:0, one launch (start us, length us, event | category | flops | bytes accessed | tf_op | source)
XLA Modules:
  0.0 266.4 jit_solution(3640901755132870467)
XLA Ops:
  7.2 1.5 copy.72
  8.7 2.4 collective-permute-start
  13.1 6.2 %scatter_custom_fusion.1 = s32[1536]{0:T(1024)S(1)} fusion(s32[1536]{0:T(1024)S(1)} %compare_select_fusion.1, s32[1536]{0:T(1024)S(1)} %iota.16, s32[]{:T(128)} %constant.30.clone.1), kind=kCustom, calls=%fused_computation.91 | custom fusion | bytes 6148 | tf_op jit(solution)/shard_map/scatter | solution.py:109
  23.0 1.6 gather_fusion.3
  25.3 8.2 %all-to-all-start.1 = ((f32[1,1,8,24]{3,1,0,2:T(1,128)}), f32[1,1,8,24]{3,1,0,2:T(1,128)S(1)}, u32[]{:S(2)}, u32[]{:S(2)}) async-start(f32[1,1,8,24]{3,1,0,2:T(1,128)} %reshape.230), calls=%async_computation.1 | async-start | bytes 8192 | tf_op jit(solution)/shard_map/all_to_all | solution.py:162
  35.4 1.4 scatter_custom_fusion.2
  37.0 2.0 all-to-all-done.1
  40.2 1.6 gather_fusion.4
  45.2 2.9 %copy-done.1 = bf16[1,288,96,128]{3,1,2,0:T(8,128)(2,1)} copy-done((bf16[1,288,96,128]{3,1,2,0:T(8,128)(2,1)}, bf16[1,288,96,128]{3,1,2,0:T(8,128)(2,1)S(1)}, u32[]{:S(2)}) %copy-start.1) | copy-done | bytes 7077912
  48.1 2.7 %fusion.2 = f32[96,128,128]{2,1,0:T(8,128)S(1)} fusion(bf16[288,128,1]{1,0,2:T(8,128)(2,1)S(1)} %bitcast.71, bf16[1,288,96,128]{3,1,2,0:T(8,128)(2,1)S(1)} %slice_dynamic-update-slice_fusion), kind=kOutput, calls=%fused_computation.16 | convolution fusion | flops 905969664 | bytes 13443072 | tf_op jit(solution)/shard_map/mkrc,kh->mrch/dot_general | solution.py:39
  50.9 6.2 %multiply_convert_fusion = (bf16[96,128,128]{2,1,0:T(8,128)(2,1)S(1)}, f32[96,128,128]{2,1,0:T(8,128)}) fusion(f32[128]{0:T(128)S(1)} %copy-done.10, bf16[128,128]{1,0:T(8,128)(2,1)S(1)} %copy-done.8, f32[96,128,128]{2,1,0:T(8,128)S(1)} %fusion.2, f32[128]{0:T(128)S(1)} %copy-done.11), kind=kOutput, calls=%fused_computation.34 | convolution fusion | flops 434110464 | bytes 15762432 | tf_op jit(solution)/shard_map/mrch,hg->mrcg/dot_general | solution.py:39
  57.1 1.8 fusion.25
  60.0 8.5 %reshape.223 = f32[14,12,8,16,8]{4,3,2,1,0:T(8,128)} reshape(f32[14,96,128]{2,1,0:T(8,128)} %copy.78) | data formatting | bytes 1376256 | tf_op jit(solution)/shard_map/reshape | solution.py:45
  68.5 5.6 %reduce_sum.72 = f32[14,12,16]{2,1,0:T(8,128)} reduce(f32[14,12,8,16,8]{4,3,2,1,0:T(8,128)} %reshape.223, f32[]{:T(128)} %constant.29.clone.1), dimensions={2,4}, to_apply=%region_0.1 | reduce | flops 169344 | bytes 698884 | tf_op jit(solution)/shard_map/reduce_sum | solution.py:46
  79.4 3.6 %all-to-all-start = ((f32[8,1,336]{2,1,0:T(1,128)}), f32[8,1,336]{2,1,0:T(1,128)S(1)}, u32[]{:S(2)}, u32[]{:S(2)}) async-start(f32[8,1,336]{2,1,0:T(1,128)} %reshape.361), calls=%async_computation | async-start | bytes 24576 | tf_op jit(solution)/shard_map/all_to_all | solution.py:155
  83.0 5.3 %all-to-all-done = f32[8,1,336]{2,1,0:T(1,128)S(1)} async-done(((f32[8,1,336]{2,1,0:T(1,128)}), f32[8,1,336]{2,1,0:T(1,128)S(1)}, u32[]{:S(2)}, u32[]{:S(2)}) %all-to-all-start) | async-done | bytes 10784 | tf_op jit(solution)/shard_map/all_to_all | solution.py:155
  90.6 1.6 multiply_reduce_fusion
  93.0 1.6 gather_fusion.5
  96.2 3.3 %all-to-all-start.2 = ((f32[8,1,336]{2,1,0:T(1,128)}), f32[8,1,336]{2,1,0:T(1,128)S(1)}, u32[]{:S(2)}, u32[]{:S(2)}) async-start(f32[8,1,336]{2,1,0:T(1,128)} %reshape.363), calls=%async_computation.2 | async-start | bytes 24576 | tf_op jit(solution)/shard_map/all_to_all | solution.py:179
  100.2 4.8 %all-to-all-done.2 = f32[8,1,336]{2,1,0:T(1,128)S(1)} async-done(((f32[8,1,336]{2,1,0:T(1,128)}), f32[8,1,336]{2,1,0:T(1,128)S(1)}, u32[]{:S(2)}, u32[]{:S(2)}) %all-to-all-start.2) | async-done | bytes 10784 | tf_op jit(solution)/shard_map/all_to_all | solution.py:179
  109.3 1.3 copy.86
  111.6 2.5 copy.87
  114.1 1.9 convert_reduce_fusion.2
  116.0 6.8 %convert_reduce_fusion = (f32[128]{0:T(128)S(1)}, bf16[96,128,128]{2,1,0:T(8,128)(2,1)S(1)}) fusion(f32[96,128,128]{2,1,0:T(8,128)} %get-tuple-element.67, f32[128]{0:T(128)S(1)} %copy-done.10, bf16[14,96,128]{2,0,1:T(8,128)(2,1)S(1)} %get-tuple-element.58, bf16[128,14]{0,1:T(8,128)(2,1)S(1)} %copy-done.6), kind=kOutput, calls=%fused_computation.32 | convolution fusion | flops 78643072 | bytes 9785856 | tf_op jit(solution)/shard_map/mprc,hp->mrch/dot_general | solution.py:39
  122.9 4.7 %convert_reduce_fusion.1 = (f32[128]{0:T(128)S(1)}, bf16[96,128,128]{2,1,0:T(8,128)(2,1)S(1)}) fusion(f32[96,128,128]{2,1,0:T(8,128)S(1)} %bitcast.75, f32[128]{0:T(128)S(1)} %copy-done.12, bf16[96,128,128]{2,1,0:T(8,128)(2,1)S(1)} %get-tuple-element.73, bf16[128,128]{1,0:T(8,128)(2,1)S(1)} %copy-done.9), kind=kOutput, calls=%fused_computation.33 | convolution fusion | flops 437256064 | bytes 12616704 | tf_op jit(solution)/shard_map/mrcg,hg->mrch/dot_general | solution.py:39
  127.7 3.2 %convolution_bitcast_fusion = f32[128,128]{1,0:T(8,128)} fusion(bf16[96,128,128]{2,1,0:T(8,128)(2,1)S(1)} %get-tuple-element.73, f32[96,128,128]{2,1,0:T(8,128)S(1)} %bitcast.75, f32[128]{0:T(128)S(1)} %copy-done.12), kind=kOutput, calls=%fused_computation.47 | convolution fusion | flops 418381824 | bytes 9503232 | tf_op jit(solution)/shard_map/mrch,mrcg->hg/dot_general | solution.py:39
  130.9 2.6 fusion
  133.5 1.5 convolution_bitcast_fusion.1
  135.1 39.5 %all-reduce.1 = (f32[128]{0:T(128)}, f32[128]{0:T(128)}, f32[128,14]{0,1:T(8,128)}, f32[14]{0:T(128)}, f32[]{:T(128)}) all-reduce(f32[128]{0:T(128)S(1)} %get-tuple-element.70, f32[128]{0:T(128)S(1)} %get-tuple-element.72, f32[128,14]{0,1:T(8,128)S(1)} %convolution_bitcast_fusion.1, ...), channel_id=1, replica_groups=mesh['dp'=4,'space'=8] {'dp','space'}, use_global_device_ids=true, to_apply=%region_9.10 | all-reduce | flops 2063 | bytes 16504 | tf_op jit(solution)/shard_map/psum | solution.py:189
  175.3 80.2 %all-reduce.5.cloned.1.call-done = (f32[3,3,32,128]{3,2,1,0:T(8,128)}, f32[128,128]{1,0:T(8,128)}) async-done(((f32[3,3,32,128]{3,2,1,0:T(8,128)}, f32[128,128]{1,0:T(8,128)}), (f32[3,3,32,128]{3,2,1,0:T(8,128)}, f32[128,128]{1,0:T(8,128)})) %all-reduce.5.cloned.1.call-update) | async-done | bytes 213008 | tf_op jit(solution)/shard_map/psum | solution.py:189
  255.4 1.6 copy.102
  257.0 1.5 copy.103
  (103 shorter events, 29.9 us)
Async XLA Ops:
  7.2 38.0 %copy-start = (bf16[3,3,32,128]{3,2,1,0:T(8,128)(2,1)S(1)}, bf16[3,3,32,128]{3,2,1,0:T(8,128)(2,1)}, u32[]{:S(2)}) copy-start(bf16[3,3,32,128]{3,2,1,0:T(8,128)(2,1)} %param.16) | copy-start | bytes 221188
  7.2 29.6 %copy-start.5 = (f32[1,14,192]{2,0,1:T(1,128)S(1)}, f32[1,14,192]{2,0,1:T(1,128)}, u32[]{:S(2)}) copy-start(f32[1,14,192]{2,0,1:T(1,128)} %param.15) | copy-start | bytes 32260
  8.7 33.2 %collective-permute-start = (bf16[1,32,1,128]{3,1,2,0:T(8,128)(2,1)S(1)}, bf16[1,32,1,128]{3,1,2,0:T(8,128)(2,1)S(1)}, u32[]{:S(2)}, u32[]{:S(2)}) collective-permute-start(bf16[1,32,1,128]{3,1,2,0:T(8,128)(2,1)S(1)} %get-tuple-element.61), channel_id=1, source_target_pairs={{0,1},{1,2},{2,3},{3,4},{4,5},{5,6},{6,7},{8,9},{9,10},{10,11},{11... | collective-permute-start | bytes 24584 | tf_op jit(solution)/shard_map/ppermute | solution.py:20
  11.0 30.8 %collective-permute-start.1 = (bf16[1,32,1,128]{3,1,2,0:T(8,128)(2,1)S(1)}, bf16[1,32,1,128]{3,1,2,0:T(8,128)(2,1)S(1)}, u32[]{:S(2)}, u32[]{:S(2)}) collective-permute-start(bf16[1,32,1,128]{3,1,2,0:T(8,128)(2,1)S(1)} %get-tuple-element.62), channel_id=1, source_target_pairs={{1,0},{2,1},{3,2},{4,3},{5,4},{6,5},{7,6},{9,8},{10,9},{11,10},{12... | collective-permute-start | bytes 24584 | tf_op jit(solution)/shard_map/ppermute | solution.py:23
  23.0 20.7 %copy-start.3 = (bf16[1,32,96,128]{3,2,1,0:T(8,128)(2,1)S(1)}, bf16[1,32,96,128]{3,2,1,0:T(8,128)(2,1)}, u32[]{:S(2)}) copy-start(bf16[1,32,96,128]{3,2,1,0:T(8,128)(2,1)} %param.11) | copy-start | bytes 2359300
  25.3 13.7 %all-to-all-start.1 = ((f32[1,1,8,24]{3,1,0,2:T(1,128)}), f32[1,1,8,24]{3,1,0,2:T(1,128)S(1)}, u32[]{:S(2)}, u32[]{:S(2)}) async-start(f32[1,1,8,24]{3,1,0,2:T(1,128)} %reshape.230), calls=%async_computation.1 | async-start | bytes 8192 | tf_op jit(solution)/shard_map/all_to_all | solution.py:162
  45.2 2.9 %copy-start.1 = (bf16[1,288,96,128]{3,1,2,0:T(8,128)(2,1)}, bf16[1,288,96,128]{3,1,2,0:T(8,128)(2,1)S(1)}, u32[]{:S(2)}) copy-start(bf16[1,288,96,128]{3,1,2,0:T(8,128)(2,1)S(1)} %slice_dynamic-update-slice_fusion) | copy-start | bytes 21233668
  48.1 2.8 %copy-start.8 = (bf16[128,128]{1,0:T(8,128)(2,1)S(1)}, bf16[128,128]{1,0:T(8,128)(2,1)}, u32[]{:S(2)}) copy-start(bf16[128,128]{1,0:T(8,128)(2,1)} %param.18) | copy-start | bytes 98308
  48.1 2.8 %copy-start.10 = (f32[128]{0:T(128)S(1)}, f32[128]{0:T(128)}, u32[]{:S(2)}) copy-start(f32[128]{0:T(128)} %param.19) | copy-start | bytes 1540
  48.1 2.8 %copy-start.11 = (f32[128]{0:T(128)S(1)}, f32[128]{0:T(128)}, u32[]{:S(2)}) copy-start(f32[128]{0:T(128)} %param.17) | copy-start | bytes 1540
  50.8 6.2 %copy-start.2 = (f32[96,128,128]{2,1,0:T(8,128)}, f32[96,128,128]{2,1,0:T(8,128)S(1)}, u32[]{:S(2)}) copy-start(f32[96,128,128]{2,1,0:T(8,128)S(1)} %fusion.2) | copy-start | bytes 18874372
  50.9 6.2 %copy-start.6 = (bf16[128,14]{0,1:T(8,128)(2,1)S(1)}, bf16[128,14]{0,1:T(8,128)(2,1)}, u32[]{:S(2)}) copy-start(bf16[128,14]{0,1:T(8,128)(2,1)} %param.20) | copy-start | bytes 10756
  50.9 6.2 %copy-start.7 = (f32[14]{0:T(128)S(1)}, f32[14]{0:T(128)}, u32[]{:S(2)}) copy-start(f32[14]{0:T(128)} %param.21) | copy-start | bytes 172
  79.4 8.9 %all-to-all-start = ((f32[8,1,336]{2,1,0:T(1,128)}), f32[8,1,336]{2,1,0:T(1,128)S(1)}, u32[]{:S(2)}, u32[]{:S(2)}) async-start(f32[8,1,336]{2,1,0:T(1,128)} %reshape.361), calls=%async_computation | async-start | bytes 24576 | tf_op jit(solution)/shard_map/all_to_all | solution.py:155
  96.2 8.9 %all-to-all-start.2 = ((f32[8,1,336]{2,1,0:T(1,128)}), f32[8,1,336]{2,1,0:T(1,128)S(1)}, u32[]{:S(2)}, u32[]{:S(2)}) async-start(f32[8,1,336]{2,1,0:T(1,128)} %reshape.363), calls=%async_computation.2 | async-start | bytes 24576 | tf_op jit(solution)/shard_map/all_to_all | solution.py:179
  99.5 155.9 %all-reduce.5.cloned.1.call-start = ((), (), s32[]{:S(2)}) async-start(), calls=%async_computation.3 | async-start | bytes 425984 | tf_op jit(solution)/shard_map/psum | solution.py:189
  114.1 8.8 %slice-start.2 = ((s8[6291456]{0:T(1024)(128)(4,1)}), s8[4194304]{0:T(1024)(128)(4,1)S(1)}, s32[]{:S(2)}) async-start(s8[6291456]{0:T(1024)(128)(4,1)} %bitcast.74), calls=%async_computation.6 | async-start | bytes 8388608
  116.0 6.9 %copy-start.4 = (bf16[14,96,128]{2,0,1:T(8,128)(2,1)}, bf16[14,96,128]{2,0,1:T(8,128)(2,1)S(1)}, u32[]{:S(2)}) copy-start(bf16[14,96,128]{2,0,1:T(8,128)(2,1)S(1)} %get-tuple-element.58) | copy-start | bytes 1032196
  116.0 6.9 %slice-start.3 = ((s8[6291456]{0:T(1024)(128)(4,1)}), s8[2097152]{0:T(1024)(128)(4,1)S(1)}, s32[]{:S(2)}) async-start(s8[6291456]{0:T(1024)(128)(4,1)} %bitcast.74), calls=%async_computation.7 | async-start | bytes 4194304
  116.0 6.9 %copy-start.9 = (bf16[128,128]{1,0:T(8,128)(2,1)S(1)}, bf16[128,128]{1,0:T(8,128)(2,1)}, u32[]{:S(2)}) copy-start(bf16[128,128]{1,0:T(8,128)(2,1)} %param.18) | copy-start | bytes 98308
  116.0 6.9 %copy-start.12 = (f32[128]{0:T(128)S(1)}, f32[128]{0:T(128)}, u32[]{:S(2)}) copy-start(f32[128]{0:T(128)} %param.17) | copy-start | bytes 1540
  116.0 14.9 %slice-start = ((s8[7077888]{0:T(1024)(128)(4,1)}), s8[4194304]{0:T(1024)(128)(4,1)S(1)}, s32[]{:S(2)}) async-start(s8[7077888]{0:T(1024)(128)(4,1)} %bitcast.72), calls=%async_computation.4 | async-start | bytes 8388608
  122.9 7.9 %slice-start.1 = ((s8[7077888]{0:T(1024)(128)(4,1)}), s8[2883584]{0:T(1024)(128)(4,1)S(1)}, s32[]{:S(2)}) async-start(s8[7077888]{0:T(1024)(128)(4,1)} %bitcast.72), calls=%async_computation.5 | async-start | bytes 5767168
Sparse Core Ops, SparseCore 0:
  133.7 121.6 all-reduce.4
where the time goes:
time: 268 us; the launch traced here: 266 us
  waiting for transfers between devices  92.3 us (34%)
  local copies, waits for them, and re-layouts  52.3 us (20%)
  blocking collectives  39.5 us (15%)
  matrix products  29.6 us (11%)
  starting transfers between devices  18.8 us (7%)
  other arithmetic  17.4 us (6%)
  between operations  16.3 us (6%)
    psum x1, waiting for transfers between devices, on_device(): lax.psum((grads[0], grads[1], grads[2], grads[3], grads[4], grads[5], squ...  80.2 us
    psum x1, blocking collectives, on_device(): lax.psum((grads[0], grads[1], grads[2], grads[3], grads[4], grads[5], squ...  39.5 us
    dot_general x8, matrix products, product(): return jnp.einsum(form, left, right, preferred_element_type=jnp.float32)  29.6 us
    unnamed x50, local copies, waits for them, and re-layouts  12.2 us
    reshape x2, local copies, waits for them, and re-layouts, block_sums(): values.reshape(leading + (height // side, side, breadth // side, side))  8.97 us
    all_to_all x1, starting transfers between devices, on_device(): lax.all_to_all(strip_weights[slot_block].reshape(1, 1, peers, capacity),...  8.23 us
    scatter x1, local copies, waits for them, and re-layouts, route_tables(): jnp.zeros((count_all,), jnp.int32).at[owner_map]  6.18 us
    broadcast_in_dim x4, local copies, waits for them, and re-layouts, backward_tile(): d_cells = jnp.repeat(jnp.repeat(d_cells, side, axis=2), side, axis=3)  5.73 us
  transfers between devices with their start and end apart: 6, of which 4 were waited for; matrix products, arithmetic and copies ran while one was open for 8% of the time, Pallas kernels for 0%

commit v1 on v0

--- a/solution.py
+++ b/solution.py
@@ -95,27 +95,56 @@
     return (conv_grad, conv_bias_grad, mix_grad, mix_bias_grad, out_grad, out_bias_grad)
 
 
-def route_tables(owner_map, position, peers, blocks):
-    capacity = blocks // peers
-    serial = jnp.arange(blocks, dtype=jnp.int32)
-    owned = lax.dynamic_slice_in_dim(owner_map, position * blocks, blocks)
-    target = owned // blocks
-    earlier = serial[None, :] < serial[:, None]
-    ranking = jnp.sum((target[None, :] == target[:, None]) & earlier, axis=1)
-    send_slot = target * capacity + ranking
-    slot_block = jnp.zeros((blocks,), jnp.int32).at[send_slot].set(serial)
-    count_all = owner_map.shape[0]
-    inverse = (
-        jnp.zeros((count_all,), jnp.int32).at[owner_map].set(jnp.arange(count_all, dtype=jnp.int32))
-    )
-    mine_list = lax.dynamic_slice_in_dim(inverse, position * blocks, blocks)
-    source = mine_list // blocks
-    within = mine_list % blocks
-    source_rows = owner_map.reshape(peers, blocks)[source] // blocks
-    before = serial[None, :] < within[:, None]
-    home_rank = jnp.sum((source_rows == position) & before, axis=1)
-    home_slot = source * capacity + home_rank
-    return (owned, send_slot, slot_block, home_slot, mine_list)
+def bits_of(size, low):
+    return [1 << k for k in range(size.bit_length() - 1) if (1 << k) >= low]
+
+
+def swapped(values, axis, bit):
+    return lax.ppermute(values, axis, [(i, i ^ bit) for i in range(lax.axis_size(axis))])
+
+
+def gather_relative(values, axis, bits):
+    for bit in bits:
+        values = jnp.concatenate([values, swapped(values, axis, bit)], axis=0)
+    return values
+
+
+def crossed(values, step):
+    dp, space = lax.axis_size("dp"), lax.axis_size("space")
+    dp_moves = [(bit, 0) for bit in bits_of(dp, 1)]
+    space_moves = [(0, bit) for bit in bits_of(space, 2)]
+    orders = (dp_moves + space_moves, space_moves + dp_moves)
+    pairs = []
+    for d in range(dp):
+        for s in range(space):
+            d_bit, s_bit = orders[s % 2][step]
+            pairs.append((d * space + s, (d ^ d_bit) * space + (s ^ s_bit)))
+    return lax.ppermute(values, ("dp", "space"), pairs)
+
+
+def reduce_all(keep, send, coarse):
+    space = lax.axis_size("space")
+    n_dp, n_space = len(bits_of(lax.axis_size("dp"), 1)), len(bits_of(space, 2))
+    core = lax.axis_index("space") % 2
+    rows = keep.shape[0]
+    got = swapped(jnp.concatenate([send, coarse], axis=0), "space", 1)
+    half = keep + got[:rows]
+    gathered = jnp.concatenate([coarse, got[rows:]], axis=0)
+    for step in range(n_dp + n_space):
+        if step < n_space:
+            got = crossed(jnp.concatenate([half, gathered], axis=0), step)
+            gathered = jnp.concatenate([gathered, got[rows:]], axis=0)
+            got = got[:rows]
+        else:
+            got = crossed(half, step)
+        half = half + got
+    got = swapped(jnp.concatenate([half, gathered], axis=0), "space", 1)
+    gathered = jnp.where(core == 1, gathered, got[rows:])
+    return half, got[:rows], gathered
+
+
+def picked(values, chosen):
+    return jnp.einsum("jpb,jbq->pq", values, chosen.astype(jnp.float32), precision=lax.Precision.HIGHEST)
 
 
 def on_device(
@@ -133,72 +162,71 @@
 ):
     peers = lax.axis_size("space")
     position = lax.axis_index("space")
-    members = fields.shape[0]
     pools = out_weight.shape[1]
     tile_rows = fields.shape[2]
     tile_cols = fields.shape[3]
     blocks = tile_rows // SIDE * (tile_cols // SIDE)
-    capacity = blocks // peers
+    serial = jnp.arange(peers, dtype=jnp.int32)
+    local = jnp.arange(blocks, dtype=jnp.int32)
     extended = padded_2(fields, (("space", 2),), 1)
+    target_rows = pools * blocks // 128
+    target_all = gather_relative(targets.reshape(target_rows, 128), "space", bits_of(peers, 1))
+    target_all = target_all.reshape(peers, pools, blocks)
+    owners = lax.dynamic_slice_in_dim(owner_map, position * blocks, blocks)
+    places = (position ^ serial)[:, None] * blocks + local[None, :]
+    target_strip = picked(target_all, places[:, :, None] == owners[None, None, :])
+
     padded = jnp.pad(extended, ((0, 0), (0, 0), (0, 0), (1, 1)))
     outputs = forward_tile(
         padded, conv_weight, conv_bias, mix_weight, mix_bias, out_weight, out_bias
     )
     weight_map = land_frac * land_mask.astype(jnp.float32)
     density = jax.nn.softplus(outputs[5]) * weight_map
-    owned, send_slot, slot_block, home_slot, mine_list = route_tables(
-        owner_map, position, peers, blocks
-    )
-    strip_values = block_sums(density, SIDE)
-    strip_weights = block_sums(weight_map, SIDE)
-    got_values, got_weights = (
-        lax.all_to_all(
-            strip_values[:, :, slot_block].reshape(members, pools, peers, capacity),
-            "space",
-            split_axis=2,
-            concat_axis=2,
-            tiled=True,
-        ),
-        lax.all_to_all(
-            strip_weights[slot_block].reshape(1, 1, peers, capacity),
-            "space",
-            split_axis=2,
-            concat_axis=2,
-            tiled=True,
-        ),
-    )
-    coarse_sum = got_values.reshape(members, pools, blocks)[:, :, home_slot]
-    coarse_weight = got_weights.reshape(blocks)[home_slot]
-    denom = jnp.maximum(coarse_weight, 1.0)
-    coarse_pred = coarse_sum / denom
-    residual = coarse_pred - targets
-    count_all = members * lax.axis_size("dp") * pools * owner_map.shape[0]
-    d_coarse = residual / (math.sqrt(count_all) * denom)
-    serial = jnp.arange(blocks, dtype=jnp.int32)
-    back_order = jnp.zeros((blocks,), jnp.int32).at[home_slot].set(serial)
-    returned = lax.all_to_all(
-        d_coarse[:, :, back_order].reshape(members, pools, peers, capacity),
-        "space",
-        split_axis=2,
-        concat_axis=2,
-        tiled=True,
-    )
-    d_block = returned.reshape(members, pools, blocks)[:, :, send_slot]
+    strip_values = block_sums(density, SIDE)[0]
+    denom = jnp.maximum(block_sums(weight_map, SIDE), 1.0)
+    coarse = strip_values / denom
+    residual = coarse - target_strip
+    count_all = lax.axis_size("dp") * pools * owner_map.shape[0]
+    d_block = (residual / (math.sqrt(count_all) * denom))[None]
     grads = backward_tile(*outputs, weight_map, d_block, mix_weight, out_weight, SIDE)
-    squares = jnp.sum(residual * residual)
-    conv_grad, conv_bias_grad, mix_grad, mix_bias_grad, out_grad, out_bias_grad, total = lax.psum(
-        (grads[0], grads[1], grads[2], grads[3], grads[4], grads[5], squares), ("dp", "space")
-    )
-    loss = 0.5 * total / count_all
-    conv_grad = conv_grad.reshape(conv_weight.shape)
+    width = mix_weight.shape[0]
+    spare = jnp.zeros((16 - pools, width), jnp.float32)
+    small = jnp.zeros((32, width), jnp.float32)
+    small = small.at[0].set(grads[1]).at[1].set(grads[3]).at[2, :pools].set(grads[5])
+    small = small.at[3].set(jnp.sum(residual * residual))
+    payload = jnp.concatenate([grads[0], grads[2], small, grads[4].T, spare], axis=0)
+    payload = jnp.pad(payload, ((0, -payload.shape[0] % 16), (0, 0)))
+    half_rows = payload.shape[0] // 2
+    core = position % 2
+    low, high = payload[:half_rows], payload[half_rows:]
+    half, other, gathered = reduce_all(
+        jnp.where(core == 0, low, high),
+        jnp.where(core == 0, high, low),
+        coarse.reshape(target_rows, 128),
+    )
+    total = jnp.concatenate(
+        [jnp.where(core == 0, half, other), jnp.where(core == 0, other, half)], axis=0
+    )
+    base = position | 1
+    strips = owner_map.reshape(peers, blocks)[base ^ serial]
+    coarse_pred = picked(
+        gathered.reshape(peers, pools, blocks),
+        strips[:, :, None] == (position * blocks + local)[None, None, :],
+    )
+    k = grads[0].shape[0]
+    conv_grad = total[:k].reshape(conv_weight.shape)
+    mix_grad = total[k : k + width]
+    small = total[k + width : k + width + 32]
+    out_grad = total[k + width + 32 : k + width + 32 + pools].T
+    loss = 0.5 * small[3, 0] / count_all
     return (
-        coarse_pred,
+        coarse_pred[None],
         conv_grad,
-        conv_bias_grad,
+        small[0],
         mix_grad,
-        mix_bias_grad,
+        small[1],
         out_grad,
-        out_bias_grad,
+        small[2, :pools],
         loss,
     )
 

time: 268 us -> 110 us (0.41)
  waiting for transfers between devices: 92.3 us -> 20.4 us
  blocking collectives: 39.5 us -> 0 us
  local copies, waits for them, and re-layouts: 52.3 us -> 27.9 us
  between operations: 16.3 us -> 2.96 us
  other arithmetic: 17.4 us -> 11.8 us
  starting transfers between devices: 18.8 us -> 15.5 us
    psum x1 -> x0, waiting for transfers between devices: 80.2 us -> none  [on_device(): lax.psum((grads[0], grads[1], grads[2], grads[3], grads[4], grads[5], squ...]
    psum x1 -> x0, blocking collectives: 39.5 us -> none  [on_device(): lax.psum((grads[0], grads[1], grads[2], grads[3], grads[4], grads[5], squ...]
    ppermute x0 -> x9, waiting for transfers between devices: none -> 20.4 us  [the longest x4 18.3 us: crossed(): return lax.ppermute(values, ('dp', 'space'), pairs)]
    all_to_all x3 -> x0, starting transfers between devices: 15.1 us -> none  [the longest x1 8.23 us: on_device(): lax.all_to_all(strip_weights[slot_block].reshape(1, 1, peers, capacity),...]
    all_to_all x3 -> x0, waiting for transfers between devices: 12.2 us -> none  [the longest x1 5.33 us: on_device(): lax.all_to_all(strip_values[:, :, slot_block].reshape(members, pools, pee...]
    ppermute x0 -> x9, starting transfers between devices: none -> 11.9 us  [the longest x5 7.82 us: swapped(): lax.ppermute(values, axis, [(i, i ^ bit) for i in range(lax.axis_size(axi...]
    gather x7 -> x1, local copies, waits for them, and re-layouts: 9.55 us -> 0.56 us  [on_device(): strips = owner_map.reshape(peers, blocks)[base ^ serial]]
    scatter x3 -> x4, local copies, waits for them, and re-layouts: 8.75 us -> 0.27 us  [the longest x3 0.23 us: on_device(): small.at[0].set(grads[1]).at[1].set(grads[3]).at[2, :pools].set(grads[5])]
  transfers between devices with their start and end apart: 6 -> 11, of which waited for: 4 -> 6; matrix products, arithmetic and copies ran while one was open for 8% -> 31% of each run, Pallas kernels for 0% -> 0%
where the time goes in v1:
time: 110 us; the launch traced here: 109 us
  matrix products  30.7 us (28%)
  local copies, waits for them, and re-layouts  27.9 us (25%)
  waiting for transfers between devices  20.4 us (19%)
  starting transfers between devices  15.5 us (14%)
  other arithmetic  11.8 us (11%)
  between operations  2.96 us (3%)
    dot_general x8, matrix products, product(): return jnp.einsum(form, left, right, preferred_element_type=jnp.float32)  27.5 us
    ppermute x4, waiting for transfers between devices, crossed(): return lax.ppermute(values, ('dp', 'space'), pairs)  18.3 us
    reshape x2, local copies, waits for them, and re-layouts, block_sums(): values.reshape(leading + (height // side, side, breadth // side, side))  8.92 us
    ppermute x5, starting transfers between devices, swapped(): lax.ppermute(values, axis, [(i, i ^ bit) for i in range(lax.axis_size(axi...  7.82 us
    broadcast_in_dim x4, local copies, waits for them, and re-layouts, backward_tile(): d_cells = jnp.repeat(jnp.repeat(d_cells, side, axis=2), side, axis=3)  5.76 us
    reduce_sum x2, other arithmetic, block_sums(): jnp.sum(shaped, axis=(-3, -1))  5.1 us
    unnamed x40, local copies, waits for them, and re-layouts  4.1 us
    ppermute x4, starting transfers between devices, crossed(): return lax.ppermute(values, ('dp', 'space'), pairs)  4.08 us
  transfers between devices with their start and end apart: 11, of which 6 were waited for; matrix products, arithmetic and copies ran while one was open for 31% of the time, Pallas kernels for 0%

profile of v1, /device:TPU:0, one launch (start us, length us, event | category | flops | bytes accessed | tf_op | source)
XLA Modules:
  0.0 109.4 jit_solution(3111661565599185503)
XLA Ops:
  0.7 1.5 %copy.39 = bf16[1,32,96,128]{3,1,2,0:T(8,128)(2,1)S(1)} copy(bf16[1,32,96,128]{3,2,1,0:T(8,128)(2,1)} %param.19) | data formatting | bytes 1572864 | tf_op args[0]
  2.2 2.4 %collective-permute-start = (bf16[1,32,1,128]{3,1,2,0:T(8,128)(2,1)S(1)}, bf16[1,32,1,128]{3,1,2,0:T(8,128)(2,1)S(1)}, u32[]{:S(2)}, u32[]{:S(2)}) collective-permute-start(bf16[1,32,1,128]{3,1,2,0:T(8,128)(2,1)S(1)} %get-tuple-element.82), channel_id=1, source_target_pairs={{0,1},{1,2},{2,3},{3,4},{4,5},{5,6},{6,7},{8,9},{9,10},{10,11},{11... | collective-permute-start | bytes 24584 | tf_op jit(solution)/shard_map/ppermute | solution.py:20
  4.6 1.3 %collective-permute-start.1 = (bf16[1,32,1,128]{3,1,2,0:T(8,128)(2,1)S(1)}, bf16[1,32,1,128]{3,1,2,0:T(8,128)(2,1)S(1)}, u32[]{:S(2)}, u32[]{:S(2)}) collective-permute-start(bf16[1,32,1,128]{3,1,2,0:T(8,128)(2,1)S(1)} %get-tuple-element.83), channel_id=1, source_target_pairs={{1,0},{2,1},{3,2},{4,3},{5,4},{6,5},{7,6},{9,8},{10,9},{11,10},{12... | collective-permute-start | bytes 24584 | tf_op jit(solution)/shard_map/ppermute | solution.py:23
  6.7 3.3 %collective-permute-start.2 = (f32[21,128]{1,0:T(8,128)S(1)}, f32[21,128]{1,0:T(8,128)S(1)}, u32[]{:S(2)}, u32[]{:S(2)}) collective-permute-start(f32[21,128]{1,0:T(8,128)S(1)} %reshape.331), channel_id=1, source_target_pairs={{0,1},{1,0},{2,3},{3,2},{4,5},{5,4},{6,7},{7,6},{8,9},{9,8},{10,11... | collective-permute-start | bytes 32264 | tf_op jit(solution)/shard_map/ppermute | solution.py:103
  12.2 1.3 %dynamic_slice.3 = s32[192]{0:T(256)} dynamic-slice(s32[1536]{0:T(1024)} %param.22, s32[]{:T(128)S(6)} %select_n.59), dynamic_slice_sizes={192} | dynamic-slice | bytes 1540 | tf_op jit(solution)/shard_map/dynamic_slice | solution.py:175
  13.6 0.9 fusion.23
  16.9 2.7 %fusion.2 = f32[96,128,128]{2,1,0:T(8,128)S(1)} fusion(bf16[288,128,1]{1,0,2:T(8,128)(2,1)S(1)} %bitcast.72, bf16[1,288,96,128]{3,1,2,0:T(8,128)(2,1)S(1)} %slice_dynamic-update-slice_fusion), kind=kOutput, calls=%fused_computation.7 | convolution fusion | flops 905969664 | bytes 13443072 | tf_op jit(solution)/shard_map/mkrc,kh->mrch/dot_general | solution.py:39
  19.8 1.7 %collective-permute-start.3 = (f32[42,128]{1,0:T(8,128)S(1)}, f32[42,128]{1,0:T(8,128)S(1)}, u32[]{:S(2)}, u32[]{:S(2)}) collective-permute-start(f32[42,128]{1,0:T(8,128)S(1)} %pad_maximum_fusion.8), channel_id=1, source_target_pairs={{0,2},{1,3},{2,0},{3,1},{4,6},{5,7},{6,4},{7,5},{8,10},{9,11},{10,... | collective-permute-start | bytes 64520 | tf_op jit(solution)/shard_map/ppermute | solution.py:103
  21.5 6.0 %multiply_convert_fusion = (bf16[96,128,128]{2,1,0:T(8,128)(2,1)S(1)}, f32[96,128,128]{2,1,0:T(8,128)}) fusion(f32[128]{0:T(128)S(1)} %copy-done.9, bf16[128,128]{1,0:T(8,128)(2,1)S(1)} %copy-done.7, f32[96,128,128]{2,1,0:T(8,128)S(1)} %fusion.2, f32[128]{0:T(128)S(1)} %copy-done.10), kind=kOutput, calls=%fused_computation.25 | convolution fusion | flops 434110464 | bytes 15762432 | tf_op jit(solution)/shard_map/mrch,hg->mrcg/dot_general | solution.py:39
  27.5 2.6 %collective-permute-start.4 = (f32[84,128]{1,0:T(8,128)S(1)}, f32[84,128]{1,0:T(8,128)}, u32[]{:S(2)}, u32[]{:S(2)}) collective-permute-start(f32[84,128]{1,0:T(8,128)S(1)} %pad_maximum_fusion.7), channel_id=1, source_target_pairs={{0,4},{1,5},{2,6},{3,7},{4,0},{5,1},{6,2},{7,3},{8,12},{9,13},{10,... | collective-permute-start | bytes 129032 | tf_op jit(solution)/shard_map/ppermute | solution.py:103
  30.2 1.8 %fusion.41 = (f32[14,96,128]{2,0,1:T(8,128)S(1)}, f32[14,96,128]{2,0,1:T(8,128)}) fusion(f32[96,128]{1,0:T(8,128)S(1)} %convert_multiply_fusion, f32[14]{0:T(128)S(1)} %copy-done.6, bf16[96,128,128]{2,1,0:T(8,128)(2,1)S(1)} %get-tuple-element.90, bf16[128,14]{0,1:T(8,128)(2,1)S(1)} %copy-done.5), kind=kOutput, calls=%fused_computation.48 | convolution fusion | flops 45416448 | bytes 4574776 | tf_op jit(solution)/shard_map/mrch,hp->mprc/dot_general | solution.py:39
  32.0 1.1 copy.45
  33.0 8.5 %reshape.329 = f32[14,12,8,16,8]{4,3,2,1,0:T(8,128)} reshape(f32[14,96,128]{2,1,0:T(8,128)} %copy.45) | data formatting | bytes 1376256 | tf_op jit(solution)/shard_map/reshape | solution.py:45
  41.5 5.0 %reduce_sum.54 = f32[14,12,16]{2,1,0:T(8,128)S(1)} reduce(f32[14,12,8,16,8]{4,3,2,1,0:T(8,128)} %reshape.329, f32[]{:T(128)} %constant.157.clone.1), dimensions={2,4}, to_apply=%region_0.1 | reduce | flops 169344 | bytes 698884 | tf_op jit(solution)/shard_map/reduce_sum | solution.py:46
  47.6 2.5 %multiply_reduce_fusion = (f32[]{:T(128)}, f32[14,192]{1,0:T(8,128)}) fusion(f32[192]{0:T(256)} %broadcast_multiply_fusion, f32[8,14,192]{2,1,0:T(8,128)S(1)} %reshape.332, s32[192]{0:T(256)} %dynamic_slice.3, s32[8,192]{1,0:T(8,128)S(1)} %iota_add_fusion, f32[14,192]{1,0:T(8,128)S(1)} %squeeze_reshape.6, f32[192]{0:T(256)S(1)} %max.29), kind=kOutput, calls=%fused_computation.86 | convolution fusion | flops 49853568 | bytes 115972 | tf_op jit(solution)/shard_map/jpb,jbq->pq/dot_general | solution.py:147
  51.0 0.9 broadcast_bitcast_fusion.1
  51.9 1.3 %copy.46 = f32[14,96,16]{1,2,0:T(8,128)S(1)} copy(f32[14,96,16]{2,1,0:T(8,128)} %broadcast_bitcast_fusion.1) | data formatting | bytes 172032 | tf_op jit(solution)/shard_map/broadcast_in_dim | solution.py:85
  53.2 1.0 broadcast_bitcast_fusion
  54.2 2.5 %copy.47 = f32[14,96,128]{2,0,1:T(8,128)} copy(f32[14,96,128]{1,2,0:T(8,128)} %broadcast_bitcast_fusion) | data formatting | bytes 1376256 | tf_op jit(solution)/shard_map/broadcast_in_dim | solution.py:85
  56.7 1.7 %convert_reduce_fusion.2 = (f32[14]{0:T(128)S(1)}, bf16[14,96,128]{2,0,1:T(8,128)(2,1)S(1)}) fusion(f32[14,96,128]{2,0,1:T(8,128)} %get-tuple-element.93, f32[14,96,128]{2,0,1:T(8,128)} %copy.47, f32[96,128]{1,0:T(8,128)S(1)} %convert_multiply_fusion), kind=kLoop, calls=%fused_computation.61 | loop fusion | flops 1376242 | bytes 1769528 | tf_op jit(solution)/shard_map/reduce_sum | solution.py:88
  59.0 7.0 %convert_reduce_fusion = (f32[128]{0:T(128)S(1)}, bf16[96,128,128]{2,1,0:T(8,128)(2,1)S(1)}) fusion(f32[96,128,128]{2,1,0:T(8,128)} %get-tuple-element.91, f32[128]{0:T(128)} %param.27, bf16[14,96,128]{2,0,1:T(8,128)(2,1)S(1)} %get-tuple-element.81, bf16[128,14]{0,1:T(8,128)(2,1)} %param.28), kind=kOutput, calls=%fused_computation.23 | convolution fusion | flops 78643072 | bytes 9785856 | tf_op jit(solution)/shard_map/mprc,hp->mrch/dot_general | solution.py:39
  66.1 5.0 %convert_reduce_fusion.1 = (f32[128]{0:T(128)S(1)}, bf16[96,128,128]{2,1,0:T(8,128)(2,1)S(1)}) fusion(f32[96,128,128]{2,1,0:T(8,128)S(1)} %bitcast.76, f32[128]{0:T(128)S(1)} %copy-done.11, bf16[96,128,128]{2,1,0:T(8,128)(2,1)S(1)} %get-tuple-element.97, bf16[128,128]{1,0:T(8,128)(2,1)S(1)} %copy-done.8), kind=kOutput, calls=%fused_computation.24 | convolution fusion | flops 437256064 | bytes 12616704 | tf_op jit(solution)/shard_map/mrcg,hg->mrch/dot_general | solution.py:39
  71.0 2.6 %convolution_bitcast_fusion = f32[128,128]{1,0:T(8,128)S(1)} fusion(bf16[96,128,128]{2,1,0:T(8,128)(2,1)S(1)} %get-tuple-element.97, f32[96,128,128]{2,1,0:T(8,128)S(1)} %bitcast.76, f32[128]{0:T(128)S(1)} %copy-done.11), kind=kOutput, calls=%fused_computation.43 | convolution fusion | flops 418381824 | bytes 9503232 | tf_op jit(solution)/shard_map/mrch,mrcg->hg/dot_general | solution.py:39
  73.7 2.0 %fusion.29 = f32[288,128]{1,0:T(8,128)S(1)} fusion(bf16[96,128,128]{2,1,0:T(8,128)(2,1)S(1)} %get-tuple-element.95, bf16[1,288,96,128]{3,1,2,0:T(8,128)(2,1)S(1)} %bitcast.74), kind=kOutput, calls=%fused_computation.42 | convolution fusion | flops 905969664 | bytes 10371072 | tf_op jit(solution)/shard_map/mkrc,mrch->kh/dot_general | solution.py:39
  76.7 1.3 %collective-permute-done.5 = f32[253,128]{1,0:T(8,128)S(1)} collective-permute-done((f32[253,128]{1,0:T(8,128)S(1)}, f32[253,128]{1,0:T(8,128)S(1)}, u32[]{:S(2)}, u32[]{:S(2)}) %collective-permute-start.5) | collective-permute-done | bytes 129568 | tf_op jit(solution)/shard_map/ppermute | solution.py:103
  78.1 1.6 %collective-permute-start.6 = (f32[274,128]{1,0:T(8,128)S(1)}, f32[274,128]{1,0:T(8,128)S(1)}, u32[]{:S(2)}, u32[]{:S(2)}) collective-permute-start(f32[274,128]{1,0:T(8,128)S(1)} %pad_maximum_fusion.4), channel_id=1, source_target_pairs={{0,8},{1,3},{2,10},{3,1},{4,12},{5,7},{6,14},{7,5},{8,0},{9,11},{1... | collective-permute-start | bytes 420872 | tf_op jit(solution)/shard_map/ppermute | solution.py:122
  79.7 3.6 %collective-permute-done.6 = f32[274,128]{1,0:T(8,128)S(1)} collective-permute-done((f32[274,128]{1,0:T(8,128)S(1)}, f32[274,128]{1,0:T(8,128)S(1)}, u32[]{:S(2)}, u32[]{:S(2)}) %collective-permute-start.6) | collective-permute-done | bytes 140320 | tf_op jit(solution)/shard_map/ppermute | solution.py:122
  83.4 1.6 %collective-permute-start.7 = (f32[316,128]{1,0:T(8,128)S(1)}, f32[316,128]{1,0:T(8,128)S(1)}, u32[]{:S(2)}, u32[]{:S(2)}) collective-permute-start(f32[316,128]{1,0:T(8,128)S(1)} %pad_maximum_fusion.2), channel_id=1, source_target_pairs={{0,16},{1,5},{2,18},{3,7},{4,20},{5,1},{6,22},{7,3},{8,24},{9,13},... | collective-permute-start | bytes 485384 | tf_op jit(solution)/shard_map/ppermute | solution.py:122
  84.9 3.8 %collective-permute-done.7 = f32[316,128]{1,0:T(8,128)S(1)} collective-permute-done((f32[316,128]{1,0:T(8,128)S(1)}, f32[316,128]{1,0:T(8,128)S(1)}, u32[]{:S(2)}, u32[]{:S(2)}) %collective-permute-start.7) | collective-permute-done | bytes 161824 | tf_op jit(solution)/shard_map/ppermute | solution.py:122
  89.3 4.4 %collective-permute-done.8 = f32[232,128]{1,0:T(8,128)S(1)} collective-permute-done((f32[232,128]{1,0:T(8,128)S(1)}, f32[232,128]{1,0:T(8,128)S(1)}, u32[]{:S(2)}, u32[]{:S(2)}) %collective-permute-start.8) | collective-permute-done | bytes 118816 | tf_op jit(solution)/shard_map/ppermute | solution.py:122
  94.2 6.5 %collective-permute-done.9 = f32[232,128]{1,0:T(8,128)S(1)} collective-permute-done((f32[232,128]{1,0:T(8,128)S(1)}, f32[232,128]{1,0:T(8,128)S(1)}, u32[]{:S(2)}, u32[]{:S(2)}) %collective-permute-start.9) | collective-permute-done | bytes 118816 | tf_op jit(solution)/shard_map/ppermute | solution.py:122
  101.9 0.8 collective-permute-done.10
  (110 shorter events, 16.3 us)
Async XLA Ops:
  0.6 16.2 %copy-start = (bf16[3,3,32,128]{3,2,1,0:T(8,128)(2,1)S(1)}, bf16[3,3,32,128]{3,2,1,0:T(8,128)(2,1)}, u32[]{:S(2)}) copy-start(bf16[3,3,32,128]{3,2,1,0:T(8,128)(2,1)} %param.24) | copy-start | bytes 221188
  0.6 14.7 %copy-start.3 = (bf16[1,32,96,128]{3,2,1,0:T(8,128)(2,1)S(1)}, bf16[1,32,96,128]{3,2,1,0:T(8,128)(2,1)}, u32[]{:S(2)}) copy-start(bf16[1,32,96,128]{3,2,1,0:T(8,128)(2,1)} %param.19) | copy-start | bytes 2359300
  2.2 11.4 %collective-permute-start = (bf16[1,32,1,128]{3,1,2,0:T(8,128)(2,1)S(1)}, bf16[1,32,1,128]{3,1,2,0:T(8,128)(2,1)S(1)}, u32[]{:S(2)}, u32[]{:S(2)}) collective-permute-start(bf16[1,32,1,128]{3,1,2,0:T(8,128)(2,1)S(1)} %get-tuple-element.82), channel_id=1, source_target_pairs={{0,1},{1,2},{2,3},{3,4},{4,5},{5,6},{6,7},{8,9},{9,10},{10,11},{11... | collective-permute-start | bytes 24584 | tf_op jit(solution)/shard_map/ppermute | solution.py:20
  4.6 9.0 %collective-permute-start.1 = (bf16[1,32,1,128]{3,1,2,0:T(8,128)(2,1)S(1)}, bf16[1,32,1,128]{3,1,2,0:T(8,128)(2,1)S(1)}, u32[]{:S(2)}, u32[]{:S(2)}) collective-permute-start(bf16[1,32,1,128]{3,1,2,0:T(8,128)(2,1)S(1)} %get-tuple-element.83), channel_id=1, source_target_pairs={{1,0},{2,1},{3,2},{4,3},{5,4},{6,5},{7,6},{9,8},{10,9},{11,10},{12... | collective-permute-start | bytes 24584 | tf_op jit(solution)/shard_map/ppermute | solution.py:23
  6.7 13.1 %collective-permute-start.2 = (f32[21,128]{1,0:T(8,128)S(1)}, f32[21,128]{1,0:T(8,128)S(1)}, u32[]{:S(2)}, u32[]{:S(2)}) collective-permute-start(f32[21,128]{1,0:T(8,128)S(1)} %reshape.331), channel_id=1, source_target_pairs={{0,1},{1,0},{2,3},{3,2},{4,5},{5,4},{6,7},{7,6},{8,9},{9,8},{10,11... | collective-permute-start | bytes 32264 | tf_op jit(solution)/shard_map/ppermute | solution.py:103
  16.9 2.9 %copy-start.1 = (bf16[1,288,96,128]{3,1,2,0:T(8,128)(2,1)}, bf16[1,288,96,128]{3,1,2,0:T(8,128)(2,1)S(1)}, u32[]{:S(2)}) copy-start(bf16[1,288,96,128]{3,1,2,0:T(8,128)(2,1)S(1)} %slice_dynamic-update-slice_fusion) | copy-start | bytes 21233668
  16.9 4.7 %copy-start.7 = (bf16[128,128]{1,0:T(8,128)(2,1)S(1)}, bf16[128,128]{1,0:T(8,128)(2,1)}, u32[]{:S(2)}) copy-start(bf16[128,128]{1,0:T(8,128)(2,1)} %param.26) | copy-start | bytes 98308
  16.9 4.6 %copy-start.9 = (f32[128]{0:T(128)S(1)}, f32[128]{0:T(128)}, u32[]{:S(2)}) copy-start(f32[128]{0:T(128)} %param.27) | copy-start | bytes 1540
  16.9 4.6 %copy-start.10 = (f32[128]{0:T(128)S(1)}, f32[128]{0:T(128)}, u32[]{:S(2)}) copy-start(f32[128]{0:T(128)} %param.25) | copy-start | bytes 1540
  19.8 7.7 %copy-start.2 = (f32[96,128,128]{2,1,0:T(8,128)}, f32[96,128,128]{2,1,0:T(8,128)S(1)}, u32[]{:S(2)}) copy-start(f32[96,128,128]{2,1,0:T(8,128)S(1)} %fusion.2) | copy-start | bytes 18874372
  19.8 10.4 %copy-start.5 = (bf16[128,14]{0,1:T(8,128)(2,1)S(1)}, bf16[128,14]{0,1:T(8,128)(2,1)}, u32[]{:S(2)}) copy-start(bf16[128,14]{0,1:T(8,128)(2,1)} %param.28) | copy-start | bytes 10756
  19.8 10.3 %copy-start.6 = (f32[14]{0:T(128)S(1)}, f32[14]{0:T(128)}, u32[]{:S(2)}) copy-start(f32[14]{0:T(128)} %param.29) | copy-start | bytes 172
  19.8 7.7 %collective-permute-start.3 = (f32[42,128]{1,0:T(8,128)S(1)}, f32[42,128]{1,0:T(8,128)S(1)}, u32[]{:S(2)}, u32[]{:S(2)}) collective-permute-start(f32[42,128]{1,0:T(8,128)S(1)} %pad_maximum_fusion.8), channel_id=1, source_target_pairs={{0,2},{1,3},{2,0},{3,1},{4,6},{5,7},{6,4},{7,5},{8,10},{9,11},{10,... | collective-permute-start | bytes 64520 | tf_op jit(solution)/shard_map/ppermute | solution.py:103
  27.5 19.2 %collective-permute-start.4 = (f32[84,128]{1,0:T(8,128)S(1)}, f32[84,128]{1,0:T(8,128)}, u32[]{:S(2)}, u32[]{:S(2)}) collective-permute-start(f32[84,128]{1,0:T(8,128)S(1)} %pad_maximum_fusion.7), channel_id=1, source_target_pairs={{0,4},{1,5},{2,6},{3,7},{4,0},{5,1},{6,2},{7,3},{8,12},{9,13},{10,... | collective-permute-start | bytes 129032 | tf_op jit(solution)/shard_map/ppermute | solution.py:103
  58.5 7.6 %slice-start.2 = ((s8[6291456]{0:T(1024)(128)(4,1)}), s8[4194304]{0:T(1024)(128)(4,1)S(1)}, s32[]{:S(2)}) async-start(s8[6291456]{0:T(1024)(128)(4,1)} %bitcast.75), calls=%async_computation.2 | async-start | bytes 8388608
  59.0 7.0 %slice-start.3 = ((s8[6291456]{0:T(1024)(128)(4,1)}), s8[2097152]{0:T(1024)(128)(4,1)S(1)}, s32[]{:S(2)}) async-start(s8[6291456]{0:T(1024)(128)(4,1)} %bitcast.75), calls=%async_computation.3 | async-start | bytes 4194304
  59.0 7.0 %copy-start.8 = (bf16[128,128]{1,0:T(8,128)(2,1)S(1)}, bf16[128,128]{1,0:T(8,128)(2,1)}, u32[]{:S(2)}) copy-start(bf16[128,128]{1,0:T(8,128)(2,1)} %param.26) | copy-start | bytes 98308
  59.0 7.0 %copy-start.11 = (f32[128]{0:T(128)S(1)}, f32[128]{0:T(128)}, u32[]{:S(2)}) copy-start(f32[128]{0:T(128)} %param.25) | copy-start | bytes 1540
  59.0 14.6 %slice-start = ((s8[7077888]{0:T(1024)(128)(4,1)}), s8[4194304]{0:T(1024)(128)(4,1)S(1)}, s32[]{:S(2)}) async-start(s8[7077888]{0:T(1024)(128)(4,1)} %bitcast.73), calls=%async_computation | async-start | bytes 8388608
  66.1 7.6 %slice-start.1 = ((s8[7077888]{0:T(1024)(128)(4,1)}), s8[2883584]{0:T(1024)(128)(4,1)S(1)}, s32[]{:S(2)}) async-start(s8[7077888]{0:T(1024)(128)(4,1)} %bitcast.73), calls=%async_computation.1 | async-start | bytes 5767168
  73.6 20.5 %copy-start.4 = (s32[1536]{0:T(1024)S(1)}, s32[1536]{0:T(1024)}, u32[]{:S(2)}) copy-start(s32[1536]{0:T(1024)} %param.22) | copy-start | bytes 18436
  76.7 1.4 %collective-permute-start.5 = (f32[253,128]{1,0:T(8,128)S(1)}, f32[253,128]{1,0:T(8,128)S(1)}, u32[]{:S(2)}, u32[]{:S(2)}) collective-permute-start(f32[253,128]{1,0:T(8,128)S(1)} %pad_maximum_fusion.5), channel_id=1, source_target_pairs={{0,1},{1,0},{2,3},{3,2},{4,5},{5,4},{6,7},{7,6},{8,9},{9,8},{10,11... | collective-permute-start | bytes 388616 | tf_op jit(solution)/shard_map/ppermute | solution.py:103
  78.1 5.2 %collective-permute-start.6 = (f32[274,128]{1,0:T(8,128)S(1)}, f32[274,128]{1,0:T(8,128)S(1)}, u32[]{:S(2)}, u32[]{:S(2)}) collective-permute-start(f32[274,128]{1,0:T(8,128)S(1)} %pad_maximum_fusion.4), channel_id=1, source_target_pairs={{0,8},{1,3},{2,10},{3,1},{4,12},{5,7},{6,14},{7,5},{8,0},{9,11},{1... | collective-permute-start | bytes 420872 | tf_op jit(solution)/shard_map/ppermute | solution.py:122
  83.4 5.4 %collective-permute-start.7 = (f32[316,128]{1,0:T(8,128)S(1)}, f32[316,128]{1,0:T(8,128)S(1)}, u32[]{:S(2)}, u32[]{:S(2)}) collective-permute-start(f32[316,128]{1,0:T(8,128)S(1)} %pad_maximum_fusion.2), channel_id=1, source_target_pairs={{0,16},{1,5},{2,18},{3,7},{4,20},{5,1},{6,22},{7,3},{8,24},{9,13},... | collective-permute-start | bytes 485384 | tf_op jit(solution)/shard_map/ppermute | solution.py:122
  88.8 4.9 %collective-permute-start.8 = (f32[232,128]{1,0:T(8,128)S(1)}, f32[232,128]{1,0:T(8,128)S(1)}, u32[]{:S(2)}, u32[]{:S(2)}) collective-permute-start(f32[232,128]{1,0:T(8,128)S(1)} %slice_add_fusion), channel_id=1, source_target_pairs={{0,2},{1,9},{2,0},{3,11},{4,6},{5,13},{6,4},{7,15},{8,10},{9,1},{1... | collective-permute-start | bytes 356360 | tf_op jit(solution)/shard_map/ppermute | solution.py:122
  93.7 7.0 %collective-permute-start.9 = (f32[232,128]{1,0:T(8,128)S(1)}, f32[232,128]{1,0:T(8,128)S(1)}, u32[]{:S(2)}, u32[]{:S(2)}) collective-permute-start(f32[232,128]{1,0:T(8,128)S(1)} %add.170), channel_id=1, source_target_pairs={{0,4},{1,17},{2,6},{3,19},{4,0},{5,21},{6,2},{7,23},{8,12},{9,25},... | collective-permute-start | bytes 356360 | tf_op jit(solution)/shard_map/ppermute | solution.py:122
  101.2 1.5 %collective-permute-start.10 = (f32[400,128]{1,0:T(8,128)S(1)}, f32[400,128]{1,0:T(8,128)S(1)}, u32[]{:S(2)}, u32[]{:S(2)}) collective-permute-start(f32[400,128]{1,0:T(8,128)S(1)} %concatenate.71), channel_id=1, source_target_pairs={{0,1},{1,0},{2,3},{3,2},{4,5},{5,4},{6,7},{7,6},{8,9},{9,8},{10,11... | collective-permute-start | bytes 614408 | tf_op jit(solution)/shard_map/ppermute | solution.py:103

commit v2 on v1

v2 whole, which is shorter than its diff:
```python
import functools
import math

import jax
import jax.numpy as jnp
from jax import lax
from jax.experimental import pallas as pl
from jax.experimental.pallas import tpu as pltpu
from jax.sharding import PartitionSpec as P

SIDE = 8
POOL_ROWS = 16
GROUP = 2
VMEM = 56 * 1024 * 1024

CUBIC = 0.044715
ROOT_TWO_PI = math.sqrt(2.0 / math.pi)

F32, BF16 = jnp.float32, jnp.bfloat16


def gelu_pair(pre):
    square = pre * pre
    half = 0.5 + 0.5 * jnp.tanh(pre * (ROOT_TWO_PI + (ROOT_TWO_PI * CUBIC) * square))
    value = pre * half
    slope = half + value * (1.0 - half) * (2.0 * ROOT_TWO_PI + (6.0 * ROOT_TWO_PI * CUBIC) * square)
    return value, slope


def mm(left, right):
    return jnp.dot(left, right, preferred_element_type=F32)


def mm_nt(left, right):
    return lax.dot_general(left, right, (((1,), (1,)), ((), ())), preferred_element_type=F32)


def thirds(values):
    high = values.astype(BF16)
    rest = values - high.astype(F32)
    middle = rest.astype(BF16)
    low = (rest - middle.astype(F32)).astype(BF16)
    return jnp.concatenate([high, middle, low], axis=0)


def picked(values, chosen):
    rows = values.shape[0]
    out = mm(thirds(values), chosen)
    return out[:rows] + out[rows : 2 * rows] + out[2 * rows :]


def ones_where(condition):
    return jnp.where(condition, 1.0, 0.0).astype(BF16)


def iota(shape, dim):
    return lax.broadcasted_iota(jnp.int32, shape, dim)


def column(row, rows):
    return jnp.broadcast_to(row, (rows, row.shape[1])).T


def step_kernel(
    count_all,
    fields_ref,
    low_ref,
    high_ref,
    frac_ref,
    mask_ref,
    owner_ref,
    target_ref,
    w1_ref,
    b1_ref,
    w2_ref,
    b2_ref,
    w3_ref,
    b3_ref,
    keep_ref,
    send_ref,
    coarse_ref,
    shifted,
    weight,
    w1t,
    w2t,
    w3p,
    w3t,
    b1c,
    b2c,
    b3c,
    hidden_one,
    slope_one,
    hidden_two,
    slope_two,
    raw_all,
    sums,
    d_cols,
    total,
):
    rows, channels, cols = fields_ref.shape
    width = w2_ref.shape[0]
    pools = w3_ref.shape[1]
    peers, blocks = owner_ref.shape
    tiles = rows // SIDE
    across = cols // SIDE
    taps = 3 * channels
    lanes = GROUP * cols
    groups = SIDE // GROUP
    position = lax.axis_index("space")
    core = lax.rem(position, 2)

    w1t[...] = w1_ref[...].astype(F32).T.astype(BF16)
    w2t[...] = w2_ref[...].astype(F32).T.astype(BF16)
    w3f = jnp.concatenate(
        [w3_ref[...].astype(F32), jnp.zeros((width, width - pools), F32)], axis=1
    ).T[:POOL_ROWS]
    w3t[...] = w3f.astype(BF16)
    w3p[...] = jnp.concatenate([w3f, jnp.zeros((width - POOL_ROWS, width), F32)], axis=0).T[
        :, :POOL_ROWS
    ].astype(BF16)
    b1c[...] = column(b1_ref[...], width)
    b2c[...] = column(b2_ref[...], width)
    b3 = jnp.concatenate([b3_ref[...], jnp.zeros((1, width - pools), F32)], axis=1)
    b3c[...] = column(b3, width)[:POOL_ROWS]
    weight[...] = frac_ref[...] * mask_ref[...].astype(F32)

    lane = iota((channels, cols), 1)

    def put(row, values):
        values32 = values.astype(F32)
        left = jnp.where(lane == 0, 0.0, pltpu.roll(values32, 1, 1))
        right = jnp.where(lane == cols - 1, 0.0, pltpu.roll(values32, cols - 1, 1))
        shifted[pl.ds(pl.multiple_of(row * taps, taps), taps), :] = jnp.concatenate(
            [left.astype(BF16), values, right.astype(BF16)], axis=0
        )

    put(0, low_ref[...])
    put(rows + 1, high_ref[...])

    @pl.loop(0, rows // 8)
    def _(step):
        for inner in range(8):
            put(step * 8 + inner + 1, fields_ref[step * 8 + inner])

    def taps_of(row, count):
        parts = [
            shifted[pl.ds(pl.multiple_of((row + i) * taps, taps), 3 * taps), :]
            for i in range(count)
        ]
        return jnp.concatenate(parts, axis=1)

    def wide(values, count):
        return jnp.concatenate([values] * count, axis=1)

    def weights_of(row, count):
        parts = [
            jnp.broadcast_to(weight[pl.ds(row + i, 1), :], (POOL_ROWS, cols)) for i in range(count)
        ]
        return jnp.concatenate(parts, axis=1)

    @pl.loop(0, tiles)
    def _(tile):
        total_cols = jnp.zeros((POOL_ROWS, cols), F32)
        for group in range(groups):
            row = tile * SIDE + group * GROUP
            at = tile * groups + group
            pre_one = mm(w1t[...], taps_of(row, GROUP)) + wide(b1c[...], GROUP)
            value_one, slope = gelu_pair(pre_one)
            slope_one[at] = slope
            value_one = value_one.astype(BF16)
            hidden_one[at] = value_one
            pre_two = mm(w2t[...], value_one) + wide(b2c[...], GROUP)
            value_two, slope = gelu_pair(pre_two)
            slope_two[at] = slope
            value_two = value_two.astype(BF16)
            hidden_two[at] = value_two
            raw = mm(w3t[...], value_two) + wide(b3c[...], GROUP)
            raw_all[at] = raw
            density = (
                jnp.maximum(raw, 0.0) + jnp.log1p(jnp.exp(-jnp.abs(raw)))
            ) * weights_of(row, GROUP)
            for i in range(GROUP):
                total_cols = total_cols + density[:, i * cols : (i + 1) * cols]
        sums[pl.ds(pl.multiple_of(tile * POOL_ROWS, POOL_ROWS), POOL_ROWS), :] = total_cols

    weight_cols = jnp.sum(weight[...].reshape(tiles, SIDE, cols), axis=1)
    weight_cols = jnp.concatenate([weight_cols, jnp.zeros((-tiles % 8, cols), F32)], axis=0)
    same = ones_where(iota((cols, cols), 0) // SIDE == iota((cols, cols), 1) // SIDE)
    summed = picked(jnp.concatenate([sums[...], weight_cols], axis=0), same)
    owners = owner_ref[pl.ds(position, 1), :]
    target = jnp.zeros((POOL_ROWS, blocks), F32)
    for peer in range(peers):
        places = iota((blocks, blocks), 0) + (position ^ peer) * blocks
        values = jnp.concatenate(
            [target_ref[peer], jnp.zeros((POOL_ROWS - pools, blocks), F32)], axis=0
        )
        target = target + picked(values, ones_where(places == owners))
    in_tile = iota((blocks, cols), 0) - iota((blocks, cols), 1) // SIDE
    spread = jnp.concatenate([ones_where(in_tile == tile * across) for tile in range(tiles)], axis=1)
    target_cols = picked(target, spread)
    first = iota((cols, blocks), 0)
    in_block = iota((cols, blocks), 1) - first // SIDE
    coarse = jnp.zeros((POOL_ROWS, blocks), F32)
    loss = jnp.zeros((POOL_ROWS, cols), F32)
    valid = iota((POOL_ROWS, cols), 0) < pools
    for tile in range(tiles):
        denom = jnp.maximum(summed[tiles * POOL_ROWS + tile : tiles * POOL_ROWS + tile + 1], 1.0)
        pred = summed[tile * POOL_ROWS : (tile + 1) * POOL_ROWS] / denom
        residual = jnp.where(valid, pred - target_cols[:, tile * cols : (tile + 1) * cols], 0.0)
        loss = loss + residual * residual
        d_cols[tile] = residual / (math.sqrt(count_all) * denom)
        leads = (first % SIDE == 0) & (in_block == tile * across)
        coarse = coarse + picked(pred, ones_where(leads))
    loss = jnp.sum(jnp.sum(loss, axis=1, keepdims=True), axis=0, keepdims=True) * (1.0 / SIDE)
    coarse_rows = jnp.concatenate(
        [
            coarse[:, :128],
            jnp.concatenate([coarse[:, 128:], jnp.zeros((POOL_ROWS, 256 - blocks), F32)], axis=1),
        ],
        axis=0,
    )
    coarse_ref[...] = coarse_rows

    total[...] = jnp.zeros_like(total)
    ones = jnp.ones((POOL_ROWS, SIDE * cols), BF16)
    conv_rows = 3 * taps
    mix_at = conv_rows
    out_at = mix_at + width
    bias_at = out_at + POOL_ROWS

    @pl.loop(0, tiles, init_carry=jnp.zeros((POOL_ROWS, cols), F32))
    def out_bias(tile, carried):
        d_raws, d_twos, d_ones = [], [], []
        for group in range(groups):
            row = tile * SIDE + group * GROUP
            at = tile * groups + group
            raw = raw_all[at]
            small = jnp.exp(-jnp.abs(raw))
            sigmoid = jnp.where(raw >= 0.0, 1.0, small) / (1.0 + small)
            d_raw = (wide(d_cols[tile], GROUP) * weights_of(row, GROUP) * sigmoid).astype(BF16)
            d_two = (mm(w3p[...], d_raw) * slope_two[at]).astype(BF16)
            d_one = (mm(w2_ref[...], d_two) * slope_one[at]).astype(BF16)
            for i in range(GROUP):
                carried = carried + d_raw[:, i * cols : (i + 1) * cols].astype(F32)
            d_raws.append(d_raw)
            d_twos.append(d_two)
            d_ones.append(d_one)
        at = tile * groups
        d_raw = jnp.concatenate(d_raws, axis=1)
        d_two = jnp.concatenate(d_twos, axis=1)
        d_one = jnp.concatenate(d_ones, axis=1)
        inputs = jnp.concatenate([taps_of(tile * SIDE, SIDE), ones], axis=0)
        got = mm_nt(inputs, d_one)
        total[:conv_rows, :] += got[:conv_rows]
        total[bias_at : bias_at + 8, :] += got[conv_rows : conv_rows + 8]
        one = jnp.concatenate([hidden_one[at + g] for g in range(groups)], axis=1)
        got = mm_nt(jnp.concatenate([one, ones], axis=0), d_two)
        total[mix_at:out_at, :] += got[:width]
        total[bias_at + 8 : bias_at + 16, :] += got[width : width + 8]
        two = jnp.concatenate([hidden_two[at + g] for g in range(groups)], axis=1)
        total[out_at:bias_at, :] += mm_nt(d_raw, two)
        return carried

    bias = jnp.sum(out_bias, axis=1, keepdims=True)
    here, there = iota((POOL_ROWS, cols), 0), iota((POOL_ROWS, cols), 1)
    bias_row = jnp.sum(jnp.where(here == there, bias, 0.0), axis=0, keepdims=True)
    part = total[out_at:bias_at, :]
    part = jnp.where(here == pools, bias_row, part)
    total[out_at:bias_at, :] = jnp.where(here == pools + 1, loss, part)
    half = keep_ref.shape[0]
    keep_ref[...] = total[pl.ds(pl.multiple_of(core * half, 8), half), :]
    send_ref[:half, :] = total[pl.ds(pl.multiple_of((1 - core) * half, 8), half), :]
    send_ref[half:, :] = coarse_rows


def finish_kernel(
    count_all,
    half_ref,
    other_ref,
    gathered_ref,
    owner_ref,
    coarse_ref,
    conv_ref,
    conv_bias_ref,
    mix_ref,
    mix_bias_ref,
    out_ref,
    out_bias_ref,
    loss_ref,
):
    position = lax.axis_index("space")
    core = lax.rem(position, 2)
    peers, blocks = owner_ref.shape
    pools = out_ref.shape[0]
    conv_rows, width = conv_ref.shape
    half, other = half_ref[...], other_ref[...]
    low = jnp.where(core == 0, half, other)
    high = jnp.where(core == 0, other, half)
    total = jnp.concatenate([low, high], axis=0)
    out_at = conv_rows + width
    bias_at = out_at + POOL_ROWS
    conv_ref[...] = total[:conv_rows]
    mix_ref[...] = total[conv_rows:out_at]
    out_ref[...] = total[out_at : out_at + pools]
    out_bias_ref[...] = total[out_at + pools : out_at + pools + 1, :pools]
    loss_ref[...] = (0.5 / count_all) * total[out_at + pools + 1 : out_at + pools + 2, :1]
    conv_bias_ref[...] = total[bias_at : bias_at + 1]
    mix_bias_ref[...] = total[bias_at + 8 : bias_at + 9]
    base = position | 1
    coarse = jnp.zeros((POOL_ROWS, blocks), F32)
    for peer in range(peers):
        owners = owner_ref[pl.ds(base ^ peer, 1), :]
        places = iota((blocks, blocks), 0) + position * blocks
        values = jnp.concatenate(
            [
                gathered_ref[peer, :POOL_ROWS, :],
                gathered_ref[peer, POOL_ROWS:, : blocks - 128],
            ],
            axis=1,
        )
        terms = thirds(values)
        got = mm_nt(terms, ones_where(places == owners))
        coarse = coarse + got[:POOL_ROWS] + got[POOL_ROWS : 2 * POOL_ROWS] + got[2 * POOL_ROWS :]
    coarse_ref[...] = coarse[:pools]


def bits_of(size, low):
    return [1 << k for k in range(size.bit_length() - 1) if (1 << k) >= low]


def swapped(values, axis, bit):
    return lax.ppermute(values, axis, [(i, i ^ bit) for i in range(lax.axis_size(axis))])


def gather_relative(values, axis, bits):
    for bit in bits:
        values = jnp.concatenate([values, swapped(values, axis, bit)], axis=0)
    return values


def crossed(values, step):
    dp, space = lax.axis_size("dp"), lax.axis_size("space")
    dp_moves = [(bit, 0) for bit in bits_of(dp, 1)]
    space_moves = [(0, bit) for bit in bits_of(space, 2)]
    orders = (dp_moves + space_moves, space_moves + dp_moves)
    pairs = []
    for d in range(dp):
        for s in range(space):
            d_bit, s_bit = orders[s % 2][step]
            pairs.append((d * space + s, (d ^ d_bit) * space + (s ^ s_bit)))
    return lax.ppermute(values, ("dp", "space"), pairs)


def reduce_all(keep, send, coarse):
    space = lax.axis_size("space")
    n_dp, n_space = len(bits_of(lax.axis_size("dp"), 1)), len(bits_of(space, 2))
    core = lax.axis_index("space") % 2
    rows = keep.shape[0]
    got = swapped(send, "space", 1)
    half = keep + got[:rows]
    gathered = jnp.concatenate([coarse, got[rows:]], axis=0)
    for step in range(n_dp + n_space):
        if step < n_space:
            got = crossed(jnp.concatenate([half, gathered], axis=0), step)
            gathered = jnp.concatenate([gathered, got[rows:]], axis=0)
            got = got[:rows]
        else:
            got = crossed(half, step)
        half = half + got
    got = swapped(jnp.concatenate([half, gathered], axis=0), "space", 1)
    gathered = jnp.where(core == 1, gathered, got[rows:])
    return half, got[:rows], gathered


def on_device(
    fields,
    land_mask,
    land_frac,
    owner_map,
    targets,
    conv_weight,
    conv_bias,
    mix_weight,
    mix_bias,
    out_weight,
    out_bias,
):
    peers = lax.axis_size("space")
    pools = out_weight.shape[1]
    width = mix_weight.shape[0]
    channels, rows, cols = fields.shape[1:]
    tiles = rows // SIDE
    blocks = tiles * (cols // SIDE)
    count_all = lax.axis_size("dp") * pools * owner_map.shape[0]
    owners = owner_map.reshape(peers, blocks)

    by_row = jnp.swapaxes(fields[0], 0, 1)
    forward = [(i, i + 1) for i in range(peers - 1)]
    backward = [(target, source) for source, target in forward]
    low = lax.ppermute(by_row[rows - 1], "space", forward)
    high = lax.ppermute(by_row[0], "space", backward)
    target_all = gather_relative(targets, "space", bits_of(peers, 1))

    conv_rows = 9 * channels
    half = conv_rows + width + 2 * POOL_ROWS
    half = (half + 31) // 32 * 16
    groups = rows // GROUP
    lanes = GROUP * cols
    f32, bf16 = F32, BF16
    keep, send, coarse = pl.pallas_call(
        functools.partial(step_kernel, count_all),
        out_shape=[
            jax.ShapeDtypeStruct((half, width), f32),
            jax.ShapeDtypeStruct((half + 2 * POOL_ROWS, width), f32),
            jax.ShapeDtypeStruct((2 * POOL_ROWS, width), f32),
        ],
        in_specs=[pl.BlockSpec(memory_space=pltpu.VMEM)] * 13,
        out_specs=[pl.BlockSpec(memory_space=pltpu.VMEM)] * 3,
        scratch_shapes=[
            pltpu.VMEM(((rows + 2) * 3 * channels, cols), bf16),
            pltpu.VMEM((rows, cols), f32),
            pltpu.VMEM((width, conv_rows), bf16),
            pltpu.VMEM((width, width), bf16),
            pltpu.VMEM((width, POOL_ROWS), bf16),
            pltpu.VMEM((POOL_ROWS, width), bf16),
            pltpu.VMEM((width, cols), f32),
            pltpu.VMEM((width, cols), f32),
            pltpu.VMEM((POOL_ROWS, cols), f32),
            pltpu.VMEM((groups, width, lanes), bf16),
            pltpu.VMEM((groups, width, lanes), f32),
            pltpu.VMEM((groups, width, lanes), bf16),
            pltpu.VMEM((groups, width, lanes), f32),
            pltpu.VMEM((groups, POOL_ROWS, lanes), f32),
            pltpu.VMEM((tiles * POOL_ROWS, cols), f32),
            pltpu.VMEM((tiles, POOL_ROWS, cols), f32),
            pltpu.VMEM((2 * half, width), f32),
        ],
        compiler_params=pltpu.CompilerParams(vmem_limit_bytes=VMEM),
        name="train_step",
    )(
        by_row,
        low,
        high,
        land_frac,
        land_mask,
        owners,
        target_all,
        conv_weight.reshape(conv_rows, width),
        conv_bias.reshape(1, width),
        mix_weight,
        mix_bias.reshape(1, width),
        out_weight,
        out_bias.reshape(1, pools),
    )
    half, other, gathered = reduce_all(keep, send, coarse)
    outs = pl.pallas_call(
        functools.partial(finish_kernel, count_all),
        out_shape=[
            jax.ShapeDtypeStruct((pools, blocks), f32),
            jax.ShapeDtypeStruct((conv_rows, width), f32),
            jax.ShapeDtypeStruct((1, width), f32),
            jax.ShapeDtypeStruct((width, width), f32),
            jax.ShapeDtypeStruct((1, width), f32),
            jax.ShapeDtypeStruct((pools, width), f32),
            jax.ShapeDtypeStruct((1, pools), f32),
            jax.ShapeDtypeStruct((1, 1), f32),
        ],
        in_specs=[pl.BlockSpec(memory_space=pltpu.VMEM)] * 4,
        out_specs=[pl.BlockSpec(memory_space=pltpu.VMEM)] * 8,
        compiler_params=pltpu.CompilerParams(vmem_limit_bytes=VMEM),
        name="finish",
    )(half, other, gathered.reshape(peers, 2 * POOL_ROWS, width), owners)
    coarse_pred, conv_grad, conv_bias_grad, mix_grad, mix_bias_grad, out_grad, out_bias_grad, loss = outs
    return (
        coarse_pred[None],
        conv_grad.reshape(conv_weight.shape),
        conv_bias_grad.reshape(width),
        mix_grad,
        mix_bias_grad.reshape(width),
        out_grad.T,
        out_bias_grad.reshape(pools),
        loss.reshape(()),
    )


def solution(mesh):
    placed = (
        P("dp", None, "space", None),
        P("space", None),
        P("space", None),
        P(),
        P("dp", None, "space"),
        P(),
        P(),
        P(),
        P(),
        P(),
        P(),
    )
    return jax.shard_map(
        on_device,
        mesh=mesh,
        in_specs=placed,
        out_specs=(P("dp", None, "space"), P(), P(), P(), P(), P(), P(), P()),
        check_vma=False,
    )
```

time: 110 us -> 88 us (0.80)
  Pallas kernels: 0 us -> 37.9 us
  matrix products: 30.7 us -> 0 us
  local copies, waits for them, and re-layouts: 27.9 us -> 6.17 us
  other arithmetic: 11.8 us -> 3 us
  waiting for transfers between devices: 20.4 us -> 23.4 us
  between operations: 2.96 us -> 0.77 us
    pallas_call x0 -> x2, Pallas kernels: none -> 37.9 us  [the longest x1 35.9 us: on_device(): pl.pallas_call(functools.partial(step_kernel, count_all), out_shape=[jax....]
    dot_general x10 -> x0, matrix products: 30.7 us -> none  [the longest x8 27.5 us: product(): return jnp.einsum(form, left, right, preferred_element_type=jnp.float32)]
    reshape x6 -> x1, local copies, waits for them, and re-layouts: 9.24 us -> 0.67 us  [on_device(): owners = owner_map.reshape(peers, blocks)]
    reduce_sum x3 -> x0, other arithmetic: 6.83 us -> none  [the longest x2 5.1 us: block_sums(): jnp.sum(shaped, axis=(-3, -1))]
    broadcast_in_dim x5 -> x0, local copies, waits for them, and re-layouts: 5.76 us -> none  [the longest x4 5.76 us: backward_tile(): d_cells = jnp.repeat(jnp.repeat(d_cells, side, axis=2), side, axis=3)]
    ppermute x5, waiting for transfers between devices: 2.19 us -> 3.97 us  [swapped(): lax.ppermute(values, axis, [(i, i ^ bit) for i in range(lax.axis_size(axi...]
    another operation x4 -> x0, local copies, waits for them, and re-layouts: 1.63 us -> none  [the longest x1 0.8 us: backward_tile(): d_cells = d_block.reshape(members, pools, height // side, breadth // side)]
    concatenate x3 -> x0, other arithmetic: 1.54 us -> none  [the longest x1 0.86 us: padded_2(): block = jnp.concatenate([low, block, high], axis=dim)]
  transfers between devices with their start and end apart: 11 -> 11, of which waited for: 6 -> 9; matrix products, arithmetic and copies ran while one was open for 31% -> 4% of each run, Pallas kernels for 0% -> 0%
where the time goes in v2:
time: 88 us; the launch traced here: 87.5 us
  Pallas kernels  37.9 us (43%)
  waiting for transfers between devices  23.4 us (27%)
  starting transfers between devices  16.3 us (19%)
  local copies, waits for them, and re-layouts  6.17 us (7%)
  other arithmetic  3 us (3%)
    pallas_call x1, Pallas kernels, on_device(): pl.pallas_call(functools.partial(step_kernel, count_all), out_shape=[jax....  35.9 us
    ppermute x4, waiting for transfers between devices, crossed(): return lax.ppermute(values, ('dp', 'space'), pairs)  18 us
    ppermute x5, starting transfers between devices, swapped(): lax.ppermute(values, axis, [(i, i ^ bit) for i in range(lax.axis_size(axi...  8.94 us
    unnamed x19, local copies, waits for them, and re-layouts  4.84 us
    ppermute x4, starting transfers between devices, crossed(): return lax.ppermute(values, ('dp', 'space'), pairs)  4.64 us
    ppermute x5, waiting for transfers between devices, swapped(): lax.ppermute(values, axis, [(i, i ^ bit) for i in range(lax.axis_size(axi...  3.97 us
    pallas_call x1, Pallas kernels, on_device(): pl.pallas_call(functools.partial(finish_kernel, count_all), out_shape=[ja...  2 us
  transfers between devices with their start and end apart: 11, of which 9 were waited for; matrix products, arithmetic and copies ran while one was open for 4% of the time, Pallas kernels for 0%

profile of v2, /device:TPU:0, one launch (start us, length us, event | category | flops | bytes accessed | tf_op | source)
XLA Modules:
  0.0 87.5 jit_solution(5744504516430964203)
XLA Ops:
  0.6 0.7 copy.23
  1.3 0.5 collective-permute-start.2
  1.8 0.8 collective-permute-done.2
  2.6 2.9 %collective-permute-start.3 = (f32[2,14,192]{2,1,0:T(8,128)S(1)}, f32[2,14,192]{2,1,0:T(8,128)S(1)}, u32[]{:S(2)}, u32[]{:S(2)}) collective-permute-start(f32[2,14,192]{2,1,0:T(8,128)S(1)} %pad_maximum_fusion.4), channel_id=1, source_target_pairs={{0,2},{1,3},{2,0},{3,1},{4,6},{5,7},{6,4},{7,5},{8,10},{9,11},{10,... | collective-permute-start | bytes 64520 | tf_op jit(solution)/shard_map/ppermute | solution.py:332
  5.6 1.4 %copy.27 = bf16[1,32,96,128]{3,1,2,0:T(8,128)(2,1)S(1)} copy(bf16[1,32,96,128]{3,2,1,0:T(8,128)(2,1)} %param.11) | data formatting | bytes 1572864 | tf_op args[0]
  7.0 0.4 collective-permute-done.3
  7.5 3.1 %collective-permute-start.4 = (f32[4,14,192]{2,1,0:T(8,128)S(1)}, f32[4,14,192]{2,1,0:T(8,128)S(1)}, u32[]{:S(2)}, u32[]{:S(2)}) collective-permute-start(f32[4,14,192]{2,1,0:T(8,128)S(1)} %pad_maximum_fusion.3), channel_id=1, source_target_pairs={{0,4},{1,5},{2,6},{3,7},{4,0},{5,1},{6,2},{7,3},{8,12},{9,13},{10,... | collective-permute-start | bytes 129032 | tf_op jit(solution)/shard_map/ppermute | solution.py:332
  10.6 1.4 %collective-permute-start = (bf16[32,128]{1,0:T(8,128)(2,1)S(1)}, bf16[32,128]{1,0:T(8,128)(2,1)S(1)}, u32[]{:S(2)}, u32[]{:S(2)}) collective-permute-start(bf16[32,128]{1,0:T(8,128)(2,1)S(1)} %get-tuple-element.41), channel_id=1, source_target_pairs={{0,1},{1,2},{2,3},{3,4},{4,5},{5,6},{6,7},{8,9},{9,10},{10,11},{11... | collective-permute-start | bytes 24584 | tf_op jit(solution)/shard_map/ppermute | solution.py:400
  12.0 1.3 %collective-permute-start.1 = (bf16[32,128]{1,0:T(8,128)(2,1)S(1)}, bf16[32,128]{1,0:T(8,128)(2,1)S(1)}, u32[]{:S(2)}, u32[]{:S(2)}) collective-permute-start(bf16[32,128]{1,0:T(8,128)(2,1)S(1)} %get-tuple-element.40), channel_id=1, source_target_pairs={{1,0},{2,1},{3,2},{4,3},{5,4},{6,5},{7,6},{9,8},{10,9},{11,10},{12... | collective-permute-start | bytes 24584 | tf_op jit(solution)/shard_map/ppermute | solution.py:401
  13.3 0.7 reshape.49.owner_ref
  14.0 0.7 copy.24.w3_ref
  14.7 0.7 pad_maximum_fusion.2.target_ref
  15.4 1.5 %collective-permute-done.1.high_ref = bf16[32,128]{1,0:T(8,128)(2,1)S(1)} collective-permute-done((bf16[32,128]{1,0:T(8,128)(2,1)S(1)}, bf16[32,128]{1,0:T(8,128)(2,1)S(1)}, u32[]{:S(2)}, u32[]{:S(2)}) %collective-permute-start.1) | collective-permute-done | bytes 8224 | tf_op jit(solution)/shard_map/ppermute | solution.py:401
  16.9 0.6 copy-done.3
  17.5 35.9 %train_step.1 = (f32[224,128]{1,0:T(8,128)}, f32[256,128]{1,0:T(8,128)}, f32[32,128]{1,0:T(8,128)}) custom-call(bf16[96,32,128]{2,1,0:T(8,128)(2,1)} %bitcast.22, bf16[32,128]{1,0:T(8,128)(2,1)} %copy-done.2, bf16[32,128]{1,0:T(8,128)(2,1)} %copy-done.3, f32[96,128]{1,0:T(8,128)} %frac_ref.1, s32[96,128]{1,0:T(8,128)} %mask_ref.1, ...), custom_call_target="tpu_custom_call" | custom-call | tf_op jit(solution)/shard_map/train_step/pallas_call | solution.py:410
  53.4 2.4 %collective-permute-start.5 = (f32[256,128]{1,0:T(8,128)}, f32[256,128]{1,0:T(8,128)S(1)}, u32[]{:S(2)}, u32[]{:S(2)}) collective-permute-start(f32[256,128]{1,0:T(8,128)} %get-tuple-element.20), channel_id=1, source_target_pairs={{0,1},{1,0},{2,3},{3,2},{4,5},{5,4},{6,7},{7,6},{8,9},{9,8},{10,11... | collective-permute-start | bytes 393224 | tf_op jit(solution)/shard_map/ppermute | solution.py:332
  55.8 1.2 %collective-permute-done.5 = f32[256,128]{1,0:T(8,128)S(1)} collective-permute-done((f32[256,128]{1,0:T(8,128)}, f32[256,128]{1,0:T(8,128)S(1)}, u32[]{:S(2)}, u32[]{:S(2)}) %collective-permute-start.5) | collective-permute-done | bytes 131104 | tf_op jit(solution)/shard_map/ppermute | solution.py:332
  57.0 0.9 %slice_add_fusion.2 = f32[224,128]{1,0:T(8,128)S(1)} fusion(f32[224,128]{1,0:T(8,128)} %get-tuple-element.19, f32[256,128]{1,0:T(8,128)S(1)} %collective-permute-done.5), kind=kLoop, calls=%fused_computation.7 | loop fusion | flops 28672 | bytes 344064 | tf_op jit(solution)/shard_map/add | solution.py:360
  57.9 1.6 %collective-permute-start.6 = (f32[288,128]{1,0:T(8,128)S(1)}, f32[288,128]{1,0:T(8,128)S(1)}, u32[]{:S(2)}, u32[]{:S(2)}) collective-permute-start(f32[288,128]{1,0:T(8,128)S(1)} %pad_maximum_fusion.1), channel_id=1, source_target_pairs={{0,8},{1,3},{2,10},{3,1},{4,12},{5,7},{6,14},{7,5},{8,0},{9,11},{1... | collective-permute-start | bytes 442376 | tf_op jit(solution)/shard_map/ppermute | solution.py:351
  59.5 3.7 %collective-permute-done.6 = f32[288,128]{1,0:T(8,128)S(1)} collective-permute-done((f32[288,128]{1,0:T(8,128)S(1)}, f32[288,128]{1,0:T(8,128)S(1)}, u32[]{:S(2)}, u32[]{:S(2)}) %collective-permute-start.6) | collective-permute-done | bytes 147488 | tf_op jit(solution)/shard_map/ppermute | solution.py:351
  63.2 1.6 %collective-permute-start.7 = (f32[352,128]{1,0:T(8,128)S(1)}, f32[352,128]{1,0:T(8,128)S(1)}, u32[]{:S(2)}, u32[]{:S(2)}) collective-permute-start(f32[352,128]{1,0:T(8,128)S(1)} %pad_maximum_fusion), channel_id=1, source_target_pairs={{0,16},{1,5},{2,18},{3,7},{4,20},{5,1},{6,22},{7,3},{8,24},{9,13},... | collective-permute-start | bytes 540680 | tf_op jit(solution)/shard_map/ppermute | solution.py:351
  64.8 4.0 %collective-permute-done.7 = f32[352,128]{1,0:T(8,128)S(1)} collective-permute-done((f32[352,128]{1,0:T(8,128)S(1)}, f32[352,128]{1,0:T(8,128)S(1)}, u32[]{:S(2)}, u32[]{:S(2)}) %collective-permute-start.7) | collective-permute-done | bytes 180256 | tf_op jit(solution)/shard_map/ppermute | solution.py:351
  68.8 1.1 %collective-permute-start.8 = (f32[224,128]{1,0:T(8,128)S(1)}, f32[224,128]{1,0:T(8,128)S(1)}, u32[]{:S(2)}, u32[]{:S(2)}) collective-permute-start(f32[224,128]{1,0:T(8,128)S(1)} %slice_add_fusion), channel_id=1, source_target_pairs={{0,2},{1,9},{2,0},{3,11},{4,6},{5,13},{6,4},{7,15},{8,10},{9,1},{1... | collective-permute-start | bytes 344072 | tf_op jit(solution)/shard_map/ppermute | solution.py:351
  69.9 3.8 %collective-permute-done.8 = f32[224,128]{1,0:T(8,128)S(1)} collective-permute-done((f32[224,128]{1,0:T(8,128)S(1)}, f32[224,128]{1,0:T(8,128)S(1)}, u32[]{:S(2)}, u32[]{:S(2)}) %collective-permute-start.8) | collective-permute-done | bytes 114720 | tf_op jit(solution)/shard_map/ppermute | solution.py:351
  73.6 0.4 collective-permute-start.9
  74.0 6.6 %collective-permute-done.9 = f32[224,128]{1,0:T(8,128)S(1)} collective-permute-done((f32[224,128]{1,0:T(8,128)S(1)}, f32[224,128]{1,0:T(8,128)S(1)}, u32[]{:S(2)}, u32[]{:S(2)}) %collective-permute-start.9) | collective-permute-done | bytes 114720 | tf_op jit(solution)/shard_map/ppermute | solution.py:351
  80.6 0.7 constant_dynamic-update-slice_fusion.4
  81.4 1.5 %collective-permute-done.10 = f32[480,128]{1,0:T(8,128)S(1)} collective-permute-done((f32[480,128]{1,0:T(8,128)S(1)}, f32[480,128]{1,0:T(8,128)S(1)}, u32[]{:S(2)}, u32[]{:S(2)}) %collective-permute-start.10) | collective-permute-done | bytes 245792 | tf_op jit(solution)/shard_map/ppermute | solution.py:332
  82.9 0.6 slice.48.other_ref
  83.5 0.7 slice_select_fusion
  84.2 2.0 %finish.1 = (f32[14,192]{1,0:T(8,128)}, f32[288,128]{1,0:T(8,128)}, f32[1,128]{1,0:T(1,128)}, f32[128,128]{1,0:T(8,128)}, f32[1,128]{1,0:T(1,128)}, /*index=5*/f...) custom-call(f32[224,128]{1,0:T(8,128)} %get-tuple-element.39.half_ref, f32[224,128]{1,0:T(8,128)} %slice.48.other_ref, ...), custom_call_target="tpu_custom_call" | custom-call | tf_op jit(solution)/shard_map/finish/pallas_call | solution.py:456
  86.2 1.3 %copy.25 = f32[1,14,192]{2,0,1:T(1,128)} copy(f32[1,14,192]{2,1,0:T(8,128)} %bitcast.25) | data formatting | bytes 21504
  (28 shorter events, 0.2 us)
Async XLA Ops:
  1.3 1.3 %collective-permute-start.2 = (f32[1,14,192]{2,1,0:T(8,128)S(1)}, f32[1,14,192]{2,1,0:T(8,128)S(1)}, u32[]{:S(2)}, u32[]{:S(2)}) collective-permute-start(f32[1,14,192]{2,1,0:T(8,128)S(1)} %copy.23), channel_id=1, source_target_pairs={{0,1},{1,0},{2,3},{3,2},{4,5},{5,4},{6,7},{7,6},{8,9},{9,8},{10,11... | collective-permute-start | bytes 32264 | tf_op jit(solution)/shard_map/ppermute | solution.py:332
  2.6 4.8 %collective-permute-start.3 = (f32[2,14,192]{2,1,0:T(8,128)S(1)}, f32[2,14,192]{2,1,0:T(8,128)S(1)}, u32[]{:S(2)}, u32[]{:S(2)}) collective-permute-start(f32[2,14,192]{2,1,0:T(8,128)S(1)} %pad_maximum_fusion.4), channel_id=1, source_target_pairs={{0,2},{1,3},{2,0},{3,1},{4,6},{5,7},{6,4},{7,5},{8,10},{9,11},{10,... | collective-permute-start | bytes 64520 | tf_op jit(solution)/shard_map/ppermute | solution.py:332
  7.0 9.9 %copy-start = (bf16[1,32,96,128]{3,1,2,0:T(8,128)(2,1)}, bf16[1,32,96,128]{3,1,2,0:T(8,128)(2,1)S(1)}, u32[]{:S(2)}) copy-start(bf16[1,32,96,128]{3,1,2,0:T(8,128)(2,1)S(1)} %copy.27) | copy-start | bytes 2359300
  7.5 7.3 %collective-permute-start.4 = (f32[4,14,192]{2,1,0:T(8,128)S(1)}, f32[4,14,192]{2,1,0:T(8,128)S(1)}, u32[]{:S(2)}, u32[]{:S(2)}) collective-permute-start(f32[4,14,192]{2,1,0:T(8,128)S(1)} %pad_maximum_fusion.3), channel_id=1, source_target_pairs={{0,4},{1,5},{2,6},{3,7},{4,0},{5,1},{6,2},{7,3},{8,12},{9,13},{10,... | collective-permute-start | bytes 129032 | tf_op jit(solution)/shard_map/ppermute | solution.py:332
  10.6 2.7 %copy-start.4 = (s32[1536]{0:T(1024)S(1)}, s32[1536]{0:T(1024)}, u32[]{:S(2)}) copy-start(s32[1536]{0:T(1024)} %param.14) | copy-start | bytes 18436
  10.6 4.8 %collective-permute-start = (bf16[32,128]{1,0:T(8,128)(2,1)S(1)}, bf16[32,128]{1,0:T(8,128)(2,1)S(1)}, u32[]{:S(2)}, u32[]{:S(2)}) collective-permute-start(bf16[32,128]{1,0:T(8,128)(2,1)S(1)} %get-tuple-element.41), channel_id=1, source_target_pairs={{0,1},{1,2},{2,3},{3,4},{4,5},{5,6},{6,7},{8,9},{9,10},{10,11},{11... | collective-permute-start | bytes 24584 | tf_op jit(solution)/shard_map/ppermute | solution.py:400
  12.0 2.0 %copy-start.5 = (bf16[128,14]{0,1:T(8,128)(2,1)S(1)}, bf16[128,14]{0,1:T(8,128)(2,1)}, u32[]{:S(2)}) copy-start(bf16[128,14]{0,1:T(8,128)(2,1)} %param.20) | copy-start | bytes 10756
  12.0 4.9 %collective-permute-start.1 = (bf16[32,128]{1,0:T(8,128)(2,1)S(1)}, bf16[32,128]{1,0:T(8,128)(2,1)S(1)}, u32[]{:S(2)}, u32[]{:S(2)}) collective-permute-start(bf16[32,128]{1,0:T(8,128)(2,1)S(1)} %get-tuple-element.40), channel_id=1, source_target_pairs={{1,0},{2,1},{3,2},{4,3},{5,4},{6,5},{7,6},{9,8},{10,9},{11,10},{12... | collective-permute-start | bytes 24584 | tf_op jit(solution)/shard_map/ppermute | solution.py:401
  15.4 1.5 %copy-start.2 = (bf16[32,128]{1,0:T(8,128)(2,1)}, bf16[32,128]{1,0:T(8,128)(2,1)S(1)}, u32[]{:S(2)}) copy-start(bf16[32,128]{1,0:T(8,128)(2,1)S(1)} %collective-permute-done.low_ref) | copy-start | bytes 24580
  16.9 0.6 copy-start.3
  53.4 3.6 %collective-permute-start.5 = (f32[256,128]{1,0:T(8,128)}, f32[256,128]{1,0:T(8,128)S(1)}, u32[]{:S(2)}, u32[]{:S(2)}) collective-permute-start(f32[256,128]{1,0:T(8,128)} %get-tuple-element.20), channel_id=1, source_target_pairs={{0,1},{1,0},{2,3},{3,2},{4,5},{5,4},{6,7},{7,6},{8,9},{9,8},{10,11... | collective-permute-start | bytes 393224 | tf_op jit(solution)/shard_map/ppermute | solution.py:332
  57.0 0.9 %copy-start.1 = (f32[32,128]{1,0:T(8,128)S(1)}, f32[32,128]{1,0:T(8,128)}, u32[]{:S(2)}) copy-start(f32[32,128]{1,0:T(8,128)} %get-tuple-element.21) | copy-start | bytes 49156
  57.9 5.2 %collective-permute-start.6 = (f32[288,128]{1,0:T(8,128)S(1)}, f32[288,128]{1,0:T(8,128)S(1)}, u32[]{:S(2)}, u32[]{:S(2)}) collective-permute-start(f32[288,128]{1,0:T(8,128)S(1)} %pad_maximum_fusion.1), channel_id=1, source_target_pairs={{0,8},{1,3},{2,10},{3,1},{4,12},{5,7},{6,14},{7,5},{8,0},{9,11},{1... | collective-permute-start | bytes 442376 | tf_op jit(solution)/shard_map/ppermute | solution.py:351
  63.2 5.6 %collective-permute-start.7 = (f32[352,128]{1,0:T(8,128)S(1)}, f32[352,128]{1,0:T(8,128)S(1)}, u32[]{:S(2)}, u32[]{:S(2)}) collective-permute-start(f32[352,128]{1,0:T(8,128)S(1)} %pad_maximum_fusion), channel_id=1, source_target_pairs={{0,16},{1,5},{2,18},{3,7},{4,20},{5,1},{6,22},{7,3},{8,24},{9,13},... | collective-permute-start | bytes 540680 | tf_op jit(solution)/shard_map/ppermute | solution.py:351
  68.8 4.9 %collective-permute-start.8 = (f32[224,128]{1,0:T(8,128)S(1)}, f32[224,128]{1,0:T(8,128)S(1)}, u32[]{:S(2)}, u32[]{:S(2)}) collective-permute-start(f32[224,128]{1,0:T(8,128)S(1)} %slice_add_fusion), channel_id=1, source_target_pairs={{0,2},{1,9},{2,0},{3,11},{4,6},{5,13},{6,4},{7,15},{8,10},{9,1},{1... | collective-permute-start | bytes 344072 | tf_op jit(solution)/shard_map/ppermute | solution.py:351
  73.6 7.0 %collective-permute-start.9 = (f32[224,128]{1,0:T(8,128)S(1)}, f32[224,128]{1,0:T(8,128)S(1)}, u32[]{:S(2)}, u32[]{:S(2)}) collective-permute-start(f32[224,128]{1,0:T(8,128)S(1)} %add.22), channel_id=1, source_target_pairs={{0,4},{1,17},{2,6},{3,19},{4,0},{5,21},{6,2},{7,23},{8,12},{9,25},... | collective-permute-start | bytes 344072 | tf_op jit(solution)/shard_map/ppermute | solution.py:351
  81.3 1.6 %collective-permute-start.10 = (f32[480,128]{1,0:T(8,128)S(1)}, f32[480,128]{1,0:T(8,128)S(1)}, u32[]{:S(2)}, u32[]{:S(2)}) collective-permute-start(f32[480,128]{1,0:T(8,128)S(1)} %get-tuple-element.43), channel_id=1, source_target_pairs={{0,1},{1,0},{2,3},{3,2},{4,5},{5,4},{6,7},{7,6},{8,9},{9,8},{10,11... | collective-permute-start | bytes 737288 | tf_op jit(solution)/shard_map/ppermute | solution.py:332

commit v3 on v2

v3 whole, which is shorter than its diff:
```python
import functools
import math

import jax
import jax.numpy as jnp
from jax import lax
from jax.experimental import pallas as pl
from jax.experimental.pallas import tpu as pltpu
from jax.sharding import PartitionSpec as P

SIDE = 8
POOL_ROWS = 16
GROUP = 2
VMEM = 40 * 1024 * 1024

CUBIC = 0.044715
ROOT_TWO_PI = math.sqrt(2.0 / math.pi)

F32, BF16 = jnp.float32, jnp.bfloat16


def gelu_pair(pre):
    square = pre * pre
    half = 0.5 + 0.5 * jnp.tanh(pre * (ROOT_TWO_PI + (ROOT_TWO_PI * CUBIC) * square))
    value = pre * half
    slope = half + value * (1.0 - half) * (2.0 * ROOT_TWO_PI + (6.0 * ROOT_TWO_PI * CUBIC) * square)
    return value, slope


def mm(left, right):
    return jnp.dot(left, right, preferred_element_type=F32)


def mm_nt(left, right):
    return lax.dot_general(left, right, (((1,), (1,)), ((), ())), preferred_element_type=F32)


def thirds(values):
    high = values.astype(BF16)
    rest = values - high.astype(F32)
    middle = rest.astype(BF16)
    low = (rest - middle.astype(F32)).astype(BF16)
    return jnp.concatenate([high, middle, low], axis=0)


def picked(values, chosen):
    rows = values.shape[0]
    out = mm(thirds(values), chosen)
    return out[:rows] + out[rows : 2 * rows] + out[2 * rows :]


def ones_where(condition):
    return jnp.where(condition, 1.0, 0.0).astype(BF16)


def iota(shape, dim):
    return lax.broadcasted_iota(jnp.int32, shape, dim)


def owners_of(owner_ref, strip, blocks):
    at = strip * blocks
    row = at // 128
    pair = jnp.concatenate([owner_ref[pl.ds(row, 1), :], owner_ref[pl.ds(row + 1, 1), :]], axis=1)
    return jnp.where(at % 128 == 0, pair, pltpu.roll(pair, 256 - blocks % 128, 1))[:, :blocks]


def step_kernel(
    count_all,
    fields_ref,
    paired_ref,
    chained_ref,
    frac_ref,
    mask_ref,
    owner_ref,
    target_ref,
    w1_ref,
    b1_ref,
    w2_ref,
    b2_ref,
    w3t_ref,
    b3_ref,
    keep_ref,
    send_ref,
    coarse_ref,
    shifted,
    weight,
    w1t,
    w2t,
    w3t,
    w3p,
    pre_one,
    hidden_one,
    slope_one,
    hidden_two,
    slope_two,
    raw_all,
    scale,
    d_raw_all,
    d_two_all,
    d_one_all,
    total,
):
    rows, channels, cols = fields_ref.shape
    width = w2_ref.shape[0]
    pools = w3t_ref.shape[0]
    blocks = target_ref.shape[2]
    peers = target_ref.shape[0] // pools
    tiles = rows // SIDE
    across = cols // SIDE
    taps = 3 * channels
    conv_rows = 3 * taps
    cells = SIDE * cols
    position = lax.axis_index("space")
    core = lax.rem(position, 2)

    def with_bias(weights, bias):
        high = bias.astype(BF16).astype(F32)
        middle = (bias - high).astype(BF16).astype(F32)
        low = bias - high - middle
        fill = jnp.zeros((POOL_ROWS - 3, bias.shape[1]), F32)
        return jnp.concatenate([weights, high, middle, low, fill], axis=0).T

    w1t[...] = with_bias(w1_ref[...].astype(F32), b1_ref[...]).astype(BF16)
    w2t[...] = with_bias(w2_ref[...].astype(F32), b2_ref[...]).astype(BF16)
    w3f = jnp.concatenate([w3t_ref[...].astype(F32), jnp.zeros((width - pools, width), F32)], axis=0).T
    w3p[...] = w3f[:, :POOL_ROWS].astype(BF16)
    b3 = jnp.concatenate([b3_ref[...], jnp.zeros((1, width - pools), F32)], axis=1)
    w3t[...] = with_bias(w3f, b3)[:POOL_ROWS].astype(BF16)
    weight[...] = frac_ref[...] * mask_ref[...].astype(F32)

    lane = iota((channels, cols), 1)

    def put(row, values):
        values32 = values.astype(F32)
        left = jnp.where(lane == 0, 0.0, pltpu.roll(values32, 1, 1))
        right = jnp.where(lane == cols - 1, 0.0, pltpu.roll(values32, cols - 1, 1))
        shifted[pl.ds(pl.multiple_of(row * taps, taps), taps), :] = jnp.concatenate(
            [left.astype(BF16), values, right.astype(BF16)], axis=0
        )

    paired, chained = paired_ref[...].astype(F32), chained_ref[...].astype(F32)
    put(0, jnp.where(core == 0, chained, paired).astype(BF16))
    put(rows + 1, jnp.where(core == 0, paired, chained).astype(BF16))

    @pl.loop(0, rows // 8)
    def _(step):
        for inner in range(8):
            put(step * 8 + inner + 1, fields_ref[step * 8 + inner])

    ones = jnp.ones((POOL_ROWS, cells), BF16)

    def taps_of(row, count):
        parts = [
            shifted[pl.ds(pl.multiple_of((row + i) * taps, taps), conv_rows), :]
            for i in range(count)
        ]
        return jnp.concatenate(
            [jnp.concatenate(parts, axis=1), ones[:, : count * cols]], axis=0
        )

    def wide(values, count):
        return jnp.concatenate([values] * count, axis=1)

    part = GROUP * cols
    parts = [slice(at, at + part) for at in range(0, cells, part)]

    def first_layer(tile):
        for group, here in enumerate(parts):
            pre_one[lax.rem(tile, 2), :, here] = mm(w1t[...], taps_of(tile * SIDE + group * GROUP, GROUP))

    hidden_two[0] = jnp.zeros(hidden_two.shape[1:], BF16)
    first_layer(0)

    @pl.loop(0, tiles)
    def _(tile):
        following = jnp.minimum(tile + 1, tiles - 1)
        now = lax.rem(tile, 2)
        pre_twos = []
        for group, here in enumerate(parts):
            ahead = mm(w1t[...], taps_of(following * SIDE + group * GROUP, GROUP))
            value, slope = gelu_pair(pre_one[now, :, here])
            value = value.astype(BF16)
            hidden_one[tile, :, here] = value
            slope_one[tile, :, here] = slope
            pre_one[1 - now, :, here] = ahead
            pre_twos.append(mm(w2t[...], jnp.concatenate([value, ones[:, :part]], axis=0)))
        raw_all[tile] = mm(w3t[...], jnp.concatenate([hidden_two[tile], ones], axis=0))
        for here, pre_two in zip(parts, pre_twos):
            value, slope = gelu_pair(pre_two)
            hidden_two[tile + 1, :, here] = value.astype(BF16)
            slope_two[tile, :, here] = slope

    raw_all[tiles] = mm(w3t[...], jnp.concatenate([hidden_two[tiles], ones], axis=0))

    sums = []
    for tile in range(tiles):
        raw = raw_all[tile + 1]
        weights = jnp.concatenate(
            [
                jnp.broadcast_to(weight[tile * SIDE + i : tile * SIDE + i + 1, :], (POOL_ROWS, cols))
                for i in range(SIDE)
            ],
            axis=1,
        )
        small = jnp.exp(-jnp.abs(raw))
        density = (jnp.maximum(raw, 0.0) + jnp.log1p(small)) * weights
        scale[tile] = jnp.where(raw >= 0.0, 1.0, small) / (1.0 + small) * weights
        sums.append(sum(density[:, i * cols : (i + 1) * cols] for i in range(SIDE)))
    weight_cols = jnp.sum(weight[...].reshape(tiles, SIDE, cols), axis=1)
    weight_cols = jnp.concatenate([weight_cols, jnp.zeros((-tiles % 8, cols), F32)], axis=0)
    same = ones_where(iota((cols, cols), 0) // SIDE == iota((cols, cols), 1) // SIDE)
    summed = picked(jnp.concatenate(sums + [weight_cols], axis=0), same)
    owners = owners_of(owner_ref, position, blocks)
    target = jnp.zeros((POOL_ROWS, blocks), F32)
    for peer in range(peers):
        places = iota((blocks, blocks), 0) + (position ^ peer) * blocks
        values = jnp.concatenate(
            [
                target_ref[peer * pools : (peer + 1) * pools, 0, :],
                jnp.zeros((POOL_ROWS - pools, blocks), F32),
            ],
            axis=0,
        )
        target = target + picked(values, ones_where(places == owners))
    in_tile = iota((blocks, cols), 0) - iota((blocks, cols), 1) // SIDE
    spread = jnp.concatenate([ones_where(in_tile == tile * across) for tile in range(tiles)], axis=1)
    target_cols = picked(target, spread)
    first = iota((cols, blocks), 0)
    in_block = iota((cols, blocks), 1) - first // SIDE
    coarse = jnp.zeros((POOL_ROWS, blocks), F32)
    loss = jnp.zeros((POOL_ROWS, cols), F32)
    valid = iota((POOL_ROWS, cols), 0) < pools
    out_bias = jnp.zeros((POOL_ROWS, cols), F32)
    for tile in range(tiles):
        denom = jnp.maximum(summed[tiles * POOL_ROWS + tile : tiles * POOL_ROWS + tile + 1], 1.0)
        pred = summed[tile * POOL_ROWS : (tile + 1) * POOL_ROWS] / denom
        residual = jnp.where(valid, pred - target_cols[:, tile * cols : (tile + 1) * cols], 0.0)
        loss = loss + residual * residual
        d_cols = residual / (math.sqrt(count_all) * denom)
        d_raw = (wide(d_cols, SIDE) * scale[tile]).astype(BF16)
        d_raw_all[tile] = d_raw
        d_raw = d_raw.astype(F32)
        out_bias = out_bias + sum(d_raw[:, i * cols : (i + 1) * cols] for i in range(SIDE))
        leads = (first % SIDE == 0) & (in_block == tile * across)
        coarse = coarse + picked(pred, ones_where(leads))
    loss = jnp.sum(jnp.sum(loss, axis=1, keepdims=True), axis=0, keepdims=True) * (1.0 / SIDE)
    coarse_rows = jnp.concatenate(
        [
            coarse[:, :128],
            jnp.concatenate([coarse[:, 128:], jnp.zeros((POOL_ROWS, 256 - blocks), F32)], axis=1),
        ],
        axis=0,
    )
    coarse_ref[...] = coarse_rows

    mix_at = conv_rows
    out_at = mix_at + width
    bias_at = out_at + POOL_ROWS
    total[...] = jnp.zeros_like(total)

    def through(tile):
        now = lax.rem(tile, 2)
        d_twos = []
        for here in parts:
            d_two = (mm(w3p[...], d_raw_all[tile, :, here]) * slope_two[tile, :, here]).astype(BF16)
            d_two_all[now, :, here] = d_two
            d_twos.append(d_two)
        for here, d_two in zip(parts, d_twos):
            d_one = mm(w2_ref[...], d_two) * slope_one[tile, :, here]
            d_one_all[now, :, here] = d_one.astype(BF16)

    def add_up(tile):
        now = lax.rem(tile, 2)
        total[out_at:bias_at, :] += mm_nt(d_raw_all[tile], hidden_two[tile + 1])
        got = mm_nt(jnp.concatenate([hidden_one[tile], ones], axis=0), d_two_all[now])
        total[mix_at:out_at, :] += got[:width]
        total[bias_at + 8 : bias_at + 16, :] += got[width : width + 8]
        got = mm_nt(taps_of(tile * SIDE, SIDE), d_one_all[now])
        total[:conv_rows, :] += got[:conv_rows]
        total[bias_at : bias_at + 8, :] += got[conv_rows : conv_rows + 8]

    through(0)

    @pl.loop(1, tiles)
    def _(tile):
        add_up(tile - 1)
        through(tile)

    add_up(tiles - 1)

    bias = jnp.sum(out_bias, axis=1, keepdims=True)
    here, there = iota((POOL_ROWS, cols), 0), iota((POOL_ROWS, cols), 1)
    bias_row = jnp.sum(jnp.where(here == there, bias, 0.0), axis=0, keepdims=True)
    last = total[out_at:bias_at, :]
    last = jnp.where(here == pools, bias_row, last)
    total[out_at:bias_at, :] = jnp.where(here == pools + 1, loss, last)
    half = keep_ref.shape[0]
    keep_ref[...] = total[pl.ds(pl.multiple_of(core * half, 8), half), :]
    send_ref[:half, :] = total[pl.ds(pl.multiple_of((1 - core) * half, 8), half), :]
    send_ref[half:, :] = coarse_rows


def finish_kernel(
    count_all,
    mine_ref,
    other_ref,
    owner_ref,
    coarse_ref,
    conv_ref,
    conv_bias_ref,
    mix_ref,
    mix_bias_ref,
    out_ref,
    out_bias_ref,
    loss_ref,
):
    position = lax.axis_index("space")
    core = lax.rem(position, 2)
    pools, _, blocks = coarse_ref.shape
    conv_rows, width = conv_ref.shape
    out_at = conv_rows + width
    bias_at = out_at + POOL_ROWS
    half = (bias_at + POOL_ROWS) // 2
    peers = (mine_ref.shape[0] - half) // (2 * POOL_ROWS)
    mine, other = mine_ref[...], other_ref[...]
    low = jnp.where(core == 0, mine[:half], other[:half])
    high = jnp.where(core == 0, other[:half], mine[:half])
    gathered = jnp.where(core == 1, mine[half:], other[half:])
    total = jnp.concatenate([low, high], axis=0)
    conv_ref[...] = total[:conv_rows]
    mix_ref[...] = total[conv_rows:out_at]
    out_ref[...] = total[out_at : out_at + pools]
    out_bias_ref[...] = total[out_at + pools : out_at + pools + 1, :pools]
    loss_ref[...] = (0.5 / count_all) * total[out_at + pools + 1 : out_at + pools + 2, :1]
    conv_bias_ref[...] = total[bias_at : bias_at + 1]
    mix_bias_ref[...] = total[bias_at + 8 : bias_at + 9]
    base = position | 1
    coarse = jnp.zeros((POOL_ROWS, blocks), F32)
    for peer in range(peers):
        owners = owners_of(owner_ref, base ^ peer, blocks)
        places = iota((blocks, blocks), 0) + position * blocks
        at = peer * 2 * POOL_ROWS
        values = jnp.concatenate(
            [
                gathered[at : at + POOL_ROWS],
                gathered[at + POOL_ROWS : at + 2 * POOL_ROWS, : blocks - 128],
            ],
            axis=1,
        )
        got = mm_nt(thirds(values), ones_where(places == owners))
        coarse = coarse + got[:POOL_ROWS] + got[POOL_ROWS : 2 * POOL_ROWS] + got[2 * POOL_ROWS :]
    coarse_ref[:, 0, :] = coarse[:pools]


def bits_of(size, low):
    return [1 << k for k in range(size.bit_length() - 1) if (1 << k) >= low]


def swapped(values, axis, bit):
    return lax.ppermute(values, axis, [(i, i ^ bit) for i in range(lax.axis_size(axis))])


def gather_relative(values, axis, bits):
    for bit in bits:
        values = jnp.concatenate([values, swapped(values, axis, bit)], axis=0)
    return values


def crossed(values, step):
    dp, space = lax.axis_size("dp"), lax.axis_size("space")
    dp_moves = [(bit, 0) for bit in bits_of(dp, 1)]
    space_moves = [(0, bit) for bit in bits_of(space, 2)]
    orders = (dp_moves + space_moves, space_moves + dp_moves)
    pairs = []
    for d in range(dp):
        for s in range(space):
            d_bit, s_bit = orders[s % 2][step]
            pairs.append((d * space + s, (d ^ d_bit) * space + (s ^ s_bit)))
    return lax.ppermute(values, ("dp", "space"), pairs)


def reduce_all(keep, send, coarse):
    space = lax.axis_size("space")
    n_dp, n_space = len(bits_of(lax.axis_size("dp"), 1)), len(bits_of(space, 2))
    rows = keep.shape[0]
    got = swapped(send, "space", 1)
    half = keep + got[:rows]
    gathered = jnp.concatenate([coarse, got[rows:]], axis=0)
    for step in range(n_dp + n_space):
        if step < n_space:
            got = crossed(jnp.concatenate([half, gathered], axis=0), step)
            gathered = jnp.concatenate([gathered, got[rows:]], axis=0)
            got = got[:rows]
        else:
            got = crossed(half, step)
        half = half + got
    mine = jnp.concatenate([half, gathered], axis=0)
    return mine, swapped(mine, "space", 1)


def on_device(
    fields,
    land_mask,
    land_frac,
    owner_map,
    targets,
    conv_weight,
    conv_bias,
    mix_weight,
    mix_bias,
    out_weight,
    out_bias,
):
    peers = lax.axis_size("space")
    pools = out_weight.shape[1]
    width = mix_weight.shape[0]
    channels, rows, cols = fields.shape[1:]
    tiles = rows // SIDE
    blocks = tiles * (cols // SIDE)
    count_all = lax.axis_size("dp") * pools * owner_map.shape[0]
    owners = owner_map.reshape(-1, 128)
    core = lax.axis_index("space") % 2

    by_row = jnp.swapaxes(fields[0], 0, 1)
    top, bottom = by_row[0], by_row[rows - 1]
    chain = [(i, i + 1) for i in range(1, peers - 1, 2)]
    chain = chain + [(target, source) for source, target in chain]
    paired = swapped(jnp.where(core == 0, bottom, top), "space", 1)
    chained = lax.ppermute(jnp.where(core == 0, top, bottom), "space", chain)
    target_all = gather_relative(jnp.swapaxes(targets, 0, 1), "space", bits_of(peers, 1))

    conv_rows = 9 * channels
    half = conv_rows + width + 2 * POOL_ROWS
    half = (half + 31) // 32 * 16
    cells = SIDE * cols
    f32, bf16 = F32, BF16
    keep, send, coarse = pl.pallas_call(
        functools.partial(step_kernel, count_all),
        out_shape=[
            jax.ShapeDtypeStruct((half, width), f32),
            jax.ShapeDtypeStruct((half + 2 * POOL_ROWS, width), f32),
            jax.ShapeDtypeStruct((2 * POOL_ROWS, width), f32),
        ],
        in_specs=[pl.BlockSpec(memory_space=pltpu.VMEM)] * 13,
        out_specs=[pl.BlockSpec(memory_space=pltpu.VMEM)] * 3,
        scratch_shapes=[
            pltpu.VMEM(((rows + 2) * 3 * channels, cols), bf16),
            pltpu.VMEM((rows, cols), f32),
            pltpu.VMEM((width, conv_rows + POOL_ROWS), bf16),
            pltpu.VMEM((width, width + POOL_ROWS), bf16),
            pltpu.VMEM((POOL_ROWS, width + POOL_ROWS), bf16),
            pltpu.VMEM((width, POOL_ROWS), bf16),
            pltpu.VMEM((2, width, cells), f32),
            pltpu.VMEM((tiles, width, cells), bf16),
            pltpu.VMEM((tiles, width, cells), f32),
            pltpu.VMEM((tiles + 1, width, cells), bf16),
            pltpu.VMEM((tiles, width, cells), f32),
            pltpu.VMEM((tiles + 1, POOL_ROWS, cells), f32),
            pltpu.VMEM((tiles, POOL_ROWS, cells), f32),
            pltpu.VMEM((tiles, POOL_ROWS, cells), bf16),
            pltpu.VMEM((2, width, cells), bf16),
            pltpu.VMEM((2, width, cells), bf16),
            pltpu.VMEM((2 * half, width), f32),
        ],
        compiler_params=pltpu.CompilerParams(vmem_limit_bytes=VMEM),
        name="train_step",
    )(
        by_row,
        paired,
        chained,
        land_frac,
        land_mask,
        owners,
        target_all,
        conv_weight.reshape(conv_rows, width),
        conv_bias.reshape(1, width),
        mix_weight,
        mix_bias.reshape(1, width),
        out_weight.T,
        out_bias.reshape(1, pools),
    )
    mine, other = reduce_all(keep, send, coarse)
    outs = pl.pallas_call(
        functools.partial(finish_kernel, count_all),
        out_shape=[
            jax.ShapeDtypeStruct((pools, 1, blocks), f32),
            jax.ShapeDtypeStruct((conv_rows, width), f32),
            jax.ShapeDtypeStruct((1, width), f32),
            jax.ShapeDtypeStruct((width, width), f32),
            jax.ShapeDtypeStruct((1, width), f32),
            jax.ShapeDtypeStruct((pools, width), f32),
            jax.ShapeDtypeStruct((1, pools), f32),
            jax.ShapeDtypeStruct((1, 1), f32),
        ],
        in_specs=[pl.BlockSpec(memory_space=pltpu.VMEM)] * 3,
        out_specs=[pl.BlockSpec(memory_space=pltpu.VMEM)] * 8,
        compiler_params=pltpu.CompilerParams(vmem_limit_bytes=VMEM),
        name="finish",
    )(mine, other, owners)
    coarse_pred, conv_grad, conv_bias_grad, mix_grad, mix_bias_grad, out_grad, out_bias_grad, loss = outs
    return (
        jnp.swapaxes(coarse_pred, 0, 1),
        conv_grad.reshape(conv_weight.shape),
        conv_bias_grad.reshape(width),
        mix_grad,
        mix_bias_grad.reshape(width),
        out_grad.T,
        out_bias_grad.reshape(pools),
        loss.reshape(()),
    )


def solution(mesh):
    placed = (
        P("dp", None, "space", None),
        P("space", None),
        P("space", None),
        P(),
        P("dp", None, "space"),
        P(),
        P(),
        P(),
        P(),
        P(),
        P(),
    )
    return jax.shard_map(
        on_device,
        mesh=mesh,
        in_specs=placed,
        out_specs=(P("dp", None, "space"), P(), P(), P(), P(), P(), P(), P()),
        check_vma=False,
    )
```

time: 88 us -> 60.8 us (0.69)
  Pallas kernels: 37.9 us -> 19.8 us
  local copies, waits for them, and re-layouts: 6.17 us -> 2.14 us
  waiting for transfers between devices: 23.4 us -> 19.9 us
  other arithmetic: 3 us -> 1.01 us
    pallas_call x1, Pallas kernels: 35.9 us -> 18.8 us  [on_device(): pl.pallas_call(functools.partial(step_kernel, count_all), out_shape=[jax....]
    unnamed x19 -> x24, local copies, waits for them, and re-layouts: 4.84 us -> 2.13 us
    ppermute x4, waiting for transfers between devices: 18 us -> 15.3 us  [crossed(): return lax.ppermute(values, ('dp', 'space'), pairs)]
    ppermute x2 -> x1, starting transfers between devices: 2.7 us -> 0.65 us  [on_device(): chained = lax.ppermute(jnp.where(core == 0, top, bottom), 'space', chain)]
    ppermute x2 -> x1, waiting for transfers between devices: 1.49 us -> 0.01 us  [on_device(): chained = lax.ppermute(jnp.where(core == 0, top, bottom), 'space', chain)]
    ppermute x4, starting transfers between devices: 4.64 us -> 6.09 us  [crossed(): return lax.ppermute(values, ('dp', 'space'), pairs)]
    ppermute x5 -> x6, starting transfers between devices: 8.94 us -> 10.1 us  [swapped(): lax.ppermute(values, axis, [(i, i ^ bit) for i in range(lax.axis_size(axi...]
    pallas_call x1, Pallas kernels: 2 us -> 1.05 us  [on_device(): pl.pallas_call(functools.partial(finish_kernel, count_all), out_shape=[ja...]
  transfers between devices with their start and end apart: 11 -> 11, of which waited for: 9 -> 9; matrix products, arithmetic and copies ran while one was open for 4% -> 3% of each run, Pallas kernels for 0% -> 0%
where the time goes in v3:
time: 60.8 us; the launch traced here: 60.6 us
  waiting for transfers between devices  19.9 us (33%)
  Pallas kernels  19.8 us (33%)
  starting transfers between devices  16.9 us (28%)
  local copies, waits for them, and re-layouts  2.14 us (4%)
  other arithmetic  1.01 us (2%)
  between operations  0.83 us (1%)
    pallas_call x1, Pallas kernels, on_device(): pl.pallas_call(functools.partial(step_kernel, count_all), out_shape=[jax....  18.8 us
    ppermute x4, waiting for transfers between devices, crossed(): return lax.ppermute(values, ('dp', 'space'), pairs)  15.3 us
    ppermute x6, starting transfers between devices, swapped(): lax.ppermute(values, axis, [(i, i ^ bit) for i in range(lax.axis_size(axi...  10.1 us
    ppermute x4, starting transfers between devices, crossed(): return lax.ppermute(values, ('dp', 'space'), pairs)  6.09 us
    ppermute x6, waiting for transfers between devices, swapped(): lax.ppermute(values, axis, [(i, i ^ bit) for i in range(lax.axis_size(axi...  4.61 us
    unnamed x24, local copies, waits for them, and re-layouts  2.13 us
  transfers between devices with their start and end apart: 11, of which 9 were waited for; matrix products, arithmetic and copies ran while one was open for 3% of the time, Pallas kernels for 0%

profile of v3, /device:TPU:0, one launch (start us, length us, event | category | flops | bytes accessed | tf_op | source)
XLA Modules:
  0.0 60.6 jit_solution(16368347092656383778)
XLA Ops:
  0.6 0.5 collective-permute-start.2
  1.1 1.0 %collective-permute-done.2 = f32[14,1,192]{2,1,0:T(1,128)S(1)} collective-permute-done((f32[14,1,192]{2,1,0:T(1,128)}, f32[14,1,192]{2,1,0:T(1,128)S(1)}, u32[]{:S(2)}, u32[]{:S(2)}) %collective-permute-start.2) | collective-permute-done | bytes 10784 | tf_op jit(solution)/shard_map/ppermute | solution.py:360
  2.2 0.7 %pad_maximum_fusion.4 = f32[28,1,192]{2,1,0:T(1,128)S(1)} fusion(f32[14,1,192]{2,1,0:T(1,128)S(1)} %collective-permute-done.2, f32[14,1,192]{2,1,0:T(1,128)} %bitcast.33), kind=kLoop, calls=%fused_computation.10 | loop fusion | flops 5376 | bytes 43008 | tf_op jit(solution)/shard_map/concatenate | solution.py:365
  2.9 3.0 %collective-permute-start.3 = (f32[28,1,192]{2,1,0:T(1,128)S(1)}, f32[28,1,192]{2,1,0:T(1,128)S(1)}, u32[]{:S(2)}, u32[]{:S(2)}) collective-permute-start(f32[28,1,192]{2,1,0:T(1,128)S(1)} %pad_maximum_fusion.4), channel_id=1, source_target_pairs={{0,2},{1,3},{2,0},{3,1},{4,6},{5,7},{6,4},{7,5},{8,10},{9,11},{10,... | collective-permute-start | bytes 64520 | tf_op jit(solution)/shard_map/ppermute | solution.py:360
  5.9 1.5 %copy.21 = bf16[1,32,96,128]{3,1,2,0:T(8,128)(2,1)S(1)} copy(bf16[1,32,96,128]{3,2,1,0:T(8,128)(2,1)} %param.11) | data formatting | bytes 1572864 | tf_op args[0]
  7.4 0.4 collective-permute-done.3
  7.8 0.1 pad_maximum_fusion.3
  7.8 3.1 %collective-permute-start.4 = (f32[56,1,192]{2,1,0:T(1,128)S(1)}, f32[56,1,192]{2,1,0:T(1,128)S(1)}, u32[]{:S(2)}, u32[]{:S(2)}) collective-permute-start(f32[56,1,192]{2,1,0:T(1,128)S(1)} %pad_maximum_fusion.3), channel_id=1, source_target_pairs={{0,4},{1,5},{2,6},{3,7},{4,0},{5,1},{6,2},{7,3},{8,12},{9,13},{10,... | collective-permute-start | bytes 129032 | tf_op jit(solution)/shard_map/ppermute | solution.py:360
  10.9 0.6 %collective-permute-start.1 = (bf16[32,128]{1,0:T(8,128)(2,1)S(1)}, bf16[32,128]{1,0:T(8,128)(2,1)S(1)}, u32[]{:S(2)}, u32[]{:S(2)}) collective-permute-start(bf16[32,128]{1,0:T(8,128)(2,1)S(1)} %get-tuple-element.30), channel_id=1, source_target_pairs={{1,2},{3,4},{5,6},{2,1},{4,3},{6,5},{9,10},{11,12},{13,14},{10,9},... | collective-permute-start | bytes 24584 | tf_op jit(solution)/shard_map/ppermute | solution.py:429
  11.6 0.0 copy-start.1
  11.6 0.0 copy-start.2
  11.6 3.0 %collective-permute-start = (bf16[32,128]{1,0:T(8,128)(2,1)S(1)}, bf16[32,128]{1,0:T(8,128)(2,1)S(1)}, u32[]{:S(2)}, u32[]{:S(2)}) collective-permute-start(bf16[32,128]{1,0:T(8,128)(2,1)S(1)} %get-tuple-element.31), channel_id=1, source_target_pairs={{0,1},{1,0},{2,3},{3,2},{4,5},{5,4},{6,7},{7,6},{8,9},{9,8},{10,11... | collective-permute-start | bytes 24584 | tf_op jit(solution)/shard_map/ppermute | solution.py:360
  14.6 0.1 pad_maximum_fusion.2.target_ref
  14.8 0.0 copy-start.3
  14.8 0.7 %collective-permute-done.paired_ref = bf16[32,128]{1,0:T(8,128)(2,1)S(1)} collective-permute-done((bf16[32,128]{1,0:T(8,128)(2,1)S(1)}, bf16[32,128]{1,0:T(8,128)(2,1)S(1)}, u32[]{:S(2)}, u32[]{:S(2)}) %collective-permute-start) | collective-permute-done | bytes 8224 | tf_op jit(solution)/shard_map/ppermute | solution.py:360
  15.5 0.6 copy-done.6
  16.1 0.0 copy-done.7
  16.1 0.0 copy-done.8
  16.2 18.8 %train_step.1 = (f32[224,128]{1,0:T(8,128)S(1)}, f32[256,128]{1,0:T(8,128)S(1)}, f32[32,128]{1,0:T(8,128)S(1)}) custom-call(bf16[96,32,128]{2,1,0:T(8,128)(2,1)S(1)} %bitcast.24, bf16[32,128]{1,0:T(8,128)(2,1)S(1)} %collective-permute-done.paired_ref, bf16[32,128]{1,0:T(8,128)(2,1)S(1)} %collective-permute-done.1.chained_ref, f32[96,128]{1,0:T(8,128)S(1)} %copy-done.1, ...), custom_call_target="tpu_custom_call" | custom-call | tf_op jit(solution)/shard_map/train_step/pallas_call | solution.py:437
  34.9 0.5 collective-permute-start.5
  35.4 1.0 %collective-permute-done.5 = f32[256,128]{1,0:T(8,128)S(1)} collective-permute-done((f32[256,128]{1,0:T(8,128)S(1)}, f32[256,128]{1,0:T(8,128)S(1)}, u32[]{:S(2)}, u32[]{:S(2)}) %collective-permute-start.5) | collective-permute-done | bytes 131104 | tf_op jit(solution)/shard_map/ppermute | solution.py:360
  36.4 1.6 %collective-permute-start.6 = (f32[288,128]{1,0:T(8,128)S(1)}, f32[288,128]{1,0:T(8,128)S(1)}, u32[]{:S(2)}, u32[]{:S(2)}) collective-permute-start(f32[288,128]{1,0:T(8,128)S(1)} %pad_maximum_fusion.1), channel_id=1, source_target_pairs={{0,8},{1,3},{2,10},{3,1},{4,12},{5,7},{6,14},{7,5},{8,0},{9,11},{1... | collective-permute-start | bytes 442376 | tf_op jit(solution)/shard_map/ppermute | solution.py:379
  38.0 3.7 %collective-permute-done.6 = f32[288,128]{1,0:T(8,128)S(1)} collective-permute-done((f32[288,128]{1,0:T(8,128)S(1)}, f32[288,128]{1,0:T(8,128)S(1)}, u32[]{:S(2)}, u32[]{:S(2)}) %collective-permute-start.6) | collective-permute-done | bytes 147488 | tf_op jit(solution)/shard_map/ppermute | solution.py:379
  41.7 1.6 %collective-permute-start.7 = (f32[352,128]{1,0:T(8,128)S(1)}, f32[352,128]{1,0:T(8,128)S(1)}, u32[]{:S(2)}, u32[]{:S(2)}) collective-permute-start(f32[352,128]{1,0:T(8,128)S(1)} %pad_maximum_fusion), channel_id=1, source_target_pairs={{0,16},{1,5},{2,18},{3,7},{4,20},{5,1},{6,22},{7,3},{8,24},{9,13},... | collective-permute-start | bytes 540680 | tf_op jit(solution)/shard_map/ppermute | solution.py:379
  43.2 4.0 %collective-permute-done.7 = f32[352,128]{1,0:T(8,128)S(1)} collective-permute-done((f32[352,128]{1,0:T(8,128)S(1)}, f32[352,128]{1,0:T(8,128)S(1)}, u32[]{:S(2)}, u32[]{:S(2)}) %collective-permute-start.7) | collective-permute-done | bytes 180256 | tf_op jit(solution)/shard_map/ppermute | solution.py:379
  47.3 2.0 %collective-permute-start.8 = (f32[224,128]{1,0:T(8,128)S(1)}, f32[224,128]{1,0:T(8,128)S(1)}, u32[]{:S(2)}, u32[]{:S(2)}) collective-permute-start(f32[224,128]{1,0:T(8,128)S(1)} %slice_add_fusion), channel_id=1, source_target_pairs={{0,2},{1,9},{2,0},{3,11},{4,6},{5,13},{6,4},{7,15},{8,10},{9,1},{1... | collective-permute-start | bytes 344072 | tf_op jit(solution)/shard_map/ppermute | solution.py:379
  49.3 2.8 %collective-permute-done.8 = f32[224,128]{1,0:T(8,128)S(1)} collective-permute-done((f32[224,128]{1,0:T(8,128)S(1)}, f32[224,128]{1,0:T(8,128)S(1)}, u32[]{:S(2)}, u32[]{:S(2)}) %collective-permute-start.8) | collective-permute-done | bytes 114720 | tf_op jit(solution)/shard_map/ppermute | solution.py:379
  52.1 0.9 %collective-permute-start.9 = (f32[224,128]{1,0:T(8,128)S(1)}, f32[224,128]{1,0:T(8,128)S(1)}, u32[]{:S(2)}, u32[]{:S(2)}) collective-permute-start(f32[224,128]{1,0:T(8,128)S(1)} %add.23), channel_id=1, source_target_pairs={{0,4},{1,17},{2,6},{3,19},{4,0},{5,21},{6,2},{7,23},{8,12},{9,25},... | collective-permute-start | bytes 344072 | tf_op jit(solution)/shard_map/ppermute | solution.py:379
  53.1 4.8 %collective-permute-done.9 = f32[224,128]{1,0:T(8,128)S(1)} collective-permute-done((f32[224,128]{1,0:T(8,128)S(1)}, f32[224,128]{1,0:T(8,128)S(1)}, u32[]{:S(2)}, u32[]{:S(2)}) %collective-permute-start.9) | collective-permute-done | bytes 114720 | tf_op jit(solution)/shard_map/ppermute | solution.py:379
  58.0 0.1 collective-permute-start.10
  58.0 1.5 %collective-permute-done.10.other_ref = f32[480,128]{1,0:T(8,128)S(1)} collective-permute-done((f32[480,128]{1,0:T(8,128)S(1)}, f32[480,128]{1,0:T(8,128)S(1)}, u32[]{:S(2)}, u32[]{:S(2)}) %collective-permute-start.10) | collective-permute-done | bytes 245792 | tf_op jit(solution)/shard_map/ppermute | solution.py:360
  59.5 1.0 %finish.1 = (f32[14,1,192]{2,1,0:T(1,128)}, f32[288,128]{1,0:T(8,128)}, f32[1,128]{1,0:T(1,128)}, f32[128,128]{1,0:T(8,128)}, f32[1,128]{1,0:T(1,128)}, /*index=...) custom-call(f32[480,128]{1,0:T(8,128)S(1)} %slice_dynamic-update-slice_fusion.mine_ref, ...), custom_call_target="tpu_custom_call" | custom-call | tf_op jit(solution)/shard_map/finish/pallas_call | solution.py:483
  (30 shorter events, 0.2 us)
Async XLA Ops:
  0.6 1.6 %collective-permute-start.2 = (f32[14,1,192]{2,1,0:T(1,128)}, f32[14,1,192]{2,1,0:T(1,128)S(1)}, u32[]{:S(2)}, u32[]{:S(2)}) collective-permute-start(f32[14,1,192]{2,1,0:T(1,128)} %bitcast.32), channel_id=1, source_target_pairs={{0,1},{1,0},{2,3},{3,2},{4,5},{5,4},{6,7},{7,6},{8,9},{9,8},{10,11... | collective-permute-start | bytes 32264 | tf_op jit(solution)/shard_map/ppermute | solution.py:360
  2.9 4.8 %collective-permute-start.3 = (f32[28,1,192]{2,1,0:T(1,128)S(1)}, f32[28,1,192]{2,1,0:T(1,128)S(1)}, u32[]{:S(2)}, u32[]{:S(2)}) collective-permute-start(f32[28,1,192]{2,1,0:T(1,128)S(1)} %pad_maximum_fusion.4), channel_id=1, source_target_pairs={{0,2},{1,3},{2,0},{3,1},{4,6},{5,7},{6,4},{7,5},{8,10},{9,11},{10,... | collective-permute-start | bytes 64520 | tf_op jit(solution)/shard_map/ppermute | solution.py:360
  5.9 1.9 %copy-start.9 = (f32[1,14,192]{2,0,1:T(1,128)S(1)}, f32[1,14,192]{2,0,1:T(1,128)}, u32[]{:S(2)}) copy-start(f32[1,14,192]{2,0,1:T(1,128)} %param.15) | copy-start | bytes 32260
  7.8 6.8 %collective-permute-start.4 = (f32[56,1,192]{2,1,0:T(1,128)S(1)}, f32[56,1,192]{2,1,0:T(1,128)S(1)}, u32[]{:S(2)}, u32[]{:S(2)}) collective-permute-start(f32[56,1,192]{2,1,0:T(1,128)S(1)} %pad_maximum_fusion.3), channel_id=1, source_target_pairs={{0,4},{1,5},{2,6},{3,7},{4,0},{5,1},{6,2},{7,3},{8,12},{9,13},{10,... | collective-permute-start | bytes 129032 | tf_op jit(solution)/shard_map/ppermute | solution.py:360
  10.9 3.8 %collective-permute-start.1 = (bf16[32,128]{1,0:T(8,128)(2,1)S(1)}, bf16[32,128]{1,0:T(8,128)(2,1)S(1)}, u32[]{:S(2)}, u32[]{:S(2)}) collective-permute-start(bf16[32,128]{1,0:T(8,128)(2,1)S(1)} %get-tuple-element.30), channel_id=1, source_target_pairs={{1,2},{3,4},{5,6},{2,1},{4,3},{6,5},{9,10},{11,12},{13,14},{10,9},... | collective-permute-start | bytes 24584 | tf_op jit(solution)/shard_map/ppermute | solution.py:429
  11.6 3.9 %copy-start = (bf16[3,3,32,128]{3,2,1,0:T(8,128)(2,1)S(1)}, bf16[3,3,32,128]{3,2,1,0:T(8,128)(2,1)}, u32[]{:S(2)}) copy-start(bf16[3,3,32,128]{3,2,1,0:T(8,128)(2,1)} %param.16) | copy-start | bytes 221188
  11.6 3.9 %copy-start.1 = (f32[96,128]{1,0:T(8,128)S(1)}, f32[96,128]{1,0:T(8,128)}, u32[]{:S(2)}) copy-start(f32[96,128]{1,0:T(8,128)} %frac_ref.1) | copy-start | bytes 147460
  11.6 3.9 %copy-start.2 = (s32[96,128]{1,0:T(8,128)S(1)}, s32[96,128]{1,0:T(8,128)}, u32[]{:S(2)}) copy-start(s32[96,128]{1,0:T(8,128)} %mask_ref.1) | copy-start | bytes 147460
  11.6 3.8 %collective-permute-start = (bf16[32,128]{1,0:T(8,128)(2,1)S(1)}, bf16[32,128]{1,0:T(8,128)(2,1)S(1)}, u32[]{:S(2)}, u32[]{:S(2)}) collective-permute-start(bf16[32,128]{1,0:T(8,128)(2,1)S(1)} %get-tuple-element.31), channel_id=1, source_target_pairs={{0,1},{1,0},{2,3},{3,2},{4,5},{5,4},{6,7},{7,6},{8,9},{9,8},{10,11... | collective-permute-start | bytes 24584 | tf_op jit(solution)/shard_map/ppermute | solution.py:360
  14.6 0.9 %copy-start.4 = (bf16[128,128]{1,0:T(8,128)(2,1)S(1)}, bf16[128,128]{1,0:T(8,128)(2,1)}, u32[]{:S(2)}) copy-start(bf16[128,128]{1,0:T(8,128)(2,1)} %w2_ref.1) | copy-start | bytes 98308
  14.6 0.9 %copy-start.5 = (bf16[128,14]{0,1:T(8,128)(2,1)S(1)}, bf16[128,14]{0,1:T(8,128)(2,1)}, u32[]{:S(2)}) copy-start(bf16[128,14]{0,1:T(8,128)(2,1)} %param.20) | copy-start | bytes 10756
  14.8 0.8 %copy-start.3 = (s32[1536]{0:T(1024)S(1)}, s32[1536]{0:T(1024)}, u32[]{:S(2)}) copy-start(s32[1536]{0:T(1024)} %param.14) | copy-start | bytes 18436
  15.5 0.7 %copy-start.6 = (f32[128]{0:T(128)S(1)}, f32[128]{0:T(128)}, u32[]{:S(2)}) copy-start(f32[128]{0:T(128)} %param.17) | copy-start | bytes 1540
  15.5 0.7 %copy-start.7 = (f32[128]{0:T(128)S(1)}, f32[128]{0:T(128)}, u32[]{:S(2)}) copy-start(f32[128]{0:T(128)} %param.19) | copy-start | bytes 1540
  15.5 0.7 %copy-start.8 = (f32[14]{0:T(128)S(1)}, f32[14]{0:T(128)}, u32[]{:S(2)}) copy-start(f32[14]{0:T(128)} %param.21) | copy-start | bytes 172
  34.9 1.4 %collective-permute-start.5 = (f32[256,128]{1,0:T(8,128)S(1)}, f32[256,128]{1,0:T(8,128)S(1)}, u32[]{:S(2)}, u32[]{:S(2)}) collective-permute-start(f32[256,128]{1,0:T(8,128)S(1)} %get-tuple-element.20), channel_id=1, source_target_pairs={{0,1},{1,0},{2,3},{3,2},{4,5},{5,4},{6,7},{7,6},{8,9},{9,8},{10,11... | collective-permute-start | bytes 393224 | tf_op jit(solution)/shard_map/ppermute | solution.py:360
  36.4 5.2 %collective-permute-start.6 = (f32[288,128]{1,0:T(8,128)S(1)}, f32[288,128]{1,0:T(8,128)S(1)}, u32[]{:S(2)}, u32[]{:S(2)}) collective-permute-start(f32[288,128]{1,0:T(8,128)S(1)} %pad_maximum_fusion.1), channel_id=1, source_target_pairs={{0,8},{1,3},{2,10},{3,1},{4,12},{5,7},{6,14},{7,5},{8,0},{9,11},{1... | collective-permute-start | bytes 442376 | tf_op jit(solution)/shard_map/ppermute | solution.py:379
  41.7 5.6 %collective-permute-start.7 = (f32[352,128]{1,0:T(8,128)S(1)}, f32[352,128]{1,0:T(8,128)S(1)}, u32[]{:S(2)}, u32[]{:S(2)}) collective-permute-start(f32[352,128]{1,0:T(8,128)S(1)} %pad_maximum_fusion), channel_id=1, source_target_pairs={{0,16},{1,5},{2,18},{3,7},{4,20},{5,1},{6,22},{7,3},{8,24},{9,13},... | collective-permute-start | bytes 540680 | tf_op jit(solution)/shard_map/ppermute | solution.py:379
  47.3 4.9 %collective-permute-start.8 = (f32[224,128]{1,0:T(8,128)S(1)}, f32[224,128]{1,0:T(8,128)S(1)}, u32[]{:S(2)}, u32[]{:S(2)}) collective-permute-start(f32[224,128]{1,0:T(8,128)S(1)} %slice_add_fusion), channel_id=1, source_target_pairs={{0,2},{1,9},{2,0},{3,11},{4,6},{5,13},{6,4},{7,15},{8,10},{9,1},{1... | collective-permute-start | bytes 344072 | tf_op jit(solution)/shard_map/ppermute | solution.py:379
  52.1 5.8 %collective-permute-start.9 = (f32[224,128]{1,0:T(8,128)S(1)}, f32[224,128]{1,0:T(8,128)S(1)}, u32[]{:S(2)}, u32[]{:S(2)}) collective-permute-start(f32[224,128]{1,0:T(8,128)S(1)} %add.23), channel_id=1, source_target_pairs={{0,4},{1,17},{2,6},{3,19},{4,0},{5,21},{6,2},{7,23},{8,12},{9,25},... | collective-permute-start | bytes 344072 | tf_op jit(solution)/shard_map/ppermute | solution.py:379
  58.0 1.6 %collective-permute-start.10 = (f32[480,128]{1,0:T(8,128)S(1)}, f32[480,128]{1,0:T(8,128)S(1)}, u32[]{:S(2)}, u32[]{:S(2)}) collective-permute-start(f32[480,128]{1,0:T(8,128)S(1)} %slice_dynamic-update-slice_fusion.mine_ref), channel_id=1, source_target_pairs={{0,1},{1,0},{2,3},{3,2},{4,5},{5,4},{6,7},{7,6},{8,9},{9,8},{10,11... | collective-permute-start | bytes 737288 | tf_op jit(solution)/shard_map/ppermute | solution.py:360

commit v4 on v3

v4 whole, which is shorter than its diff:
```python
import functools
import math

import jax
import jax.numpy as jnp
from jax import lax
from jax.experimental import pallas as pl
from jax.experimental.pallas import tpu as pltpu
from jax.sharding import PartitionSpec as P

SIDE = 8
POOL_ROWS = 16
PACK_ROWS = 24
PART = 256
VMEM = 48 * 1024 * 1024

CUBIC = 0.044715
ROOT_TWO_PI = math.sqrt(2.0 / math.pi)

F32, BF16 = jnp.float32, jnp.bfloat16


def gelu_pair(pre):
    square = pre * pre
    half = 0.5 + 0.5 * jnp.tanh(pre * (ROOT_TWO_PI + (ROOT_TWO_PI * CUBIC) * square))
    value = pre * half
    slope = half + value * (1.0 - half) * (2.0 * ROOT_TWO_PI + (6.0 * ROOT_TWO_PI * CUBIC) * square)
    return value, slope


def mm(left, right):
    return jnp.dot(left, right, preferred_element_type=F32)


def mm_nt(left, right):
    return lax.dot_general(left, right, (((1,), (1,)), ((), ())), preferred_element_type=F32)


def thirds(values):
    high = values.astype(BF16)
    rest = values - high.astype(F32)
    middle = rest.astype(BF16)
    low = (rest - middle.astype(F32)).astype(BF16)
    return jnp.concatenate([high, middle, low], axis=0)


def picked(values, chosen):
    rows = values.shape[0]
    out = mm(thirds(values), chosen)
    return out[:rows] + out[rows : 2 * rows] + out[2 * rows :]


def ones_where(condition):
    return jnp.where(condition, 1.0, 0.0).astype(BF16)


def iota(shape, dim):
    return lax.broadcasted_iota(jnp.int32, shape, dim)


def pack(values):
    tails = jnp.concatenate([values[:8, 128:], values[8:, 128:]], axis=1)
    return jnp.concatenate([values[:, :128], tails], axis=0)


def unpack(packed, blocks):
    tails = packed[POOL_ROWS:]
    tails = jnp.concatenate([tails[:, : blocks - 128], tails[:, blocks - 128 :]], axis=0)
    return jnp.concatenate([packed[:POOL_ROWS], tails], axis=1)


def owners_of(owner_ref, strip, blocks):
    at = strip * blocks
    row = at // 128
    pair = jnp.concatenate([owner_ref[pl.ds(row, 1), :], owner_ref[pl.ds(row + 1, 1), :]], axis=1)
    return jnp.where(at % 128 == 0, pair, pltpu.roll(pair, 256 - blocks % 128, 1))[:, :blocks]


def step_kernel(
    count_all,
    masks,
    *refs,

):
    sent_ref, *got_refs = refs[: len(masks) + 1]
    fields_ref, frac_ref, mask_ref, owner_ref, w1_ref, b1_ref, w2_ref, b2_ref, w3t_ref, b3_ref = refs[
        len(masks) + 1 : len(masks) + 11
    ]
    keep_ref, send_ref, coarse_ref = refs[len(masks) + 11 : len(masks) + 14]
    shifted, weight, w1t, w2t, w2d, w3t, w3p, b3c, pre_one, pre_two, hidden_one, slope_one, hidden_two = refs[
        len(masks) + 14 : len(masks) + 27
    ]
    slope_two, raw_all, scale, d_raw_all, d_two_all, d_one_all, total = refs[len(masks) + 27 :]
    rows, channels, cols = fields_ref.shape
    width = w2_ref.shape[0]
    pools = w3t_ref.shape[0]
    tiles = rows // SIDE
    across = cols // SIDE
    blocks = tiles * across
    taps = 3 * channels
    conv_rows = 3 * taps
    cells = SIDE * cols // 2
    position = lax.axis_index("space")
    core = lax.rem(position, 2)

    def terms(bias):
        high = bias.astype(BF16).astype(F32)
        middle = (bias - high).astype(BF16).astype(F32)
        fill = jnp.zeros((POOL_ROWS - 3, bias.shape[1]), F32)
        return jnp.concatenate([high, middle, bias - high - middle, fill], axis=0)

    def twice(values):
        none = jnp.zeros_like(values)
        return jnp.concatenate(
            [jnp.concatenate([values, none], axis=1), jnp.concatenate([none, values], axis=1)], axis=0
        )

    def doubled(values):
        return jnp.concatenate([values, values], axis=1)

    first_weights, none = w1_ref[...].astype(F32), jnp.zeros((taps, width), F32)
    bias = terms(b1_ref[...])
    w1t[:width, :] = jnp.concatenate([first_weights, none, bias], axis=0).T.astype(BF16)
    w1t[width:, :] = jnp.concatenate([none, first_weights, bias], axis=0).T.astype(BF16)
    second_weights = twice(w2_ref[...].astype(F32))
    w2d[...] = second_weights.astype(BF16)
    w2t[...] = jnp.concatenate([second_weights, doubled(terms(b2_ref[...]))], axis=0).T.astype(BF16)
    last_weights = jnp.concatenate(
        [w3t_ref[...].astype(F32), jnp.zeros((POOL_ROWS - pools, width), F32)], axis=0
    )
    w3t[...] = twice(last_weights).astype(BF16)
    four = twice(twice(last_weights))
    w3p[...] = jnp.concatenate([four, jnp.zeros((128 - 4 * POOL_ROWS, 4 * width), F32)], axis=0).T[
        :, : 4 * POOL_ROWS
    ].astype(BF16)
    bias = jnp.concatenate([b3_ref[...], jnp.zeros((1, width - pools), F32)], axis=1)
    bias = jnp.broadcast_to(bias, (width, width)).T[:POOL_ROWS]
    b3c[...] = jnp.concatenate([bias, bias], axis=0)
    weight[...] = frac_ref[...] * mask_ref[...].astype(F32)

    lane = iota((channels, cols), 1)

    def put(row, values):
        values32 = values.astype(F32)
        left = jnp.where(lane == 0, 0.0, pltpu.roll(values32, 1, 1))
        right = jnp.where(lane == cols - 1, 0.0, pltpu.roll(values32, cols - 1, 1))
        shifted[pl.ds(pl.multiple_of(row * taps, taps), taps), :] = jnp.concatenate(
            [left.astype(BF16), values, right.astype(BF16)], axis=0
        )

    low = high = jnp.zeros((channels, cols), F32)
    for got_ref, mask in zip(got_refs, masks):
        row = got_ref[got_ref.shape[0] - channels :, :]
        low = jnp.where(position ^ mask == position - 1, row, low)
        high = jnp.where(position ^ mask == position + 1, row, high)
    put(0, low.astype(BF16))
    put(rows + 1, high.astype(BF16))

    @pl.loop(0, rows // 8)
    def _(step):
        for inner in range(8):
            put(step * 8 + inner + 1, fields_ref[step * 8 + inner])

    ones = jnp.ones((POOL_ROWS, cells), BF16)

    def taps_of(tile, start, count):
        parts = [
            shifted[pl.ds((tile * SIDE + 2 * (start + i)) * taps, 4 * taps), :]
            for i in range(count)
        ]
        return jnp.concatenate(
            [jnp.concatenate(parts, axis=1), ones[:, : count * cols]], axis=0
        )

    def wide(values, count):
        return jnp.concatenate([values] * count, axis=1)

    parts = [slice(at, at + PART) for at in range(0, cells, PART)]
    pairs = PART // cols

    def first_layer(tile, group):
        here = parts[group]
        pre_one[tile % 2, :, here] = mm(w1t[...], taps_of(tile, group * pairs, pairs))

    for group in range(len(parts)):
        first_layer(0, group)
    halves = (slice(0, width), slice(width, 2 * width))
    for tile in range(tiles):
        now = tile % 2
        for group, here in enumerate(parts):
            if tile + 1 < tiles:
                first_layer(tile + 1, group)
            for rows_of in halves:
                value, slope = gelu_pair(pre_one[now, rows_of, here])
                hidden_one[tile, rows_of, here] = value.astype(BF16)
                slope_one[tile, rows_of, here] = slope
            hidden = jnp.concatenate([hidden_one[tile, :, here], ones[:, :PART]], axis=0)
            pre_two[now, :, here] = mm(w2t[...], hidden)
        if tile > 0:
            raw_all[tile - 1] = mm(w3t[...], hidden_two[tile - 1])
        for here in parts:
            for rows_of in halves:
                value, slope = gelu_pair(pre_two[now, rows_of, here])
                hidden_two[tile, rows_of, here] = value.astype(BF16)
                slope_two[tile, rows_of, here] = slope
    raw_all[tiles - 1] = mm(w3t[...], hidden_two[tiles - 1])

    def over_rows(values):
        both = sum(values[:, i * cols : (i + 1) * cols] for i in range(SIDE // 2))
        return both[:POOL_ROWS] + both[POOL_ROWS:]

    sums = []
    for tile in range(tiles):
        raw = raw_all[tile] + wide(b3c[...], SIDE // 2)
        weights = [
            jnp.broadcast_to(weight[tile * SIDE + i : tile * SIDE + i + 1, :], (POOL_ROWS, cols))
            for i in range(SIDE)
        ]
        weights = jnp.concatenate(
            [jnp.concatenate(weights[i : i + 2], axis=0) for i in range(0, SIDE, 2)], axis=1
        )
        small = jnp.exp(-jnp.abs(raw))
        density = (jnp.maximum(raw, 0.0) + jnp.log1p(small)) * weights
        scale[tile] = jnp.where(raw >= 0.0, 1.0, small) / (1.0 + small) * weights
        sums.append(over_rows(density))
    weight_cols = jnp.sum(weight[...].reshape(tiles, SIDE, cols), axis=1)
    weight_cols = jnp.concatenate([weight_cols, jnp.zeros((-tiles % 8, cols), F32)], axis=0)
    same = ones_where(iota((cols, cols), 0) // SIDE == iota((cols, cols), 1) // SIDE)
    summed = picked(jnp.concatenate(sums + [weight_cols], axis=0), same)
    owners = owners_of(owner_ref, position, blocks)
    target = jnp.zeros((POOL_ROWS, blocks), F32)
    held = [(0, sent_ref, 0)]
    for got_ref, mask in zip(got_refs, masks):
        held = held + [(mask ^ other, got_ref, at) for at, (other, _, _) in enumerate(held)]
    for mask, ref, at in held:
        places = iota((blocks, blocks), 0) + (position ^ mask) * blocks
        packed = ref[at * PACK_ROWS : (at + 1) * PACK_ROWS, :]
        target = target + picked(unpack(packed, blocks), ones_where(places == owners))
    in_tile = iota((blocks, cols), 0) - iota((blocks, cols), 1) // SIDE
    spread = jnp.concatenate([ones_where(in_tile == tile * across) for tile in range(tiles)], axis=1)
    target_cols = picked(target, spread)
    first = iota((cols, blocks), 0)
    in_block = iota((cols, blocks), 1) - first // SIDE
    coarse = jnp.zeros((POOL_ROWS, blocks), F32)
    loss = jnp.zeros((POOL_ROWS, cols), F32)
    valid = iota((POOL_ROWS, cols), 0) < pools
    out_bias = jnp.zeros((POOL_ROWS, cols), F32)
    for tile in range(tiles):
        denom = jnp.maximum(summed[tiles * POOL_ROWS + tile : tiles * POOL_ROWS + tile + 1], 1.0)
        pred = summed[tile * POOL_ROWS : (tile + 1) * POOL_ROWS] / denom
        residual = jnp.where(valid, pred - target_cols[:, tile * cols : (tile + 1) * cols], 0.0)
        loss = loss + residual * residual
        d_cols = residual / (math.sqrt(count_all) * denom)
        d_cols = jnp.concatenate([d_cols, d_cols], axis=0)
        d_raw = (wide(d_cols, SIDE // 2) * scale[tile]).astype(BF16)
        d_raw_all[tile] = d_raw
        out_bias = out_bias + over_rows(d_raw.astype(F32))
        leads = (first % SIDE == 0) & (in_block == tile * across)
        coarse = coarse + picked(pred, ones_where(leads))
    loss = jnp.sum(jnp.sum(loss, axis=1, keepdims=True), axis=0, keepdims=True) * (1.0 / SIDE)
    coarse_rows = pack(coarse)
    coarse_ref[...] = coarse_rows

    mix_at = conv_rows
    out_at = mix_at + width
    bias_at = out_at + POOL_ROWS
    total[...] = jnp.zeros_like(total)

    def to_second(tile):
        d_raw = jnp.concatenate([d_raw_all[tile, :, here] for here in parts], axis=0)
        back = mm(w3p[...], d_raw)
        for group, here in enumerate(parts):
            d_two = back[2 * group * width : 2 * (group + 1) * width] * slope_two[tile, :, here]
            d_two_all[tile % 2, :, here] = d_two.astype(BF16)

    def to_first(tile):
        for here in parts:
            d_one = mm(w2d[...], d_two_all[tile % 2, :, here]) * slope_one[tile, :, here]
            d_one_all[tile % 2, :, here] = d_one.astype(BF16)

    def add_upper(tile):
        got = mm_nt(d_raw_all[tile], hidden_two[tile])
        total[out_at:bias_at, :] += got[:POOL_ROWS, :width] + got[POOL_ROWS:, width:]
        got = mm_nt(jnp.concatenate([hidden_one[tile], ones], axis=0), d_two_all[tile % 2])
        total[mix_at:out_at, :] += got[:width, :width] + got[width : 2 * width, width:]
        extra = got[2 * width : 2 * width + 8]
        total[bias_at + 8 : bias_at + 16, :] += extra[:, :width] + extra[:, width:]

    def add_lower(tile):
        got = mm_nt(taps_of(tile, 0, SIDE // 2), d_one_all[tile % 2])
        total[:conv_rows, :] += got[:conv_rows, :width] + got[taps : taps + conv_rows, width:]
        extra = got[taps + conv_rows : taps + conv_rows + 8]
        total[bias_at : bias_at + 8, :] += extra[:, :width] + extra[:, width:]

    to_second(0)
    to_first(0)
    for tile in range(1, tiles):
        to_second(tile)
        add_upper(tile - 1)
        to_first(tile)
        add_lower(tile - 1)
    add_upper(tiles - 1)
    add_lower(tiles - 1)

    bias = jnp.sum(out_bias, axis=1, keepdims=True)
    here, there = iota((POOL_ROWS, cols), 0), iota((POOL_ROWS, cols), 1)
    bias_row = jnp.sum(jnp.where(here == there, bias, 0.0), axis=0, keepdims=True)
    last = total[out_at:bias_at, :]
    last = jnp.where(here == pools, bias_row, last)
    total[out_at:bias_at, :] = jnp.where(here == pools + 1, loss, last)
    half = keep_ref.shape[0]
    keep_ref[...] = total[pl.ds(pl.multiple_of(core * half, 8), half), :]
    send_ref[:half, :] = total[pl.ds(pl.multiple_of((1 - core) * half, 8), half), :]
    send_ref[half:, :] = coarse_rows


def finish_kernel(
    count_all,
    mine_ref,
    other_ref,
    owner_ref,
    coarse_ref,
    conv_ref,
    conv_bias_ref,
    mix_ref,
    mix_bias_ref,
    out_ref,
    out_bias_ref,
    loss_ref,
):
    position = lax.axis_index("space")
    core = lax.rem(position, 2)
    pools, _, blocks = coarse_ref.shape
    conv_rows, width = conv_ref.shape
    out_at = conv_rows + width
    bias_at = out_at + POOL_ROWS
    half = (bias_at + POOL_ROWS) // 2
    peers = (mine_ref.shape[0] - half) // PACK_ROWS
    mine, other = mine_ref[...], other_ref[...]
    low = jnp.where(core == 0, mine[:half], other[:half])
    high = jnp.where(core == 0, other[:half], mine[:half])
    gathered = jnp.where(core == 1, mine[half:], other[half:])
    total = jnp.concatenate([low, high], axis=0)
    conv_ref[...] = total[:conv_rows]
    mix_ref[...] = total[conv_rows:out_at]
    out_ref[...] = total[out_at : out_at + pools]
    out_bias_ref[...] = total[out_at + pools : out_at + pools + 1, :pools]
    loss_ref[...] = (0.5 / count_all) * total[out_at + pools + 1 : out_at + pools + 2, :1]
    conv_bias_ref[...] = total[bias_at : bias_at + 1]
    mix_bias_ref[...] = total[bias_at + 8 : bias_at + 9]
    base = position | 1
    coarse = jnp.zeros((POOL_ROWS, blocks), F32)
    for peer in range(peers):
        owners = owners_of(owner_ref, base ^ peer, blocks)
        places = iota((blocks, blocks), 0) + position * blocks
        values = unpack(gathered[peer * PACK_ROWS : (peer + 1) * PACK_ROWS], blocks)
        got = mm_nt(thirds(values), ones_where(places == owners))
        coarse = coarse + got[:POOL_ROWS] + got[POOL_ROWS : 2 * POOL_ROWS] + got[2 * POOL_ROWS :]
    coarse_ref[:, 0, :] = coarse[:pools]


def bits_of(size, low):
    return [1 << k for k in range(size.bit_length() - 1) if (1 << k) >= low]


def swapped(values, axis, bit):
    return lax.ppermute(values, axis, [(i, i ^ bit) for i in range(lax.axis_size(axis))])


def crossed(values, step):
    dp, space = lax.axis_size("dp"), lax.axis_size("space")
    dp_moves = [(bit, 0) for bit in bits_of(dp, 1)]
    space_moves = [(0, bit) for bit in bits_of(space, 2)]
    orders = (dp_moves + space_moves, space_moves + dp_moves)
    pairs = []
    for d in range(dp):
        for s in range(space):
            d_bit, s_bit = orders[s % 2][step]
            pairs.append((d * space + s, (d ^ d_bit) * space + (s ^ s_bit)))
    return lax.ppermute(values, ("dp", "space"), pairs)


def reduce_all(keep, send, coarse):
    space = lax.axis_size("space")
    n_dp, n_space = len(bits_of(lax.axis_size("dp"), 1)), len(bits_of(space, 2))
    rows = keep.shape[0]
    got = swapped(send, "space", 1)
    half = keep + got[:rows]
    gathered = jnp.concatenate([coarse, got[rows:]], axis=0)
    for step in range(n_dp + n_space):
        if step < n_space:
            got = crossed(jnp.concatenate([half, gathered], axis=0), step)
            gathered = jnp.concatenate([gathered, got[rows:]], axis=0)
            got = got[:rows]
        else:
            got = crossed(half, step)
        half = half + got
    mine = jnp.concatenate([half, gathered], axis=0)
    return mine, swapped(mine, "space", 1)


def on_device(
    fields,
    land_mask,
    land_frac,
    owner_map,
    targets,
    conv_weight,
    conv_bias,
    mix_weight,
    mix_bias,
    out_weight,
    out_bias,
):
    peers = lax.axis_size("space")
    pools = out_weight.shape[1]
    width = mix_weight.shape[0]
    channels, rows, cols = fields.shape[1:]
    tiles = rows // SIDE
    blocks = tiles * (cols // SIDE)
    count_all = lax.axis_size("dp") * pools * owner_map.shape[0]
    owners = owner_map.reshape(-1, 128)
    position = lax.axis_index("space")
    masks = [2 * bit - 1 for bit in bits_of(peers, 2)] + [1]
    top, bottom = fields[0, :, 0, :].astype(F32), fields[0, :, rows - 1, :].astype(F32)
    held = pack(jnp.pad(targets[0], ((0, POOL_ROWS - pools), (0, 0))))
    gots = []
    for mask in masks:
        payload = jnp.concatenate([held, jnp.where(position ^ mask > position, bottom, top)], axis=0)
        if not gots:
            sent = payload
        got = swapped(payload, "space", mask)
        gots.append(got)
        held = jnp.concatenate([held, got[: held.shape[0]]], axis=0)
    by_row = jnp.swapaxes(fields[0], 0, 1)

    conv_rows = 9 * channels
    half = conv_rows + width + 2 * POOL_ROWS
    half = (half + 31) // 32 * 16
    cells = SIDE * cols // 2
    f32, bf16 = F32, BF16
    keep, send, coarse = pl.pallas_call(
        functools.partial(step_kernel, count_all, masks),
        out_shape=[
            jax.ShapeDtypeStruct((half, width), f32),
            jax.ShapeDtypeStruct((half + PACK_ROWS, width), f32),
            jax.ShapeDtypeStruct((PACK_ROWS, width), f32),
        ],
        in_specs=[pl.BlockSpec(memory_space=pltpu.VMEM)] * (len(masks) + 11),
        out_specs=[pl.BlockSpec(memory_space=pltpu.VMEM)] * 3,
        scratch_shapes=[
            pltpu.VMEM(((rows + 2) * 3 * channels, cols), bf16),
            pltpu.VMEM((rows, cols), f32),
            pltpu.VMEM((2 * width, conv_rows + 3 * channels + POOL_ROWS), bf16),
            pltpu.VMEM((2 * width, 2 * width + POOL_ROWS), bf16),
            pltpu.VMEM((2 * width, 2 * width), bf16),
            pltpu.VMEM((2 * POOL_ROWS, 2 * width), bf16),
            pltpu.VMEM((4 * width, 4 * POOL_ROWS), bf16),
            pltpu.VMEM((2 * POOL_ROWS, cols), f32),
            pltpu.VMEM((2, 2 * width, cells), f32),
            pltpu.VMEM((2, 2 * width, cells), f32),
            pltpu.VMEM((tiles, 2 * width, cells), bf16),
            pltpu.VMEM((tiles, 2 * width, cells), f32),
            pltpu.VMEM((tiles, 2 * width, cells), bf16),
            pltpu.VMEM((tiles, 2 * width, cells), f32),
            pltpu.VMEM((tiles, 2 * POOL_ROWS, cells), f32),
            pltpu.VMEM((tiles, 2 * POOL_ROWS, cells), f32),
            pltpu.VMEM((tiles, 2 * POOL_ROWS, cells), bf16),
            pltpu.VMEM((2, 2 * width, cells), bf16),
            pltpu.VMEM((2, 2 * width, cells), bf16),
            pltpu.VMEM((2 * half, width), f32),
        ],
        compiler_params=pltpu.CompilerParams(vmem_limit_bytes=VMEM),
        name="train_step",
    )(
        sent,
        *gots,
        by_row,
        land_frac,
        land_mask,
        owners,
        conv_weight.reshape(conv_rows, width),
        conv_bias.reshape(1, width),
        mix_weight,
        mix_bias.reshape(1, width),
        out_weight.T,
        out_bias.reshape(1, pools),
    )
    mine, other = reduce_all(keep, send, coarse)
    outs = pl.pallas_call(
        functools.partial(finish_kernel, count_all),
        out_shape=[
            jax.ShapeDtypeStruct((pools, 1, blocks), f32),
            jax.ShapeDtypeStruct((conv_rows, width), f32),
            jax.ShapeDtypeStruct((1, width), f32),
            jax.ShapeDtypeStruct((width, width), f32),
            jax.ShapeDtypeStruct((1, width), f32),
            jax.ShapeDtypeStruct((pools, width), f32),
            jax.ShapeDtypeStruct((1, pools), f32),
            jax.ShapeDtypeStruct((1, 1), f32),
        ],
        in_specs=[pl.BlockSpec(memory_space=pltpu.VMEM)] * 3,
        out_specs=[pl.BlockSpec(memory_space=pltpu.VMEM)] * 8,
        compiler_params=pltpu.CompilerParams(vmem_limit_bytes=VMEM),
        name="finish",
    )(mine, other, owners)
    coarse_pred, conv_grad, conv_bias_grad, mix_grad, mix_bias_grad, out_grad, out_bias_grad, loss = outs
    return (
        jnp.swapaxes(coarse_pred, 0, 1),
        conv_grad.reshape(conv_weight.shape),
        conv_bias_grad.reshape(width),
        mix_grad,
        mix_bias_grad.reshape(width),
        out_grad.T,
        out_bias_grad.reshape(pools),
        loss.reshape(()),
    )


def solution(mesh):
    placed = (
        P("dp", None, "space", None),
        P("space", None),
        P("space", None),
        P(),
        P("dp", None, "space"),
        P(),
        P(),
        P(),
        P(),
        P(),
        P(),
    )
    return jax.shard_map(
        on_device,
        mesh=mesh,
        in_specs=placed,
        out_specs=(P("dp", None, "space"), P(), P(), P(), P(), P(), P(), P()),
        check_vma=False,
    )
```

time: 60.8 us -> 54.5 us (0.90)
  Pallas kernels: 19.8 us -> 13.6 us
  starting transfers between devices: 16.9 us -> 14.1 us
  waiting for transfers between devices: 19.9 us -> 22.6 us
  local copies, waits for them, and re-layouts: 2.14 us -> 2.85 us
  other arithmetic: 1.01 us -> 0.35 us
    pallas_call x1, Pallas kernels: 18.8 us -> 12.5 us  [on_device(): pl.pallas_call(functools.partial(step_kernel, count_all, masks), out_shap...]
    ppermute x6 -> x5, starting transfers between devices: 10.1 us -> 7.54 us  [swapped(): lax.ppermute(values, axis, [(i, i ^ bit) for i in range(lax.axis_size(axi...]
    ppermute x6 -> x5, waiting for transfers between devices: 4.61 us -> 6.79 us  [swapped(): lax.ppermute(values, axis, [(i, i ^ bit) for i in range(lax.axis_size(axi...]
    concatenate x3, other arithmetic: 0.91 us -> 0.16 us  [on_device(): jnp.concatenate([held, jnp.where(position ^ mask > position, bottom, top)...]
    unnamed x24 -> x26, local copies, waits for them, and re-layouts: 2.13 us -> 2.83 us
    ppermute x1 -> x0, starting transfers between devices: 0.65 us -> none  [on_device(): chained = lax.ppermute(jnp.where(core == 0, top, bottom), 'space', chain)]
  transfers between devices with their start and end apart: 11 -> 9, of which waited for: 9 -> 9; matrix products, arithmetic and copies ran while one was open for 3% -> 0% of each run, Pallas kernels for 0% -> 0%
where the time goes in v4:
time: 54.5 us; the launch traced here: 54.3 us
  waiting for transfers between devices  22.6 us (41%)
  starting transfers between devices  14.1 us (26%)
  Pallas kernels  13.6 us (25%)
  local copies, waits for them, and re-layouts  2.85 us (5%)
  between operations  0.81 us (1%)
    ppermute x4, waiting for transfers between devices, crossed(): return lax.ppermute(values, ('dp', 'space'), pairs)  15.8 us
    pallas_call x1, Pallas kernels, on_device(): pl.pallas_call(functools.partial(step_kernel, count_all, masks), out_shap...  12.5 us
    ppermute x5, starting transfers between devices, swapped(): lax.ppermute(values, axis, [(i, i ^ bit) for i in range(lax.axis_size(axi...  7.54 us
    ppermute x5, waiting for transfers between devices, swapped(): lax.ppermute(values, axis, [(i, i ^ bit) for i in range(lax.axis_size(axi...  6.79 us
    ppermute x4, starting transfers between devices, crossed(): return lax.ppermute(values, ('dp', 'space'), pairs)  6.51 us
    unnamed x26, local copies, waits for them, and re-layouts  2.83 us
  transfers between devices with their start and end apart: 9, of which 9 were waited for; matrix products, arithmetic and copies ran while one was open for 0% of the time, Pallas kernels for 0%

profile of v4, /device:TPU:0, one launch (start us, length us, event | category | flops | bytes accessed | tf_op | source)
XLA Modules:
  0.0 54.3 jit_solution(17072790616592505235)
XLA Ops:
  0.6 0.7 %copy.26 = f32[1,14,192]{2,1,0:T(8,128)S(1)} copy(f32[1,14,192]{2,0,1:T(1,128)} %param.15) | data formatting | bytes 21504
  1.4 1.4 %copy.27 = bf16[1,32,96,128]{3,1,2,0:T(8,128)(2,1)S(1)} copy(bf16[1,32,96,128]{3,2,1,0:T(8,128)(2,1)} %param.11) | data formatting | bytes 1572864 | tf_op args[0]
  2.8 0.1 pad_maximum_fusion.3.refs_0_
  2.9 2.5 %collective-permute-start = (f32[56,128]{1,0:T(8,128)S(1)}, f32[56,128]{1,0:T(8,128)S(1)}, u32[]{:S(2)}, u32[]{:S(2)}) collective-permute-start(f32[56,128]{1,0:T(8,128)S(1)} %pad_maximum_fusion.3.refs_0_), channel_id=1, source_target_pairs={{0,3},{1,2},{2,1},{3,0},{4,7},{5,6},{6,5},{7,4},{8,11},{9,10},{10,... | collective-permute-start | bytes 86024 | tf_op jit(solution)/shard_map/ppermute | solution.py:367
  5.4 0.1 constant_dynamic-update-slice_fusion.2
  5.5 1.6 %collective-permute-done.refs_1_ = f32[56,128]{1,0:T(8,128)S(1)} collective-permute-done((f32[56,128]{1,0:T(8,128)S(1)}, f32[56,128]{1,0:T(8,128)S(1)}, u32[]{:S(2)}, u32[]{:S(2)}) %collective-permute-start) | collective-permute-done | bytes 28704 | tf_op jit(solution)/shard_map/ppermute | solution.py:367
  7.1 0.0 copy-start.5
  7.1 0.1 pad_maximum_fusion.2
  7.2 4.2 %collective-permute-start.1 = (f32[80,128]{1,0:T(8,128)S(1)}, f32[80,128]{1,0:T(8,128)S(1)}, u32[]{:S(2)}, u32[]{:S(2)}) collective-permute-start(f32[80,128]{1,0:T(8,128)S(1)} %pad_maximum_fusion.2), channel_id=1, source_target_pairs={{0,7},{1,6},{2,5},{3,4},{4,3},{5,2},{6,1},{7,0},{8,15},{9,14},{10,... | collective-permute-start | bytes 122888 | tf_op jit(solution)/shard_map/ppermute | solution.py:367
  11.4 1.8 %collective-permute-done.1.refs_2_ = f32[80,128]{1,0:T(8,128)S(1)} collective-permute-done((f32[80,128]{1,0:T(8,128)S(1)}, f32[80,128]{1,0:T(8,128)S(1)}, u32[]{:S(2)}, u32[]{:S(2)}) %collective-permute-start.1) | collective-permute-done | bytes 40992 | tf_op jit(solution)/shard_map/ppermute | solution.py:367
  13.2 0.4 collective-permute-start.2
  13.6 0.9 %collective-permute-done.2.refs_3_ = f32[128,128]{1,0:T(8,128)S(1)} collective-permute-done((f32[128,128]{1,0:T(8,128)S(1)}, f32[128,128]{1,0:T(8,128)S(1)}, u32[]{:S(2)}, u32[]{:S(2)}) %collective-permute-start.2) | collective-permute-done | bytes 65568 | tf_op jit(solution)/shard_map/ppermute | solution.py:367
  14.5 0.0 copy-done
  14.5 0.0 copy-done.3
  14.5 0.0 copy-done.5
  14.6 0.6 %copy-done.6 = f32[128]{0:T(128)S(1)} copy-done((f32[128]{0:T(128)S(1)}, f32[128]{0:T(128)}, u32[]{:S(2)}) %copy-start.6) | copy-done | bytes 536
  15.2 0.0 copy-done.7
  15.2 0.0 copy-done.8
  15.2 12.5 %train_step.1 = (f32[224,128]{1,0:T(8,128)S(1)}, f32[248,128]{1,0:T(8,128)S(1)}, f32[24,128]{1,0:T(8,128)S(1)}) custom-call(f32[56,128]{1,0:T(8,128)S(1)} %pad_maximum_fusion.3.refs_0_, f32[56,128]{1,0:T(8,128)S(1)} %collective-permute-done.refs_1_, f32[80,128]{1,0:T(8,128)S(1)} %collective-permute-done.1.refs_2_, ...), custom_call_target="tpu_custom_call" | custom-call | tf_op jit(solution)/shard_map/train_step/pallas_call | solution.py:442
  27.7 0.4 collective-permute-start.3
  28.1 1.0 %collective-permute-done.3 = f32[248,128]{1,0:T(8,128)S(1)} collective-permute-done((f32[248,128]{1,0:T(8,128)S(1)}, f32[248,128]{1,0:T(8,128)S(1)}, u32[]{:S(2)}, u32[]{:S(2)}) %collective-permute-start.3) | collective-permute-done | bytes 127008 | tf_op jit(solution)/shard_map/ppermute | solution.py:367
  29.2 1.7 %collective-permute-start.4 = (f32[272,128]{1,0:T(8,128)S(1)}, f32[272,128]{1,0:T(8,128)S(1)}, u32[]{:S(2)}, u32[]{:S(2)}) collective-permute-start(f32[272,128]{1,0:T(8,128)S(1)} %pad_maximum_fusion.1), channel_id=1, source_target_pairs={{0,8},{1,3},{2,10},{3,1},{4,12},{5,7},{6,14},{7,5},{8,0},{9,11},{1... | collective-permute-start | bytes 417800 | tf_op jit(solution)/shard_map/ppermute | solution.py:380
  30.8 3.5 %collective-permute-done.4 = f32[272,128]{1,0:T(8,128)S(1)} collective-permute-done((f32[272,128]{1,0:T(8,128)S(1)}, f32[272,128]{1,0:T(8,128)S(1)}, u32[]{:S(2)}, u32[]{:S(2)}) %collective-permute-start.4) | collective-permute-done | bytes 139296 | tf_op jit(solution)/shard_map/ppermute | solution.py:380
  34.4 1.7 %collective-permute-start.5 = (f32[320,128]{1,0:T(8,128)S(1)}, f32[320,128]{1,0:T(8,128)S(1)}, u32[]{:S(2)}, u32[]{:S(2)}) collective-permute-start(f32[320,128]{1,0:T(8,128)S(1)} %pad_maximum_fusion), channel_id=1, source_target_pairs={{0,16},{1,5},{2,18},{3,7},{4,20},{5,1},{6,22},{7,3},{8,24},{9,13},... | collective-permute-start | bytes 491528 | tf_op jit(solution)/shard_map/ppermute | solution.py:380
  36.0 3.7 %collective-permute-done.5 = f32[320,128]{1,0:T(8,128)S(1)} collective-permute-done((f32[320,128]{1,0:T(8,128)S(1)}, f32[320,128]{1,0:T(8,128)S(1)}, u32[]{:S(2)}, u32[]{:S(2)}) %collective-permute-start.5) | collective-permute-done | bytes 163872 | tf_op jit(solution)/shard_map/ppermute | solution.py:380
  39.8 0.7 %collective-permute-start.6 = (f32[224,128]{1,0:T(8,128)S(1)}, f32[224,128]{1,0:T(8,128)S(1)}, u32[]{:S(2)}, u32[]{:S(2)}) collective-permute-start(f32[224,128]{1,0:T(8,128)S(1)} %slice_add_fusion), channel_id=1, source_target_pairs={{0,2},{1,9},{2,0},{3,11},{4,6},{5,13},{6,4},{7,15},{8,10},{9,1},{1... | collective-permute-start | bytes 344072 | tf_op jit(solution)/shard_map/ppermute | solution.py:380
  40.5 4.1 %collective-permute-done.6 = f32[224,128]{1,0:T(8,128)S(1)} collective-permute-done((f32[224,128]{1,0:T(8,128)S(1)}, f32[224,128]{1,0:T(8,128)S(1)}, u32[]{:S(2)}, u32[]{:S(2)}) %collective-permute-start.6) | collective-permute-done | bytes 114720 | tf_op jit(solution)/shard_map/ppermute | solution.py:380
  44.6 2.5 %collective-permute-start.7 = (f32[224,128]{1,0:T(8,128)S(1)}, f32[224,128]{1,0:T(8,128)S(1)}, u32[]{:S(2)}, u32[]{:S(2)}) collective-permute-start(f32[224,128]{1,0:T(8,128)S(1)} %add.20), channel_id=1, source_target_pairs={{0,4},{1,17},{2,6},{3,19},{4,0},{5,21},{6,2},{7,23},{8,12},{9,25},... | collective-permute-start | bytes 344072 | tf_op jit(solution)/shard_map/ppermute | solution.py:380
  47.1 4.5 %collective-permute-done.7 = f32[224,128]{1,0:T(8,128)S(1)} collective-permute-done((f32[224,128]{1,0:T(8,128)S(1)}, f32[224,128]{1,0:T(8,128)S(1)}, u32[]{:S(2)}, u32[]{:S(2)}) %collective-permute-start.7) | collective-permute-done | bytes 114720 | tf_op jit(solution)/shard_map/ppermute | solution.py:380
  51.7 0.1 collective-permute-start.8
  51.8 1.5 %collective-permute-done.8.other_ref = f32[416,128]{1,0:T(8,128)S(1)} collective-permute-done((f32[416,128]{1,0:T(8,128)S(1)}, f32[416,128]{1,0:T(8,128)S(1)}, u32[]{:S(2)}, u32[]{:S(2)}) %collective-permute-start.8) | collective-permute-done | bytes 213024 | tf_op jit(solution)/shard_map/ppermute | solution.py:367
  53.2 1.0 %finish.1 = (f32[14,1,192]{2,1,0:T(1,128)}, f32[288,128]{1,0:T(8,128)}, f32[1,128]{1,0:T(1,128)}, f32[128,128]{1,0:T(8,128)}, f32[1,128]{1,0:T(1,128)}, /*index=...) custom-call(f32[416,128]{1,0:T(8,128)S(1)} %slice_dynamic-update-slice_fusion.mine_ref, ...), custom_call_target="tpu_custom_call" | custom-call | tf_op jit(solution)/shard_map/finish/pallas_call | solution.py:490
  (30 shorter events, 0.2 us)
Async XLA Ops:
  2.9 4.2 %collective-permute-start = (f32[56,128]{1,0:T(8,128)S(1)}, f32[56,128]{1,0:T(8,128)S(1)}, u32[]{:S(2)}, u32[]{:S(2)}) collective-permute-start(f32[56,128]{1,0:T(8,128)S(1)} %pad_maximum_fusion.3.refs_0_), channel_id=1, source_target_pairs={{0,3},{1,2},{2,1},{3,0},{4,7},{5,6},{6,5},{7,4},{8,11},{9,10},{10,... | collective-permute-start | bytes 86024 | tf_op jit(solution)/shard_map/ppermute | solution.py:367
  7.1 7.4 %copy-start.4 = (bf16[128,128]{1,0:T(8,128)(2,1)S(1)}, bf16[128,128]{1,0:T(8,128)(2,1)}, u32[]{:S(2)}) copy-start(bf16[128,128]{1,0:T(8,128)(2,1)} %refs_10_.1) | copy-start | bytes 98308
  7.1 7.4 %copy-start = (bf16[3,3,32,128]{3,2,1,0:T(8,128)(2,1)S(1)}, bf16[3,3,32,128]{3,2,1,0:T(8,128)(2,1)}, u32[]{:S(2)}) copy-start(bf16[3,3,32,128]{3,2,1,0:T(8,128)(2,1)} %param.16) | copy-start | bytes 221188
  7.1 7.5 %copy-start.3 = (s32[1536]{0:T(1024)S(1)}, s32[1536]{0:T(1024)}, u32[]{:S(2)}) copy-start(s32[1536]{0:T(1024)} %param.14) | copy-start | bytes 18436
  7.1 7.5 %copy-start.5 = (bf16[128,14]{0,1:T(8,128)(2,1)S(1)}, bf16[128,14]{0,1:T(8,128)(2,1)}, u32[]{:S(2)}) copy-start(bf16[128,14]{0,1:T(8,128)(2,1)} %param.20) | copy-start | bytes 10756
  7.2 6.0 %collective-permute-start.1 = (f32[80,128]{1,0:T(8,128)S(1)}, f32[80,128]{1,0:T(8,128)S(1)}, u32[]{:S(2)}, u32[]{:S(2)}) collective-permute-start(f32[80,128]{1,0:T(8,128)S(1)} %pad_maximum_fusion.2), channel_id=1, source_target_pairs={{0,7},{1,6},{2,5},{3,4},{4,3},{5,2},{6,1},{7,0},{8,15},{9,14},{10,... | collective-permute-start | bytes 122888 | tf_op jit(solution)/shard_map/ppermute | solution.py:367
  11.4 3.2 %copy-start.2 = (s32[96,128]{1,0:T(8,128)S(1)}, s32[96,128]{1,0:T(8,128)}, u32[]{:S(2)}) copy-start(s32[96,128]{1,0:T(8,128)} %refs_6_.1) | copy-start | bytes 147460
  11.4 3.2 %copy-start.1 = (f32[96,128]{1,0:T(8,128)S(1)}, f32[96,128]{1,0:T(8,128)}, u32[]{:S(2)}) copy-start(f32[96,128]{1,0:T(8,128)} %refs_5_.1) | copy-start | bytes 147460
  13.2 1.3 %collective-permute-start.2 = (f32[128,128]{1,0:T(8,128)S(1)}, f32[128,128]{1,0:T(8,128)S(1)}, u32[]{:S(2)}, u32[]{:S(2)}) collective-permute-start(f32[128,128]{1,0:T(8,128)S(1)} %constant_dynamic-update-slice_fusion), channel_id=1, source_target_pairs={{0,1},{1,0},{2,3},{3,2},{4,5},{5,4},{6,7},{7,6},{8,9},{9,8},{10,11... | collective-permute-start | bytes 196616 | tf_op jit(solution)/shard_map/ppermute | solution.py:367
  14.5 0.7 %copy-start.6 = (f32[128]{0:T(128)S(1)}, f32[128]{0:T(128)}, u32[]{:S(2)}) copy-start(f32[128]{0:T(128)} %param.17) | copy-start | bytes 1540
  14.5 0.7 %copy-start.7 = (f32[128]{0:T(128)S(1)}, f32[128]{0:T(128)}, u32[]{:S(2)}) copy-start(f32[128]{0:T(128)} %param.19) | copy-start | bytes 1540
  14.5 0.7 %copy-start.8 = (f32[14]{0:T(128)S(1)}, f32[14]{0:T(128)}, u32[]{:S(2)}) copy-start(f32[14]{0:T(128)} %param.21) | copy-start | bytes 172
  27.7 1.4 %collective-permute-start.3 = (f32[248,128]{1,0:T(8,128)S(1)}, f32[248,128]{1,0:T(8,128)S(1)}, u32[]{:S(2)}, u32[]{:S(2)}) collective-permute-start(f32[248,128]{1,0:T(8,128)S(1)} %get-tuple-element.20), channel_id=1, source_target_pairs={{0,1},{1,0},{2,3},{3,2},{4,5},{5,4},{6,7},{7,6},{8,9},{9,8},{10,11... | collective-permute-start | bytes 380936 | tf_op jit(solution)/shard_map/ppermute | solution.py:367
  29.2 5.1 %collective-permute-start.4 = (f32[272,128]{1,0:T(8,128)S(1)}, f32[272,128]{1,0:T(8,128)S(1)}, u32[]{:S(2)}, u32[]{:S(2)}) collective-permute-start(f32[272,128]{1,0:T(8,128)S(1)} %pad_maximum_fusion.1), channel_id=1, source_target_pairs={{0,8},{1,3},{2,10},{3,1},{4,12},{5,7},{6,14},{7,5},{8,0},{9,11},{1... | collective-permute-start | bytes 417800 | tf_op jit(solution)/shard_map/ppermute | solution.py:380
  34.4 5.4 %collective-permute-start.5 = (f32[320,128]{1,0:T(8,128)S(1)}, f32[320,128]{1,0:T(8,128)S(1)}, u32[]{:S(2)}, u32[]{:S(2)}) collective-permute-start(f32[320,128]{1,0:T(8,128)S(1)} %pad_maximum_fusion), channel_id=1, source_target_pairs={{0,16},{1,5},{2,18},{3,7},{4,20},{5,1},{6,22},{7,3},{8,24},{9,13},... | collective-permute-start | bytes 491528 | tf_op jit(solution)/shard_map/ppermute | solution.py:380
  39.8 4.9 %collective-permute-start.6 = (f32[224,128]{1,0:T(8,128)S(1)}, f32[224,128]{1,0:T(8,128)S(1)}, u32[]{:S(2)}, u32[]{:S(2)}) collective-permute-start(f32[224,128]{1,0:T(8,128)S(1)} %slice_add_fusion), channel_id=1, source_target_pairs={{0,2},{1,9},{2,0},{3,11},{4,6},{5,13},{6,4},{7,15},{8,10},{9,1},{1... | collective-permute-start | bytes 344072 | tf_op jit(solution)/shard_map/ppermute | solution.py:380
  44.6 7.0 %collective-permute-start.7 = (f32[224,128]{1,0:T(8,128)S(1)}, f32[224,128]{1,0:T(8,128)S(1)}, u32[]{:S(2)}, u32[]{:S(2)}) collective-permute-start(f32[224,128]{1,0:T(8,128)S(1)} %add.20), channel_id=1, source_target_pairs={{0,4},{1,17},{2,6},{3,19},{4,0},{5,21},{6,2},{7,23},{8,12},{9,25},... | collective-permute-start | bytes 344072 | tf_op jit(solution)/shard_map/ppermute | solution.py:380
  51.7 1.5 %collective-permute-start.8 = (f32[416,128]{1,0:T(8,128)S(1)}, f32[416,128]{1,0:T(8,128)S(1)}, u32[]{:S(2)}, u32[]{:S(2)}) collective-permute-start(f32[416,128]{1,0:T(8,128)S(1)} %slice_dynamic-update-slice_fusion.mine_ref), channel_id=1, source_target_pairs={{0,1},{1,0},{2,3},{3,2},{4,5},{5,4},{6,7},{7,6},{8,9},{9,8},{10,11... | collective-permute-start | bytes 638984 | tf_op jit(solution)/shard_map/ppermute | solution.py:367

commit v5 on v4

--- a/solution.py
+++ b/solution.py
@@ -12,7 +12,8 @@
 POOL_ROWS = 16
 PACK_ROWS = 24
 PART = 256
-VMEM = 48 * 1024 * 1024
+VMEM = 46 * 1024 * 1024
+PREPARE_VMEM = 8 * 1024 * 1024
 
 CUBIC = 0.044715
 ROOT_TWO_PI = math.sqrt(2.0 / math.pi)
@@ -76,32 +77,55 @@
     return jnp.where(at % 128 == 0, pair, pltpu.roll(pair, 256 - blocks % 128, 1))[:, :blocks]
 
 
-def step_kernel(
-    count_all,
-    masks,
-    *refs,
-
+def three_taps(row):
+    lane = iota(row.shape, 1)
+    last = row.shape[1] - 1
+    left = jnp.where(lane == 0, 0.0, pltpu.roll(row, 1, 1))
+    right = jnp.where(lane == last, 0.0, pltpu.roll(row, last, 1))
+    return jnp.concatenate([left, row, right], axis=0).astype(BF16)
+
+
+def pack_kernel(masks, top_ref, bottom_ref, target_ref, sent_ref, rows_ref):
+    position = lax.axis_index("space")
+    pools, _, blocks = target_ref.shape
+    channels = top_ref.shape[1]
+    edge = bottom_ref.shape[2] - 1
+    top = top_ref[0].astype(F32)[:, 0, :]
+    bottom = bottom_ref[0].astype(F32)[:, edge, :]
+    values = jnp.concatenate(
+        [target_ref[:, 0, :], jnp.zeros((POOL_ROWS - pools, blocks), F32)], axis=0
+    )
+    sent_ref[:PACK_ROWS, :] = pack(values)
+    for at, mask in enumerate(masks):
+        row = jnp.where(position ^ mask > position, bottom, top)
+        rows_ref[at] = row
+        if at == 0:
+            sent_ref[PACK_ROWS:, :] = row
+
+
+def prepare_kernel(
+    fields_ref,
+    frac_ref,
+    mask_ref,
+    w1_ref,
+    b1_ref,
+    w2_ref,
+    b2_ref,
+    w3t_ref,
+    b3_ref,
+    shifted,
+    weight,
+    w1t,
+    w2t,
+    w2d,
+    w3t,
+    w3p,
+    b3c,
 ):
-    sent_ref, *got_refs = refs[: len(masks) + 1]
-    fields_ref, frac_ref, mask_ref, owner_ref, w1_ref, b1_ref, w2_ref, b2_ref, w3t_ref, b3_ref = refs[
-        len(masks) + 1 : len(masks) + 11
-    ]
-    keep_ref, send_ref, coarse_ref = refs[len(masks) + 11 : len(masks) + 14]
-    shifted, weight, w1t, w2t, w2d, w3t, w3p, b3c, pre_one, pre_two, hidden_one, slope_one, hidden_two = refs[
-        len(masks) + 14 : len(masks) + 27
-    ]
-    slope_two, raw_all, scale, d_raw_all, d_two_all, d_one_all, total = refs[len(masks) + 27 :]
     rows, channels, cols = fields_ref.shape
     width = w2_ref.shape[0]
     pools = w3t_ref.shape[0]
-    tiles = rows // SIDE
-    across = cols // SIDE
-    blocks = tiles * across
     taps = 3 * channels
-    conv_rows = 3 * taps
-    cells = SIDE * cols // 2
-    position = lax.axis_index("space")
-    core = lax.rem(position, 2)
 
     def terms(bias):
         high = bias.astype(BF16).astype(F32)
@@ -138,36 +162,58 @@
     b3c[...] = jnp.concatenate([bias, bias], axis=0)
     weight[...] = frac_ref[...] * mask_ref[...].astype(F32)
 
-    lane = iota((channels, cols), 1)
-
-    def put(row, values):
-        values32 = values.astype(F32)
-        left = jnp.where(lane == 0, 0.0, pltpu.roll(values32, 1, 1))
-        right = jnp.where(lane == cols - 1, 0.0, pltpu.roll(values32, cols - 1, 1))
-        shifted[pl.ds(pl.multiple_of(row * taps, taps), taps), :] = jnp.concatenate(
-            [left.astype(BF16), values, right.astype(BF16)], axis=0
-        )
+    for row in range(rows):
+        shifted[row * taps : (row + 1) * taps, :] = three_taps(fields_ref[row].astype(F32))
+
+
+def step_kernel(
+    count_all,
+    masks,
+    pools,
+    *refs,
+
+):
+    sent_ref, *got_refs = refs[: len(masks) + 1]
+    owner_ref, shifted, weight, w1t, w2t, w2d, w3t, w3p, b3c = refs[len(masks) + 1 : len(masks) + 10]
+    keep_ref, send_ref, coarse_ref = refs[len(masks) + 10 : len(masks) + 13]
+    lower, upper, pre_one, pre_two, hidden_one, slope_one, hidden_two, slope_two = refs[
+        len(masks) + 13 : len(masks) + 21
+    ]
+    raw_all, scale, d_raw_all, d_two_all, d_one_all, total = refs[len(masks) + 21 :]
+    rows, cols = weight.shape
+    channels = lower.shape[0] // 12
+    width = w2d.shape[0] // 2
+    tiles = rows // SIDE
+    across = cols // SIDE
+    blocks = tiles * across
+    taps = 3 * channels
+    conv_rows = 3 * taps
+    cells = SIDE * cols // 2
+    position = lax.axis_index("space")
+    core = lax.rem(position, 2)
 
     low = high = jnp.zeros((channels, cols), F32)
     for got_ref, mask in zip(got_refs, masks):
         row = got_ref[got_ref.shape[0] - channels :, :]
         low = jnp.where(position ^ mask == position - 1, row, low)
         high = jnp.where(position ^ mask == position + 1, row, high)
-    put(0, low.astype(BF16))
-    put(rows + 1, high.astype(BF16))
-
-    @pl.loop(0, rows // 8)
-    def _(step):
-        for inner in range(8):
-            put(step * 8 + inner + 1, fields_ref[step * 8 + inner])
+    lower[:taps, :] = three_taps(low)
+    lower[taps:, :] = shifted[:conv_rows, :]
+    upper[:conv_rows, :] = shifted[rows * taps - conv_rows :, :]
+    upper[conv_rows:, :] = three_taps(high)
 
     ones = jnp.ones((POOL_ROWS, cells), BF16)
 
     def taps_of(tile, start, count):
-        parts = [
-            shifted[pl.ds((tile * SIDE + 2 * (start + i)) * taps, 4 * taps), :]
-            for i in range(count)
-        ]
+        parts = []
+        for i in range(start, start + count):
+            row = tile * SIDE + 2 * i - 1
+            if row < 0:
+                parts.append(lower[...])
+            elif row + 4 > rows:
+                parts.append(upper[...])
+            else:
+                parts.append(shifted[row * taps : (row + 4) * taps, :])
         return jnp.concatenate(
             [jnp.concatenate(parts, axis=1), ones[:, : count * cols]], axis=0
         )
@@ -422,34 +468,41 @@
     owners = owner_map.reshape(-1, 128)
     position = lax.axis_index("space")
     masks = [2 * bit - 1 for bit in bits_of(peers, 2)] + [1]
-    top, bottom = fields[0, :, 0, :].astype(F32), fields[0, :, rows - 1, :].astype(F32)
-    held = pack(jnp.pad(targets[0], ((0, POOL_ROWS - pools), (0, 0))))
-    gots = []
-    for mask in masks:
-        payload = jnp.concatenate([held, jnp.where(position ^ mask > position, bottom, top)], axis=0)
-        if not gots:
-            sent = payload
+    sent, edges = pl.pallas_call(
+        functools.partial(pack_kernel, masks),
+        out_shape=[
+            jax.ShapeDtypeStruct((PACK_ROWS + channels, cols), F32),
+            jax.ShapeDtypeStruct((len(masks), channels, cols), F32),
+        ],
+        grid=(1,),
+        in_specs=[
+            pl.BlockSpec((1, channels, 16, cols), lambda i: (0, 0, 0, 0)),
+            pl.BlockSpec((1, channels, 16, cols), lambda i: (0, 0, rows // 16 - 1, 0)),
+            pl.BlockSpec((pools, 1, blocks), lambda i: (0, 0, 0)),
+        ],
+        name="pack_edges",
+    )(fields, fields, jnp.swapaxes(targets, 0, 1))
+    payload, gots = sent, []
+    for at, mask in enumerate(masks):
+        if at > 0:
+            payload = jnp.concatenate([held, edges[at]], axis=0)
         got = swapped(payload, "space", mask)
         gots.append(got)
-        held = jnp.concatenate([held, got[: held.shape[0]]], axis=0)
-    by_row = jnp.swapaxes(fields[0], 0, 1)
+        had = payload.shape[0] - channels
+        held = jnp.concatenate([payload[:had], got[:had]], axis=0)
+    later, _ = lax.optimization_barrier((fields, sent))
+    by_row = jnp.swapaxes(later[0], 0, 1)
+    by_row, _ = lax.optimization_barrier((by_row, gots[0]))
 
     conv_rows = 9 * channels
     half = conv_rows + width + 2 * POOL_ROWS
     half = (half + 31) // 32 * 16
     cells = SIDE * cols // 2
     f32, bf16 = F32, BF16
-    keep, send, coarse = pl.pallas_call(
-        functools.partial(step_kernel, count_all, masks),
+    prepared = pl.pallas_call(
+        prepare_kernel,
         out_shape=[
-            jax.ShapeDtypeStruct((half, width), f32),
-            jax.ShapeDtypeStruct((half + PACK_ROWS, width), f32),
-            jax.ShapeDtypeStruct((PACK_ROWS, width), f32),
-        ],
-        in_specs=[pl.BlockSpec(memory_space=pltpu.VMEM)] * (len(masks) + 11),
-        out_specs=[pl.BlockSpec(memory_space=pltpu.VMEM)] * 3,
-        scratch_shapes=[
-            pltpu.VMEM(((rows + 2) * 3 * channels, cols), bf16),
+            pltpu.VMEM((rows * 3 * channels, cols), bf16),
             pltpu.VMEM((rows, cols), f32),
             pltpu.VMEM((2 * width, conv_rows + 3 * channels + POOL_ROWS), bf16),
             pltpu.VMEM((2 * width, 2 * width + POOL_ROWS), bf16),
@@ -457,6 +510,35 @@
             pltpu.VMEM((2 * POOL_ROWS, 2 * width), bf16),
             pltpu.VMEM((4 * width, 4 * POOL_ROWS), bf16),
             pltpu.VMEM((2 * POOL_ROWS, cols), f32),
+        ],
+        in_specs=[pl.BlockSpec(memory_space=pltpu.VMEM)] * 9,
+        out_specs=[pl.BlockSpec(memory_space=pltpu.VMEM)] * 8,
+        compiler_params=pltpu.CompilerParams(vmem_limit_bytes=PREPARE_VMEM),
+        cost_estimate=pl.CostEstimate(flops=10**9, bytes_accessed=4 * 10**6, transcendentals=0),
+        name="prepare",
+    )(
+        by_row,
+        land_frac,
+        land_mask,
+        conv_weight.reshape(conv_rows, width),
+        conv_bias.reshape(1, width),
+        mix_weight,
+        mix_bias.reshape(1, width),
+        out_weight.T,
+        out_bias.reshape(1, pools),
+    )
+    keep, send, coarse = pl.pallas_call(
+        functools.partial(step_kernel, count_all, masks, pools),
+        out_shape=[
+            jax.ShapeDtypeStruct((half, width), f32),
+            jax.ShapeDtypeStruct((half + PACK_ROWS, width), f32),
+            jax.ShapeDtypeStruct((PACK_ROWS, width), f32),
+        ],
+        in_specs=[pl.BlockSpec(memory_space=pltpu.VMEM)] * (len(masks) + 10),
+        out_specs=[pl.BlockSpec(memory_space=pltpu.VMEM)] * 3,
+        scratch_shapes=[
+            pltpu.VMEM((12 * channels, cols), bf16),
+            pltpu.VMEM((12 * channels, cols), bf16),
             pltpu.VMEM((2, 2 * width, cells), f32),
             pltpu.VMEM((2, 2 * width, cells), f32),
             pltpu.VMEM((tiles, 2 * width, cells), bf16),
@@ -475,16 +557,8 @@
     )(
         sent,
         *gots,
-        by_row,
-        land_frac,
-        land_mask,
         owners,
-        conv_weight.reshape(conv_rows, width),
-        conv_bias.reshape(1, width),
-        mix_weight,
-        mix_bias.reshape(1, width),
-        out_weight.T,
-        out_bias.reshape(1, pools),
+        *prepared,
     )
     mine, other = reduce_all(keep, send, coarse)
     outs = pl.pallas_call(

time: 54.5 us -> 52.9 us (0.971)
  waiting for transfers between devices: 22.6 us -> 19.3 us
  Pallas kernels: 13.6 us -> 15.1 us
    ppermute x5, waiting for transfers between devices: 6.79 us -> 3.45 us  [swapped(): lax.ppermute(values, axis, [(i, i ^ bit) for i in range(lax.axis_size(axi...]
    unnamed x26 -> x23, local copies, waits for them, and re-layouts: 2.83 us -> 0.06 us
    pallas_call x1 -> x3, Pallas kernels: 12.5 us -> 14.1 us  [the longest x1 11.7 us: on_device(): pl.pallas_call(functools.partial(step_kernel, count_all, masks, pools), o...]
    optimization_barrier x0 -> x1, local copies, waits for them, and re-layouts: none -> 1.44 us  [on_device(): later, _ = lax.optimization_barrier((fields, sent))]
    squeeze x0 -> x1, local copies, waits for them, and re-layouts: none -> 0.74 us  [on_device(): payload = jnp.concatenate([held, edges[at]], axis=0)]
    slice x1 -> x3, local copies, waits for them, and re-layouts: 0.01 us -> 0.71 us  [on_device(): held = jnp.concatenate([payload[:had], got[:had]], axis=0)]
  transfers between devices with their start and end apart: 9 -> 9, of which waited for: 9 -> 9; matrix products, arithmetic and copies ran while one was open for 0% -> 6% of each run, Pallas kernels for 0% -> 1%
where the time goes in v5:
time: 52.9 us; the launch traced here: 52.4 us
  waiting for transfers between devices  19.3 us (36%)
  Pallas kernels  15.1 us (29%)
  starting transfers between devices  14.2 us (27%)
  local copies, waits for them, and re-layouts  2.96 us (6%)
  between operations  0.85 us (2%)
    ppermute x4, waiting for transfers between devices, crossed(): return lax.ppermute(values, ('dp', 'space'), pairs)  15.8 us
    pallas_call x1, Pallas kernels, on_device(): pl.pallas_call(functools.partial(step_kernel, count_all, masks, pools), o...  11.7 us
    ppermute x5, starting transfers between devices, swapped(): lax.ppermute(values, axis, [(i, i ^ bit) for i in range(lax.axis_size(axi...  7.61 us
    ppermute x4, starting transfers between devices, crossed(): return lax.ppermute(values, ('dp', 'space'), pairs)  6.55 us
    ppermute x5, waiting for transfers between devices, swapped(): lax.ppermute(values, axis, [(i, i ^ bit) for i in range(lax.axis_size(axi...  3.45 us
    pallas_call x1, Pallas kernels, on_device(): pl.pallas_call(functools.partial(pack_kernel, masks), out_shape=[jax.Shap...  1.75 us
    optimization_barrier x1, local copies, waits for them, and re-layouts, on_device(): later, _ = lax.optimization_barrier((fields, sent))  1.44 us
  transfers between devices with their start and end apart: 9, of which 9 were waited for; matrix products, arithmetic and copies ran while one was open for 6% of the time, Pallas kernels for 1%

profile of v5, /device:TPU:0, one launch (start us, length us, event | category | flops | bytes accessed | tf_op | source)
XLA Modules:
  0.0 52.4 jit_solution(11402937550768110259)
XLA Ops:
  0.6 0.0 copy-start.9
  0.6 0.0 copy-start.6
  0.7 0.0 copy-start.8
  0.7 0.0 copy-start.5
  0.7 0.0 copy-start.7
  0.7 0.0 copy-start.2
  0.7 1.7 %pack_edges.1 = (f32[56,128]{1,0:T(8,128)}, f32[3,32,128]{2,1,0:T(8,128)}) custom-call(bf16[1,32,96,128]{3,2,1,0:T(8,128)(2,1)} %bottom_ref.1, bf16[1,32,96,128]{3,2,1,0:T(8,128)(2,1)} %bottom_ref.1, f32[14,1,192]{2,1,0:T(1,128)} %bitcast.31), custom_call_target="tpu_custom_call" | custom-call | tf_op jit(solution)/shard_map/pack_edges/pallas_call | solution.py:471
  2.5 2.5 %collective-permute-start = (f32[56,128]{1,0:T(8,128)}, f32[56,128]{1,0:T(8,128)S(1)}, u32[]{:S(2)}, u32[]{:S(2)}) collective-permute-start(f32[56,128]{1,0:T(8,128)} %get-tuple-element.31.refs_0_), channel_id=1, source_target_pairs={{0,3},{1,2},{2,1},{3,0},{4,7},{5,6},{6,5},{7,4},{8,11},{9,10},{10,... | collective-permute-start | bytes 86024 | tf_op jit(solution)/shard_map/ppermute | solution.py:413
  4.9 0.7 %slice_bitcast_fusion = (f32[32,128]{1,0:T(8,128)S(1)}, f32[32,128]{1,0:T(8,128)S(1)}) fusion(f32[3,32,128]{2,1,0:T(8,128)} %get-tuple-element.32), kind=kLoop, calls=%fused_computation.10 | loop fusion | bytes 65536 | tf_op jit(solution)/shard_map/squeeze | solution.py:488
  5.7 0.7 %slice.33 = f32[24,128]{1,0:T(8,128)S(1)} slice(f32[56,128]{1,0:T(8,128)} %get-tuple-element.31.refs_0_), slice={[0:24], [0:128]} | slice | bytes 24576 | tf_op jit(solution)/shard_map/slice | solution.py:492
  6.4 0.5 collective-permute-done.refs_1_
  6.8 0.0 copy-start.1
  6.9 4.3 %collective-permute-start.1 = (f32[80,128]{1,0:T(8,128)S(1)}, f32[80,128]{1,0:T(8,128)S(1)}, u32[]{:S(2)}, u32[]{:S(2)}) collective-permute-start(f32[80,128]{1,0:T(8,128)S(1)} %pad_maximum_fusion.3), channel_id=1, source_target_pairs={{0,7},{1,6},{2,5},{3,4},{4,3},{5,2},{6,1},{7,0},{8,15},{9,14},{10,... | collective-permute-start | bytes 122888 | tf_op jit(solution)/shard_map/ppermute | solution.py:413
  11.1 1.4 %copy.21 = bf16[1,32,96,128]{3,1,2,0:T(8,128)(2,1)S(1)} copy(bf16[1,32,96,128]{3,2,1,0:T(8,128)(2,1)} %bottom_ref.1) | data formatting | bytes 1572864 | tf_op jit(solution)/shard_map/optimization_barrier | solution.py:493
  12.6 0.4 collective-permute-done.1.refs_2_
  12.9 0.4 collective-permute-start.2
  13.4 0.7 %prepare.1 = (bf16[9216,128]{1,0:T(8,128)(2,1)S(1)}, f32[96,128]{1,0:T(8,128)S(1)}, bf16[256,400]{1,0:T(8,128)(2,1)S(1)}, bf16[256,272]{1,0:T(8,128)(2,1)S(1)}, ...) custom-call(bf16[96,32,128]{2,1,0:T(8,128)(2,1)S(1)} %bitcast.23, ...), custom_call_target="tpu_custom_call" | custom-call | flops 1000000000 | bytes 4000000 | tf_op jit(solution)/shard_map/prepare/pallas_call | solution.py:502
  14.1 0.2 collective-permute-done.2.refs_3_
  14.3 11.7 %train_step.1 = (f32[224,128]{1,0:T(8,128)S(1)}, f32[248,128]{1,0:T(8,128)S(1)}, f32[24,128]{1,0:T(8,128)S(1)}) custom-call(f32[56,128]{1,0:T(8,128)S(1)} %copy-done, f32[56,128]{1,0:T(8,128)S(1)} %collective-permute-done.refs_1_, f32[80,128]{1,0:T(8,128)S(1)} %collective-permute-done.1.refs_2_, f32[128,128]{1,0:T(8,128)S(1)} %collective-permute-done.2.refs_3_, ...), custom_call_target="tpu_custom_call" | custom-call | tf_op jit(solution)/shard_map/train_step/pallas_call | solution.py:530
  25.9 0.4 collective-permute-start.3
  26.3 1.0 %collective-permute-done.3 = f32[248,128]{1,0:T(8,128)S(1)} collective-permute-done((f32[248,128]{1,0:T(8,128)S(1)}, f32[248,128]{1,0:T(8,128)S(1)}, u32[]{:S(2)}, u32[]{:S(2)}) %collective-permute-start.3) | collective-permute-done | bytes 127008 | tf_op jit(solution)/shard_map/ppermute | solution.py:413
  27.4 1.7 %collective-permute-start.4 = (f32[272,128]{1,0:T(8,128)S(1)}, f32[272,128]{1,0:T(8,128)S(1)}, u32[]{:S(2)}, u32[]{:S(2)}) collective-permute-start(f32[272,128]{1,0:T(8,128)S(1)} %pad_maximum_fusion.1), channel_id=1, source_target_pairs={{0,8},{1,3},{2,10},{3,1},{4,12},{5,7},{6,14},{7,5},{8,0},{9,11},{1... | collective-permute-start | bytes 417800 | tf_op jit(solution)/shard_map/ppermute | solution.py:426
  29.0 3.5 %collective-permute-done.4 = f32[272,128]{1,0:T(8,128)S(1)} collective-permute-done((f32[272,128]{1,0:T(8,128)S(1)}, f32[272,128]{1,0:T(8,128)S(1)}, u32[]{:S(2)}, u32[]{:S(2)}) %collective-permute-start.4) | collective-permute-done | bytes 139296 | tf_op jit(solution)/shard_map/ppermute | solution.py:426
  32.5 1.7 %collective-permute-start.5 = (f32[320,128]{1,0:T(8,128)S(1)}, f32[320,128]{1,0:T(8,128)S(1)}, u32[]{:S(2)}, u32[]{:S(2)}) collective-permute-start(f32[320,128]{1,0:T(8,128)S(1)} %pad_maximum_fusion), channel_id=1, source_target_pairs={{0,16},{1,5},{2,18},{3,7},{4,20},{5,1},{6,22},{7,3},{8,24},{9,13},... | collective-permute-start | bytes 491528 | tf_op jit(solution)/shard_map/ppermute | solution.py:426
  34.2 3.7 %collective-permute-done.5 = f32[320,128]{1,0:T(8,128)S(1)} collective-permute-done((f32[320,128]{1,0:T(8,128)S(1)}, f32[320,128]{1,0:T(8,128)S(1)}, u32[]{:S(2)}, u32[]{:S(2)}) %collective-permute-start.5) | collective-permute-done | bytes 163872 | tf_op jit(solution)/shard_map/ppermute | solution.py:426
  37.9 0.7 %collective-permute-start.6 = (f32[224,128]{1,0:T(8,128)S(1)}, f32[224,128]{1,0:T(8,128)S(1)}, u32[]{:S(2)}, u32[]{:S(2)}) collective-permute-start(f32[224,128]{1,0:T(8,128)S(1)} %slice_add_fusion), channel_id=1, source_target_pairs={{0,2},{1,9},{2,0},{3,11},{4,6},{5,13},{6,4},{7,15},{8,10},{9,1},{1... | collective-permute-start | bytes 344072 | tf_op jit(solution)/shard_map/ppermute | solution.py:426
  38.7 4.1 %collective-permute-done.6 = f32[224,128]{1,0:T(8,128)S(1)} collective-permute-done((f32[224,128]{1,0:T(8,128)S(1)}, f32[224,128]{1,0:T(8,128)S(1)}, u32[]{:S(2)}, u32[]{:S(2)}) %collective-permute-start.6) | collective-permute-done | bytes 114720 | tf_op jit(solution)/shard_map/ppermute | solution.py:426
  42.8 2.5 %collective-permute-start.7 = (f32[224,128]{1,0:T(8,128)S(1)}, f32[224,128]{1,0:T(8,128)S(1)}, u32[]{:S(2)}, u32[]{:S(2)}) collective-permute-start(f32[224,128]{1,0:T(8,128)S(1)} %add.18), channel_id=1, source_target_pairs={{0,4},{1,17},{2,6},{3,19},{4,0},{5,21},{6,2},{7,23},{8,12},{9,25},... | collective-permute-start | bytes 344072 | tf_op jit(solution)/shard_map/ppermute | solution.py:426
  45.3 4.5 %collective-permute-done.7 = f32[224,128]{1,0:T(8,128)S(1)} collective-permute-done((f32[224,128]{1,0:T(8,128)S(1)}, f32[224,128]{1,0:T(8,128)S(1)}, u32[]{:S(2)}, u32[]{:S(2)}) %collective-permute-start.7) | collective-permute-done | bytes 114720 | tf_op jit(solution)/shard_map/ppermute | solution.py:426
  49.9 0.1 collective-permute-start.8
  49.9 1.5 %collective-permute-done.8.other_ref = f32[416,128]{1,0:T(8,128)S(1)} collective-permute-done((f32[416,128]{1,0:T(8,128)S(1)}, f32[416,128]{1,0:T(8,128)S(1)}, u32[]{:S(2)}, u32[]{:S(2)}) %collective-permute-start.8) | collective-permute-done | bytes 213024 | tf_op jit(solution)/shard_map/ppermute | solution.py:413
  51.4 1.0 %finish.1 = (f32[14,1,192]{2,1,0:T(1,128)}, f32[288,128]{1,0:T(8,128)}, f32[1,128]{1,0:T(1,128)}, f32[128,128]{1,0:T(8,128)}, f32[1,128]{1,0:T(1,128)}, /*index=...) custom-call(f32[416,128]{1,0:T(8,128)S(1)} %slice_dynamic-update-slice_fusion.mine_ref, ...), custom_call_target="tpu_custom_call" | custom-call | tf_op jit(solution)/shard_map/finish/pallas_call | solution.py:564
  (30 shorter events, 0.2 us)
Async XLA Ops:
  0.6 12.7 %copy-start.9 = (f32[14]{0:T(128)S(1)}, f32[14]{0:T(128)}, u32[]{:S(2)}) copy-start(f32[14]{0:T(128)} %param.21) | copy-start | bytes 172
  0.6 12.7 %copy-start.6 = (bf16[128,14]{0,1:T(8,128)(2,1)S(1)}, bf16[128,14]{0,1:T(8,128)(2,1)}, u32[]{:S(2)}) copy-start(bf16[128,14]{0,1:T(8,128)(2,1)} %param.20) | copy-start | bytes 10756
  0.7 12.7 %copy-start.8 = (f32[128]{0:T(128)S(1)}, f32[128]{0:T(128)}, u32[]{:S(2)}) copy-start(f32[128]{0:T(128)} %param.19) | copy-start | bytes 1540
  0.7 12.7 %copy-start.5 = (bf16[128,128]{1,0:T(8,128)(2,1)S(1)}, bf16[128,128]{1,0:T(8,128)(2,1)}, u32[]{:S(2)}) copy-start(bf16[128,128]{1,0:T(8,128)(2,1)} %w2_ref.1) | copy-start | bytes 98308
  0.7 12.7 %copy-start.7 = (f32[128]{0:T(128)S(1)}, f32[128]{0:T(128)}, u32[]{:S(2)}) copy-start(f32[128]{0:T(128)} %param.17) | copy-start | bytes 1540
  0.7 12.7 %copy-start.2 = (bf16[3,3,32,128]{3,2,1,0:T(8,128)(2,1)S(1)}, bf16[3,3,32,128]{3,2,1,0:T(8,128)(2,1)}, u32[]{:S(2)}) copy-start(bf16[3,3,32,128]{3,2,1,0:T(8,128)(2,1)} %param.16) | copy-start | bytes 221188
  0.7 12.7 %copy-start.3 = (f32[96,128]{1,0:T(8,128)S(1)}, f32[96,128]{1,0:T(8,128)}, u32[]{:S(2)}) copy-start(f32[96,128]{1,0:T(8,128)} %frac_ref.1) | copy-start | bytes 147460
  0.7 12.7 %copy-start.4 = (s32[96,128]{1,0:T(8,128)S(1)}, s32[96,128]{1,0:T(8,128)}, u32[]{:S(2)}) copy-start(s32[96,128]{1,0:T(8,128)} %mask_ref.1) | copy-start | bytes 147460
  2.5 4.4 %collective-permute-start = (f32[56,128]{1,0:T(8,128)}, f32[56,128]{1,0:T(8,128)S(1)}, u32[]{:S(2)}, u32[]{:S(2)}) collective-permute-start(f32[56,128]{1,0:T(8,128)} %get-tuple-element.31.refs_0_), channel_id=1, source_target_pairs={{0,3},{1,2},{2,1},{3,0},{4,7},{5,6},{6,5},{7,4},{8,11},{9,10},{10,... | collective-permute-start | bytes 86024 | tf_op jit(solution)/shard_map/ppermute | solution.py:413
  6.8 7.4 %copy-start = (f32[56,128]{1,0:T(8,128)S(1)}, f32[56,128]{1,0:T(8,128)}, u32[]{:S(2)}) copy-start(f32[56,128]{1,0:T(8,128)} %get-tuple-element.31.refs_0_) | copy-start | bytes 86020
  6.8 7.4 %copy-start.1 = (s32[1536]{0:T(1024)S(1)}, s32[1536]{0:T(1024)}, u32[]{:S(2)}) copy-start(s32[1536]{0:T(1024)} %param.14) | copy-start | bytes 18436
  6.9 6.1 %collective-permute-start.1 = (f32[80,128]{1,0:T(8,128)S(1)}, f32[80,128]{1,0:T(8,128)S(1)}, u32[]{:S(2)}, u32[]{:S(2)}) collective-permute-start(f32[80,128]{1,0:T(8,128)S(1)} %pad_maximum_fusion.3), channel_id=1, source_target_pairs={{0,7},{1,6},{2,5},{3,4},{4,3},{5,2},{6,1},{7,0},{8,15},{9,14},{10,... | collective-permute-start | bytes 122888 | tf_op jit(solution)/shard_map/ppermute | solution.py:413
  12.9 1.3 %collective-permute-start.2 = (f32[128,128]{1,0:T(8,128)S(1)}, f32[128,128]{1,0:T(8,128)S(1)}, u32[]{:S(2)}, u32[]{:S(2)}) collective-permute-start(f32[128,128]{1,0:T(8,128)S(1)} %pad_maximum_fusion.2), channel_id=1, source_target_pairs={{0,1},{1,0},{2,3},{3,2},{4,5},{5,4},{6,7},{7,6},{8,9},{9,8},{10,11... | collective-permute-start | bytes 196616 | tf_op jit(solution)/shard_map/ppermute | solution.py:413
  25.9 1.4 %collective-permute-start.3 = (f32[248,128]{1,0:T(8,128)S(1)}, f32[248,128]{1,0:T(8,128)S(1)}, u32[]{:S(2)}, u32[]{:S(2)}) collective-permute-start(f32[248,128]{1,0:T(8,128)S(1)} %get-tuple-element.44), channel_id=1, source_target_pairs={{0,1},{1,0},{2,3},{3,2},{4,5},{5,4},{6,7},{7,6},{8,9},{9,8},{10,11... | collective-permute-start | bytes 380936 | tf_op jit(solution)/shard_map/ppermute | solution.py:413
  27.4 5.1 %collective-permute-start.4 = (f32[272,128]{1,0:T(8,128)S(1)}, f32[272,128]{1,0:T(8,128)S(1)}, u32[]{:S(2)}, u32[]{:S(2)}) collective-permute-start(f32[272,128]{1,0:T(8,128)S(1)} %pad_maximum_fusion.1), channel_id=1, source_target_pairs={{0,8},{1,3},{2,10},{3,1},{4,12},{5,7},{6,14},{7,5},{8,0},{9,11},{1... | collective-permute-start | bytes 417800 | tf_op jit(solution)/shard_map/ppermute | solution.py:426
  32.5 5.4 %collective-permute-start.5 = (f32[320,128]{1,0:T(8,128)S(1)}, f32[320,128]{1,0:T(8,128)S(1)}, u32[]{:S(2)}, u32[]{:S(2)}) collective-permute-start(f32[320,128]{1,0:T(8,128)S(1)} %pad_maximum_fusion), channel_id=1, source_target_pairs={{0,16},{1,5},{2,18},{3,7},{4,20},{5,1},{6,22},{7,3},{8,24},{9,13},... | collective-permute-start | bytes 491528 | tf_op jit(solution)/shard_map/ppermute | solution.py:426
  37.9 4.9 %collective-permute-start.6 = (f32[224,128]{1,0:T(8,128)S(1)}, f32[224,128]{1,0:T(8,128)S(1)}, u32[]{:S(2)}, u32[]{:S(2)}) collective-permute-start(f32[224,128]{1,0:T(8,128)S(1)} %slice_add_fusion), channel_id=1, source_target_pairs={{0,2},{1,9},{2,0},{3,11},{4,6},{5,13},{6,4},{7,15},{8,10},{9,1},{1... | collective-permute-start | bytes 344072 | tf_op jit(solution)/shard_map/ppermute | solution.py:426
  42.8 7.0 %collective-permute-start.7 = (f32[224,128]{1,0:T(8,128)S(1)}, f32[224,128]{1,0:T(8,128)S(1)}, u32[]{:S(2)}, u32[]{:S(2)}) collective-permute-start(f32[224,128]{1,0:T(8,128)S(1)} %add.18), channel_id=1, source_target_pairs={{0,4},{1,17},{2,6},{3,19},{4,0},{5,21},{6,2},{7,23},{8,12},{9,25},... | collective-permute-start | bytes 344072 | tf_op jit(solution)/shard_map/ppermute | solution.py:426
  49.9 1.5 %collective-permute-start.8 = (f32[416,128]{1,0:T(8,128)S(1)}, f32[416,128]{1,0:T(8,128)S(1)}, u32[]{:S(2)}, u32[]{:S(2)}) collective-permute-start(f32[416,128]{1,0:T(8,128)S(1)} %slice_dynamic-update-slice_fusion.mine_ref), channel_id=1, source_target_pairs={{0,1},{1,0},{2,3},{3,2},{4,5},{5,4},{6,7},{7,6},{8,9},{9,8},{10,11... | collective-permute-start | bytes 638984 | tf_op jit(solution)/shard_map/ppermute | solution.py:413

commit v6 on v5

--- a/solution.py
+++ b/solution.py
@@ -14,6 +14,7 @@
 PART = 256
 VMEM = 46 * 1024 * 1024
 PREPARE_VMEM = 8 * 1024 * 1024
+ALL_VMEM = 127 * 512 * 1024
 
 CUBIC = 0.044715
 ROOT_TWO_PI = math.sqrt(2.0 / math.pi)
@@ -21,11 +22,12 @@
 F32, BF16 = jnp.float32, jnp.bfloat16
 
 
-def gelu_pair(pre):
-    square = pre * pre
-    half = 0.5 + 0.5 * jnp.tanh(pre * (ROOT_TWO_PI + (ROOT_TWO_PI * CUBIC) * square))
-    value = pre * half
-    slope = half + value * (1.0 - half) * (2.0 * ROOT_TWO_PI + (6.0 * ROOT_TWO_PI * CUBIC) * square)
+def gelu_pair(half):
+    square = half * half
+    tanh_value = jnp.tanh(half * (2.0 * ROOT_TWO_PI + (8.0 * ROOT_TWO_PI * CUBIC) * square))
+    above = 1.0 + tanh_value
+    value = half * above
+    slope = above + value * (1.0 - tanh_value) * (2.0 * ROOT_TWO_PI + (24.0 * ROOT_TWO_PI * CUBIC) * square)
     return value, slope
 
 
@@ -85,22 +87,30 @@
     return jnp.concatenate([left, row, right], axis=0).astype(BF16)
 
 
-def pack_kernel(masks, top_ref, bottom_ref, target_ref, sent_ref, rows_ref):
-    position = lax.axis_index("space")
+def pack_kernel(
+    fields_ref, target_ref, sent_ref, outer_ref, inner_ref, top_rows, bottom_rows, targets, done
+):
+    rows, some = fields_ref.shape[2], top_rows.shape[1]
+    copies = [
+        pltpu.make_async_copy(fields_ref.at[0, :, pl.ds(0, some), :], top_rows, done.at[0]),
+        pltpu.make_async_copy(fields_ref.at[0, :, pl.ds(rows - some, some), :], bottom_rows, done.at[1]),
+        pltpu.make_async_copy(target_ref, targets, done.at[2]),
+    ]
+    for copy in copies:
+        copy.start()
+    for copy in copies:
+        copy.wait()
+    core = lax.rem(lax.axis_index("space"), 2)
     pools, _, blocks = target_ref.shape
-    channels = top_ref.shape[1]
-    edge = bottom_ref.shape[2] - 1
-    top = top_ref[0].astype(F32)[:, 0, :]
-    bottom = bottom_ref[0].astype(F32)[:, edge, :]
+    top = top_rows[...].astype(F32)[:, 0, :]
+    bottom = bottom_rows[...].astype(F32)[:, some - 1, :]
     values = jnp.concatenate(
-        [target_ref[:, 0, :], jnp.zeros((POOL_ROWS - pools, blocks), F32)], axis=0
+        [targets[:, 0, :], jnp.zeros((POOL_ROWS - pools, blocks), F32)], axis=0
     )
     sent_ref[:PACK_ROWS, :] = pack(values)
-    for at, mask in enumerate(masks):
-        row = jnp.where(position ^ mask > position, bottom, top)
-        rows_ref[at] = row
-        if at == 0:
-            sent_ref[PACK_ROWS:, :] = row
+    sent_ref[PACK_ROWS:, :] = jnp.where(core == 0, top, bottom)
+    outer_ref[...] = jnp.where(core == 0, top, bottom)
+    inner_ref[...] = jnp.where(core == 0, bottom, top)
 
 
 def prepare_kernel(
@@ -113,8 +123,10 @@
     b2_ref,
     w3t_ref,
     b3_ref,
+    owner_ref,
     shifted,
     weight,
+    owners,
     w1t,
     w2t,
     w2d,
@@ -142,18 +154,18 @@
     def doubled(values):
         return jnp.concatenate([values, values], axis=1)
 
-    first_weights, none = w1_ref[...].astype(F32), jnp.zeros((taps, width), F32)
-    bias = terms(b1_ref[...])
+    first_weights, none = 0.5 * w1_ref[...].astype(F32), jnp.zeros((taps, width), F32)
+    bias = terms(0.5 * b1_ref[...])
     w1t[:width, :] = jnp.concatenate([first_weights, none, bias], axis=0).T.astype(BF16)
     w1t[width:, :] = jnp.concatenate([none, first_weights, bias], axis=0).T.astype(BF16)
-    second_weights = twice(w2_ref[...].astype(F32))
+    second_weights = twice(0.5 * w2_ref[...].astype(F32))
     w2d[...] = second_weights.astype(BF16)
-    w2t[...] = jnp.concatenate([second_weights, doubled(terms(b2_ref[...]))], axis=0).T.astype(BF16)
+    w2t[...] = jnp.concatenate([second_weights, doubled(terms(0.5 * b2_ref[...]))], axis=0).T.astype(BF16)
     last_weights = jnp.concatenate(
         [w3t_ref[...].astype(F32), jnp.zeros((POOL_ROWS - pools, width), F32)], axis=0
     )
     w3t[...] = twice(last_weights).astype(BF16)
-    four = twice(twice(last_weights))
+    four = twice(twice(0.5 * last_weights))
     w3p[...] = jnp.concatenate([four, jnp.zeros((128 - 4 * POOL_ROWS, 4 * width), F32)], axis=0).T[
         :, : 4 * POOL_ROWS
     ].astype(BF16)
@@ -161,6 +173,7 @@
     bias = jnp.broadcast_to(bias, (width, width)).T[:POOL_ROWS]
     b3c[...] = jnp.concatenate([bias, bias], axis=0)
     weight[...] = frac_ref[...] * mask_ref[...].astype(F32)
+    owners[...] = owner_ref[...]
 
     for row in range(rows):
         shifted[row * taps : (row + 1) * taps, :] = three_taps(fields_ref[row].astype(F32))
@@ -174,7 +187,7 @@
 
 ):
     sent_ref, *got_refs = refs[: len(masks) + 1]
-    owner_ref, shifted, weight, w1t, w2t, w2d, w3t, w3p, b3c = refs[len(masks) + 1 : len(masks) + 10]
+    shifted, weight, owner_ref, w1t, w2t, w2d, w3t, w3p, b3c = refs[len(masks) + 1 : len(masks) + 10]
     keep_ref, send_ref, coarse_ref = refs[len(masks) + 10 : len(masks) + 13]
     lower, upper, pre_one, pre_two, hidden_one, slope_one, hidden_two, slope_two = refs[
         len(masks) + 13 : len(masks) + 21
@@ -192,11 +205,11 @@
     position = lax.axis_index("space")
     core = lax.rem(position, 2)
 
-    low = high = jnp.zeros((channels, cols), F32)
-    for got_ref, mask in zip(got_refs, masks):
-        row = got_ref[got_ref.shape[0] - channels :, :]
-        low = jnp.where(position ^ mask == position - 1, row, low)
-        high = jnp.where(position ^ mask == position + 1, row, high)
+    outer, inner = [ref[ref.shape[0] - channels :, :] for ref in got_refs[-2:]]
+    peers = owner_ref.shape[0] * 128 // blocks
+    outer = jnp.where((position == 0) | (position == peers - 1), 0.0, outer)
+    low = jnp.where(core == 0, outer, inner)
+    high = jnp.where(core == 0, inner, outer)
     lower[:taps, :] = three_taps(low)
     lower[taps:, :] = shifted[:conv_rows, :]
     upper[:conv_rows, :] = shifted[rows * taps - conv_rows :, :]
@@ -467,29 +480,38 @@
     count_all = lax.axis_size("dp") * pools * owner_map.shape[0]
     owners = owner_map.reshape(-1, 128)
     position = lax.axis_index("space")
-    masks = [2 * bit - 1 for bit in bits_of(peers, 2)] + [1]
-    sent, edges = pl.pallas_call(
-        functools.partial(pack_kernel, masks),
+    masks = bits_of(peers, 4)[::-1] + [3, 1]
+    apart = jnp.where(position % 2 == 0, position ^ (position - 1), position ^ (position + 1))
+    sent, outer, inner = pl.pallas_call(
+        pack_kernel,
         out_shape=[
-            jax.ShapeDtypeStruct((PACK_ROWS + channels, cols), F32),
-            jax.ShapeDtypeStruct((len(masks), channels, cols), F32),
+            pltpu.VMEM((PACK_ROWS + channels, cols), F32),
+            pltpu.VMEM((channels, cols), F32),
+            pltpu.VMEM((channels, cols), F32),
         ],
-        grid=(1,),
-        in_specs=[
-            pl.BlockSpec((1, channels, 16, cols), lambda i: (0, 0, 0, 0)),
-            pl.BlockSpec((1, channels, 16, cols), lambda i: (0, 0, rows // 16 - 1, 0)),
-            pl.BlockSpec((pools, 1, blocks), lambda i: (0, 0, 0)),
+        in_specs=[pl.BlockSpec(memory_space=pltpu.HBM)] * 2,
+        out_specs=[pl.BlockSpec(memory_space=pltpu.VMEM)] * 3,
+        compiler_params=pltpu.CompilerParams(vmem_limit_bytes=ALL_VMEM),
+        scratch_shapes=[
+            pltpu.VMEM((channels, 16, cols), BF16),
+            pltpu.VMEM((channels, 16, cols), BF16),
+            pltpu.VMEM((pools, 1, blocks), F32),
+            pltpu.SemaphoreType.DMA((3,)),
         ],
         name="pack_edges",
-    )(fields, fields, jnp.swapaxes(targets, 0, 1))
+    )(fields, jnp.swapaxes(targets, 0, 1))
     payload, gots = sent, []
     for at, mask in enumerate(masks):
-        if at > 0:
-            payload = jnp.concatenate([held, edges[at]], axis=0)
+        if mask == 1:
+            payload = jnp.concatenate([held, inner], axis=0)
+        elif at > 0:
+            mine = apart == (mask if mask == 3 else 2 * mask - 1)
+            payload = jnp.concatenate([held, jnp.where(mine, outer, passing)], axis=0)
         got = swapped(payload, "space", mask)
         gots.append(got)
         had = payload.shape[0] - channels
         held = jnp.concatenate([payload[:had], got[:had]], axis=0)
+        passing = got[had:]
     later, _ = lax.optimization_barrier((fields, sent))
     by_row = jnp.swapaxes(later[0], 0, 1)
     by_row, _ = lax.optimization_barrier((by_row, gots[0]))
@@ -504,6 +526,7 @@
         out_shape=[
             pltpu.VMEM((rows * 3 * channels, cols), bf16),
             pltpu.VMEM((rows, cols), f32),
+            pltpu.VMEM(owners.shape, jnp.int32),
             pltpu.VMEM((2 * width, conv_rows + 3 * channels + POOL_ROWS), bf16),
             pltpu.VMEM((2 * width, 2 * width + POOL_ROWS), bf16),
             pltpu.VMEM((2 * width, 2 * width), bf16),
@@ -511,8 +534,8 @@
             pltpu.VMEM((4 * width, 4 * POOL_ROWS), bf16),
             pltpu.VMEM((2 * POOL_ROWS, cols), f32),
         ],
-        in_specs=[pl.BlockSpec(memory_space=pltpu.VMEM)] * 9,
-        out_specs=[pl.BlockSpec(memory_space=pltpu.VMEM)] * 8,
+        in_specs=[pl.BlockSpec(memory_space=pltpu.VMEM)] * 10,
+        out_specs=[pl.BlockSpec(memory_space=pltpu.VMEM)] * 9,
         compiler_params=pltpu.CompilerParams(vmem_limit_bytes=PREPARE_VMEM),
         cost_estimate=pl.CostEstimate(flops=10**9, bytes_accessed=4 * 10**6, transcendentals=0),
         name="prepare",
@@ -526,7 +549,9 @@
         mix_bias.reshape(1, width),
         out_weight.T,
         out_bias.reshape(1, pools),
+        owners,
     )
+    owners = prepared[2]
     keep, send, coarse = pl.pallas_call(
         functools.partial(step_kernel, count_all, masks, pools),
         out_shape=[
@@ -557,7 +582,6 @@
     )(
         sent,
         *gots,
-        owners,
         *prepared,
     )
     mine, other = reduce_all(keep, send, coarse)

time: 52.9 us -> 51.2 us (0.968)
  local copies, waits for them, and re-layouts: 2.96 us -> 1.51 us
  waiting for transfers between devices: 19.3 us -> 20.2 us
  Pallas kernels: 15.1 us -> 14.3 us
    ppermute x5, waiting for transfers between devices: 3.45 us -> 6.35 us  [swapped(): lax.ppermute(values, axis, [(i, i ^ bit) for i in range(lax.axis_size(axi...]
    ppermute x5, starting transfers between devices: 7.61 us -> 5.19 us  [swapped(): lax.ppermute(values, axis, [(i, i ^ bit) for i in range(lax.axis_size(axi...]
    ppermute x4, starting transfers between devices: 6.55 us -> 8.86 us  [crossed(): return lax.ppermute(values, ('dp', 'space'), pairs)]
    ppermute x4, waiting for transfers between devices: 15.8 us -> 13.9 us  [crossed(): return lax.ppermute(values, ('dp', 'space'), pairs)]
    squeeze x1 -> x0, local copies, waits for them, and re-layouts: 0.74 us -> none  [on_device(): payload = jnp.concatenate([held, edges[at]], axis=0)]
    slice x3, local copies, waits for them, and re-layouts: 0.71 us -> 0.01 us  [on_device(): held = jnp.concatenate([payload[:had], got[:had]], axis=0)]
    pallas_call x1, Pallas kernels: 1.75 us -> 1.17 us  [on_device(): pl.pallas_call(pack_kernel, out_shape=[pltpu.VMEM((PACK_ROWS + channels,...]
  transfers between devices with their start and end apart: 9 -> 9, of which waited for: 9 -> 9; matrix products, arithmetic and copies ran while one was open for 6% -> 3% of each run, Pallas kernels for 1% -> 1%
where the time goes in v6:
time: 51.2 us; the launch traced here: 51 us
  waiting for transfers between devices  20.2 us (39%)
  Pallas kernels  14.3 us (28%)
  starting transfers between devices  14 us (27%)
  local copies, waits for them, and re-layouts  1.51 us (3%)
  between operations  0.86 us (2%)
    ppermute x4, waiting for transfers between devices, crossed(): return lax.ppermute(values, ('dp', 'space'), pairs)  13.9 us
    pallas_call x1, Pallas kernels, on_device(): pl.pallas_call(functools.partial(step_kernel, count_all, masks, pools), o...  11.4 us
    ppermute x4, starting transfers between devices, crossed(): return lax.ppermute(values, ('dp', 'space'), pairs)  8.86 us
    ppermute x5, waiting for transfers between devices, swapped(): lax.ppermute(values, axis, [(i, i ^ bit) for i in range(lax.axis_size(axi...  6.35 us
    ppermute x5, starting transfers between devices, swapped(): lax.ppermute(values, axis, [(i, i ^ bit) for i in range(lax.axis_size(axi...  5.19 us
    optimization_barrier x1, local copies, waits for them, and re-layouts, on_device(): later, _ = lax.optimization_barrier((fields, sent))  1.44 us
    pallas_call x1, Pallas kernels, on_device(): pl.pallas_call(pack_kernel, out_shape=[pltpu.VMEM((PACK_ROWS + channels,...  1.17 us
    pallas_call x1, Pallas kernels, on_device(): pl.pallas_call(functools.partial(finish_kernel, count_all), out_shape=[ja...  1.04 us
  transfers between devices with their start and end apart: 9, of which 9 were waited for; matrix products, arithmetic and copies ran while one was open for 3% of the time, Pallas kernels for 1%

profile of v6, /device:TPU:0, one launch (start us, length us, event | category | flops | bytes accessed | tf_op | source)
XLA Modules:
  0.0 51.0 jit_solution(408521078440286604)
XLA Ops:
  0.6 0.0 copy-start.8
  0.6 0.0 copy-start.5
  0.7 0.0 copy-start.7
  0.7 0.0 copy-start.3
  0.7 0.0 copy-start.6
  0.7 0.0 copy-start
  0.7 0.0 copy-start.4
  0.7 0.0 copy-start.1
  0.7 0.0 copy-start.2
  0.7 1.2 %pack_edges.1 = (f32[56,128]{1,0:T(8,128)S(1)}, f32[32,128]{1,0:T(8,128)S(1)}, f32[32,128]{1,0:T(8,128)S(1)}) custom-call(bf16[1,32,96,128]{3,2,1,0:T(8,128)(2,1)} %fields_ref.1, f32[14,1,192]{2,1,0:T(1,128)} %bitcast.26), custom_call_target="tpu_custom_call" | custom-call | tf_op jit(solution)/shard_map/pack_edges/pallas_call | solution.py:485
  1.9 4.1 %collective-permute-start = (f32[56,128]{1,0:T(8,128)S(1)}, f32[56,128]{1,0:T(8,128)S(1)}, u32[]{:S(2)}, u32[]{:S(2)}) collective-permute-start(f32[56,128]{1,0:T(8,128)S(1)} %get-tuple-element.33.refs_0_), channel_id=1, source_target_pairs={{0,4},{1,5},{2,6},{3,7},{4,0},{5,1},{6,2},{7,3},{8,12},{9,13},{10,... | collective-permute-start | bytes 86024 | tf_op jit(solution)/shard_map/ppermute | solution.py:426
  6.0 1.9 %collective-permute-done.refs_1_ = f32[56,128]{1,0:T(8,128)S(1)} collective-permute-done((f32[56,128]{1,0:T(8,128)S(1)}, f32[56,128]{1,0:T(8,128)S(1)}, u32[]{:S(2)}, u32[]{:S(2)}) %collective-permute-start) | collective-permute-done | bytes 28704 | tf_op jit(solution)/shard_map/ppermute | solution.py:426
  7.9 0.4 collective-permute-start.1
  8.2 1.4 %copy.21 = bf16[1,32,96,128]{3,1,2,0:T(8,128)(2,1)S(1)} copy(bf16[1,32,96,128]{3,2,1,0:T(8,128)(2,1)} %fields_ref.1) | data formatting | bytes 1572864 | tf_op jit(solution)/shard_map/optimization_barrier | solution.py:515
  9.7 1.7 %collective-permute-done.1.refs_2_ = f32[80,128]{1,0:T(8,128)S(1)} collective-permute-done((f32[80,128]{1,0:T(8,128)S(1)}, f32[80,128]{1,0:T(8,128)S(1)}, u32[]{:S(2)}, u32[]{:S(2)}) %collective-permute-start.1) | collective-permute-done | bytes 40992 | tf_op jit(solution)/shard_map/ppermute | solution.py:426
  11.4 0.3 collective-permute-start.2
  11.8 0.7 %prepare.1 = (bf16[9216,128]{1,0:T(8,128)(2,1)S(1)}, f32[96,128]{1,0:T(8,128)S(1)}, s32[12,128]{1,0:T(8,128)S(1)}, bf16[256,400]{1,0:T(8,128)(2,1)S(1)}, bf16[25...) custom-call(bf16[96,32,128]{2,1,0:T(8,128)(2,1)S(1)} %bitcast.19, ...), custom_call_target="tpu_custom_call" | custom-call | flops 1000000000 | bytes 4000000 | tf_op jit(solution)/shard_map/prepare/pallas_call | solution.py:524
  12.5 0.3 collective-permute-done.2.refs_3_
  12.7 11.4 %train_step.1 = (f32[224,128]{1,0:T(8,128)S(1)}, f32[248,128]{1,0:T(8,128)S(1)}, f32[24,128]{1,0:T(8,128)S(1)}) custom-call(f32[56,128]{1,0:T(8,128)S(1)} %get-tuple-element.33.refs_0_, f32[56,128]{1,0:T(8,128)S(1)} %collective-permute-done.refs_1_, f32[80,128]{1,0:T(8,128)S(1)} %collective-permute-done.1.refs_2_, ...), custom_call_target="tpu_custom_call" | custom-call | tf_op jit(solution)/shard_map/train_step/pallas_call | solution.py:555
  24.1 0.3 collective-permute-start.3
  24.4 1.1 %collective-permute-done.3 = f32[248,128]{1,0:T(8,128)S(1)} collective-permute-done((f32[248,128]{1,0:T(8,128)S(1)}, f32[248,128]{1,0:T(8,128)S(1)}, u32[]{:S(2)}, u32[]{:S(2)}) %collective-permute-start.3) | collective-permute-done | bytes 127008 | tf_op jit(solution)/shard_map/ppermute | solution.py:426
  25.6 2.4 %collective-permute-start.4 = (f32[272,128]{1,0:T(8,128)S(1)}, f32[272,128]{1,0:T(8,128)S(1)}, u32[]{:S(2)}, u32[]{:S(2)}) collective-permute-start(f32[272,128]{1,0:T(8,128)S(1)} %pad_maximum_fusion.1), channel_id=1, source_target_pairs={{0,8},{1,3},{2,10},{3,1},{4,12},{5,7},{6,14},{7,5},{8,0},{9,11},{1... | collective-permute-start | bytes 417800 | tf_op jit(solution)/shard_map/ppermute | solution.py:439
  28.0 3.0 %collective-permute-done.4 = f32[272,128]{1,0:T(8,128)S(1)} collective-permute-done((f32[272,128]{1,0:T(8,128)S(1)}, f32[272,128]{1,0:T(8,128)S(1)}, u32[]{:S(2)}, u32[]{:S(2)}) %collective-permute-start.4) | collective-permute-done | bytes 139296 | tf_op jit(solution)/shard_map/ppermute | solution.py:439
  31.1 2.1 %collective-permute-start.5 = (f32[320,128]{1,0:T(8,128)S(1)}, f32[320,128]{1,0:T(8,128)S(1)}, u32[]{:S(2)}, u32[]{:S(2)}) collective-permute-start(f32[320,128]{1,0:T(8,128)S(1)} %pad_maximum_fusion), channel_id=1, source_target_pairs={{0,16},{1,5},{2,18},{3,7},{4,20},{5,1},{6,22},{7,3},{8,24},{9,13},... | collective-permute-start | bytes 491528 | tf_op jit(solution)/shard_map/ppermute | solution.py:439
  33.2 3.3 %collective-permute-done.5 = f32[320,128]{1,0:T(8,128)S(1)} collective-permute-done((f32[320,128]{1,0:T(8,128)S(1)}, f32[320,128]{1,0:T(8,128)S(1)}, u32[]{:S(2)}, u32[]{:S(2)}) %collective-permute-start.5) | collective-permute-done | bytes 163872 | tf_op jit(solution)/shard_map/ppermute | solution.py:439
  36.5 1.6 %collective-permute-start.6 = (f32[224,128]{1,0:T(8,128)S(1)}, f32[224,128]{1,0:T(8,128)S(1)}, u32[]{:S(2)}, u32[]{:S(2)}) collective-permute-start(f32[224,128]{1,0:T(8,128)S(1)} %slice_add_fusion), channel_id=1, source_target_pairs={{0,2},{1,9},{2,0},{3,11},{4,6},{5,13},{6,4},{7,15},{8,10},{9,1},{1... | collective-permute-start | bytes 344072 | tf_op jit(solution)/shard_map/ppermute | solution.py:439
  38.1 3.3 %collective-permute-done.6 = f32[224,128]{1,0:T(8,128)S(1)} collective-permute-done((f32[224,128]{1,0:T(8,128)S(1)}, f32[224,128]{1,0:T(8,128)S(1)}, u32[]{:S(2)}, u32[]{:S(2)}) %collective-permute-start.6) | collective-permute-done | bytes 114720 | tf_op jit(solution)/shard_map/ppermute | solution.py:439
  41.4 2.7 %collective-permute-start.7 = (f32[224,128]{1,0:T(8,128)S(1)}, f32[224,128]{1,0:T(8,128)S(1)}, u32[]{:S(2)}, u32[]{:S(2)}) collective-permute-start(f32[224,128]{1,0:T(8,128)S(1)} %add.28), channel_id=1, source_target_pairs={{0,4},{1,17},{2,6},{3,19},{4,0},{5,21},{6,2},{7,23},{8,12},{9,25},... | collective-permute-start | bytes 344072 | tf_op jit(solution)/shard_map/ppermute | solution.py:439
  44.1 4.3 %collective-permute-done.7 = f32[224,128]{1,0:T(8,128)S(1)} collective-permute-done((f32[224,128]{1,0:T(8,128)S(1)}, f32[224,128]{1,0:T(8,128)S(1)}, u32[]{:S(2)}, u32[]{:S(2)}) %collective-permute-start.7) | collective-permute-done | bytes 114720 | tf_op jit(solution)/shard_map/ppermute | solution.py:439
  48.4 0.1 collective-permute-start.8
  48.5 1.5 %collective-permute-done.8.other_ref = f32[416,128]{1,0:T(8,128)S(1)} collective-permute-done((f32[416,128]{1,0:T(8,128)S(1)}, f32[416,128]{1,0:T(8,128)S(1)}, u32[]{:S(2)}, u32[]{:S(2)}) %collective-permute-start.8) | collective-permute-done | bytes 213024 | tf_op jit(solution)/shard_map/ppermute | solution.py:426
  50.0 1.0 %finish.1 = (f32[14,1,192]{2,1,0:T(1,128)}, f32[288,128]{1,0:T(8,128)}, f32[1,128]{1,0:T(1,128)}, f32[128,128]{1,0:T(8,128)}, f32[1,128]{1,0:T(1,128)}, /*index=...) custom-call(f32[416,128]{1,0:T(8,128)S(1)} %slice_dynamic-update-slice_fusion.mine_ref, ...), custom_call_target="tpu_custom_call" | custom-call | tf_op jit(solution)/shard_map/finish/pallas_call | solution.py:588
  (28 shorter events, 0.2 us)
Async XLA Ops:
  0.6 11.1 %copy-start.8 = (f32[14]{0:T(128)S(1)}, f32[14]{0:T(128)}, u32[]{:S(2)}) copy-start(f32[14]{0:T(128)} %param.21) | copy-start | bytes 172
  0.6 11.1 %copy-start.5 = (bf16[128,14]{0,1:T(8,128)(2,1)S(1)}, bf16[128,14]{0,1:T(8,128)(2,1)}, u32[]{:S(2)}) copy-start(bf16[128,14]{0,1:T(8,128)(2,1)} %param.20) | copy-start | bytes 10756
  0.7 11.1 %copy-start.7 = (f32[128]{0:T(128)S(1)}, f32[128]{0:T(128)}, u32[]{:S(2)}) copy-start(f32[128]{0:T(128)} %param.19) | copy-start | bytes 1540
  0.7 11.1 %copy-start.3 = (bf16[128,128]{1,0:T(8,128)(2,1)S(1)}, bf16[128,128]{1,0:T(8,128)(2,1)}, u32[]{:S(2)}) copy-start(bf16[128,128]{1,0:T(8,128)(2,1)} %w2_ref.1) | copy-start | bytes 98308
  0.7 11.1 %copy-start.6 = (f32[128]{0:T(128)S(1)}, f32[128]{0:T(128)}, u32[]{:S(2)}) copy-start(f32[128]{0:T(128)} %param.17) | copy-start | bytes 1540
  0.7 11.1 %copy-start = (bf16[3,3,32,128]{3,2,1,0:T(8,128)(2,1)S(1)}, bf16[3,3,32,128]{3,2,1,0:T(8,128)(2,1)}, u32[]{:S(2)}) copy-start(bf16[3,3,32,128]{3,2,1,0:T(8,128)(2,1)} %param.16) | copy-start | bytes 221188
  0.7 11.1 %copy-start.4 = (s32[1536]{0:T(1024)S(1)}, s32[1536]{0:T(1024)}, u32[]{:S(2)}) copy-start(s32[1536]{0:T(1024)} %param.14) | copy-start | bytes 18436
  0.7 11.1 %copy-start.1 = (f32[96,128]{1,0:T(8,128)S(1)}, f32[96,128]{1,0:T(8,128)}, u32[]{:S(2)}) copy-start(f32[96,128]{1,0:T(8,128)} %frac_ref.1) | copy-start | bytes 147460
  0.7 11.1 %copy-start.2 = (s32[96,128]{1,0:T(8,128)S(1)}, s32[96,128]{1,0:T(8,128)}, u32[]{:S(2)}) copy-start(s32[96,128]{1,0:T(8,128)} %mask_ref.1) | copy-start | bytes 147460
  1.9 6.0 %collective-permute-start = (f32[56,128]{1,0:T(8,128)S(1)}, f32[56,128]{1,0:T(8,128)S(1)}, u32[]{:S(2)}, u32[]{:S(2)}) collective-permute-start(f32[56,128]{1,0:T(8,128)S(1)} %get-tuple-element.33.refs_0_), channel_id=1, source_target_pairs={{0,4},{1,5},{2,6},{3,7},{4,0},{5,1},{6,2},{7,3},{8,12},{9,13},{10,... | collective-permute-start | bytes 86024 | tf_op jit(solution)/shard_map/ppermute | solution.py:426
  7.9 3.5 %collective-permute-start.1 = (f32[80,128]{1,0:T(8,128)S(1)}, f32[80,128]{1,0:T(8,128)S(1)}, u32[]{:S(2)}, u32[]{:S(2)}) collective-permute-start(f32[80,128]{1,0:T(8,128)S(1)} %pad_maximum_fusion.3), channel_id=1, source_target_pairs={{0,3},{1,2},{2,1},{3,0},{4,7},{5,6},{6,5},{7,4},{8,11},{9,10},{10,... | collective-permute-start | bytes 122888 | tf_op jit(solution)/shard_map/ppermute | solution.py:426
  11.4 1.3 %collective-permute-start.2 = (f32[128,128]{1,0:T(8,128)S(1)}, f32[128,128]{1,0:T(8,128)S(1)}, u32[]{:S(2)}, u32[]{:S(2)}) collective-permute-start(f32[128,128]{1,0:T(8,128)S(1)} %pad_maximum_fusion.2), channel_id=1, source_target_pairs={{0,1},{1,0},{2,3},{3,2},{4,5},{5,4},{6,7},{7,6},{8,9},{9,8},{10,11... | collective-permute-start | bytes 196616 | tf_op jit(solution)/shard_map/ppermute | solution.py:426
  24.1 1.4 %collective-permute-start.3 = (f32[248,128]{1,0:T(8,128)S(1)}, f32[248,128]{1,0:T(8,128)S(1)}, u32[]{:S(2)}, u32[]{:S(2)}) collective-permute-start(f32[248,128]{1,0:T(8,128)S(1)} %get-tuple-element.48), channel_id=1, source_target_pairs={{0,1},{1,0},{2,3},{3,2},{4,5},{5,4},{6,7},{7,6},{8,9},{9,8},{10,11... | collective-permute-start | bytes 380936 | tf_op jit(solution)/shard_map/ppermute | solution.py:426
  25.6 5.5 %collective-permute-start.4 = (f32[272,128]{1,0:T(8,128)S(1)}, f32[272,128]{1,0:T(8,128)S(1)}, u32[]{:S(2)}, u32[]{:S(2)}) collective-permute-start(f32[272,128]{1,0:T(8,128)S(1)} %pad_maximum_fusion.1), channel_id=1, source_target_pairs={{0,8},{1,3},{2,10},{3,1},{4,12},{5,7},{6,14},{7,5},{8,0},{9,11},{1... | collective-permute-start | bytes 417800 | tf_op jit(solution)/shard_map/ppermute | solution.py:439
  31.1 5.4 %collective-permute-start.5 = (f32[320,128]{1,0:T(8,128)S(1)}, f32[320,128]{1,0:T(8,128)S(1)}, u32[]{:S(2)}, u32[]{:S(2)}) collective-permute-start(f32[320,128]{1,0:T(8,128)S(1)} %pad_maximum_fusion), channel_id=1, source_target_pairs={{0,16},{1,5},{2,18},{3,7},{4,20},{5,1},{6,22},{7,3},{8,24},{9,13},... | collective-permute-start | bytes 491528 | tf_op jit(solution)/shard_map/ppermute | solution.py:439
  36.5 4.9 %collective-permute-start.6 = (f32[224,128]{1,0:T(8,128)S(1)}, f32[224,128]{1,0:T(8,128)S(1)}, u32[]{:S(2)}, u32[]{:S(2)}) collective-permute-start(f32[224,128]{1,0:T(8,128)S(1)} %slice_add_fusion), channel_id=1, source_target_pairs={{0,2},{1,9},{2,0},{3,11},{4,6},{5,13},{6,4},{7,15},{8,10},{9,1},{1... | collective-permute-start | bytes 344072 | tf_op jit(solution)/shard_map/ppermute | solution.py:439
  41.4 7.0 %collective-permute-start.7 = (f32[224,128]{1,0:T(8,128)S(1)}, f32[224,128]{1,0:T(8,128)S(1)}, u32[]{:S(2)}, u32[]{:S(2)}) collective-permute-start(f32[224,128]{1,0:T(8,128)S(1)} %add.28), channel_id=1, source_target_pairs={{0,4},{1,17},{2,6},{3,19},{4,0},{5,21},{6,2},{7,23},{8,12},{9,25},... | collective-permute-start | bytes 344072 | tf_op jit(solution)/shard_map/ppermute | solution.py:439
  48.4 1.5 %collective-permute-start.8 = (f32[416,128]{1,0:T(8,128)S(1)}, f32[416,128]{1,0:T(8,128)S(1)}, u32[]{:S(2)}, u32[]{:S(2)}) collective-permute-start(f32[416,128]{1,0:T(8,128)S(1)} %slice_dynamic-update-slice_fusion.mine_ref), channel_id=1, source_target_pairs={{0,1},{1,0},{2,3},{3,2},{4,5},{5,4},{6,7},{7,6},{8,9},{9,8},{10,11... | collective-permute-start | bytes 638984 | tf_op jit(solution)/shard_map/ppermute | solution.py:426

commit v7 on v6

--- a/solution.py
+++ b/solution.py
@@ -11,6 +11,7 @@
 SIDE = 8
 POOL_ROWS = 16
 PACK_ROWS = 24
+MOST_PICKS = 8
 PART = 256
 VMEM = 46 * 1024 * 1024
 PREPARE_VMEM = 8 * 1024 * 1024
@@ -113,7 +114,13 @@
     inner_ref[...] = jnp.where(core == 0, bottom, top)
 
 
+def picks_of(mine, owner):
+    blocks = mine.shape[1]
+    return ones_where(iota((blocks, blocks), 0) == mine - owner * blocks)
+
+
 def prepare_kernel(
+    held,
     fields_ref,
     frac_ref,
     mask_ref,
@@ -133,6 +140,9 @@
     w3t,
     w3p,
     b3c,
+    picks,
+    spread,
+    leads,
 ):
     rows, channels, cols = fields_ref.shape
     width = w2_ref.shape[0]
@@ -175,6 +185,19 @@
     weight[...] = frac_ref[...] * mask_ref[...].astype(F32)
     owners[...] = owner_ref[...]
 
+    position = lax.axis_index("space")
+    blocks = picks.shape[1]
+    mine = owners_of(owner_ref, position, blocks)
+    for at, mask in enumerate(held[: picks.shape[0] // blocks]):
+        picks[at * blocks : (at + 1) * blocks, :] = picks_of(mine, position ^ mask)
+    tiles, across = rows // SIDE, cols // SIDE
+    in_tile = iota((blocks, cols), 0) - iota((blocks, cols), 1) // SIDE
+    first = iota((cols, blocks), 0)
+    in_block = jnp.where(first % SIDE == 0, iota((cols, blocks), 1) - first // SIDE, -1)
+    for tile in range(tiles):
+        spread[:, tile * cols : (tile + 1) * cols] = ones_where(in_tile == tile * across)
+        leads[tile * cols : (tile + 1) * cols, :] = ones_where(in_block == tile * across)
+
     for row in range(rows):
         shifted[row * taps : (row + 1) * taps, :] = three_taps(fields_ref[row].astype(F32))
 
@@ -187,12 +210,14 @@
 
 ):
     sent_ref, *got_refs = refs[: len(masks) + 1]
-    shifted, weight, owner_ref, w1t, w2t, w2d, w3t, w3p, b3c = refs[len(masks) + 1 : len(masks) + 10]
-    keep_ref, send_ref, coarse_ref = refs[len(masks) + 10 : len(masks) + 13]
+    shifted, weight, owner_ref, w1t, w2t, w2d, w3t, w3p, b3c, picks, spread, leads = refs[
+        len(masks) + 1 : len(masks) + 13
+    ]
+    keep_ref, send_ref, coarse_ref = refs[len(masks) + 13 : len(masks) + 16]
     lower, upper, pre_one, pre_two, hidden_one, slope_one, hidden_two, slope_two = refs[
-        len(masks) + 13 : len(masks) + 21
+        len(masks) + 16 : len(masks) + 24
     ]
-    raw_all, scale, d_raw_all, d_two_all, d_one_all, total = refs[len(masks) + 21 :]
+    raw_all, scale, d_raw_all, d_two_all, d_one_all, total = refs[len(masks) + 24 :]
     rows, cols = weight.shape
     channels = lower.shape[0] // 12
     width = w2d.shape[0] // 2
@@ -286,20 +311,19 @@
     weight_cols = jnp.concatenate([weight_cols, jnp.zeros((-tiles % 8, cols), F32)], axis=0)
     same = ones_where(iota((cols, cols), 0) // SIDE == iota((cols, cols), 1) // SIDE)
     summed = picked(jnp.concatenate(sums + [weight_cols], axis=0), same)
-    owners = owners_of(owner_ref, position, blocks)
     target = jnp.zeros((POOL_ROWS, blocks), F32)
     held = [(0, sent_ref, 0)]
     for got_ref, mask in zip(got_refs, masks):
         held = held + [(mask ^ other, got_ref, at) for at, (other, _, _) in enumerate(held)]
-    for mask, ref, at in held:
-        places = iota((blocks, blocks), 0) + (position ^ mask) * blocks
+    mine = owners_of(owner_ref, position, blocks)
+    for number, (mask, ref, at) in enumerate(held):
         packed = ref[at * PACK_ROWS : (at + 1) * PACK_ROWS, :]
-        target = target + picked(unpack(packed, blocks), ones_where(places == owners))
-    in_tile = iota((blocks, cols), 0) - iota((blocks, cols), 1) // SIDE
-    spread = jnp.concatenate([ones_where(in_tile == tile * across) for tile in range(tiles)], axis=1)
-    target_cols = picked(target, spread)
-    first = iota((cols, blocks), 0)
-    in_block = iota((cols, blocks), 1) - first // SIDE
+        if (number + 1) * blocks <= picks.shape[0]:
+            chosen = picks[number * blocks : (number + 1) * blocks, :]
+        else:
+            chosen = picks_of(mine, position ^ mask)
+        target = target + picked(unpack(packed, blocks), chosen)
+    target_cols = picked(target, spread[...])
     coarse = jnp.zeros((POOL_ROWS, blocks), F32)
     loss = jnp.zeros((POOL_ROWS, cols), F32)
     valid = iota((POOL_ROWS, cols), 0) < pools
@@ -314,8 +338,7 @@
         d_raw = (wide(d_cols, SIDE // 2) * scale[tile]).astype(BF16)
         d_raw_all[tile] = d_raw
         out_bias = out_bias + over_rows(d_raw.astype(F32))
-        leads = (first % SIDE == 0) & (in_block == tile * across)
-        coarse = coarse + picked(pred, ones_where(leads))
+        coarse = coarse + picked(pred, leads[tile * cols : (tile + 1) * cols, :])
     loss = jnp.sum(jnp.sum(loss, axis=1, keepdims=True), axis=0, keepdims=True) * (1.0 / SIDE)
     coarse_rows = pack(coarse)
     coarse_ref[...] = coarse_rows
@@ -375,6 +398,7 @@
 
 def finish_kernel(
     count_all,
+    strides,
     mine_ref,
     other_ref,
     owner_ref,
@@ -408,9 +432,12 @@
     conv_bias_ref[...] = total[bias_at : bias_at + 1]
     mix_bias_ref[...] = total[bias_at + 8 : bias_at + 9]
     base = position | 1
+    apart = [0]
+    for bit in strides:
+        apart = apart + [bit ^ other for other in apart]
     coarse = jnp.zeros((POOL_ROWS, blocks), F32)
     for peer in range(peers):
-        owners = owners_of(owner_ref, base ^ peer, blocks)
+        owners = owners_of(owner_ref, base ^ apart[peer], blocks)
         places = iota((blocks, blocks), 0) + position * blocks
         values = unpack(gathered[peer * PACK_ROWS : (peer + 1) * PACK_ROWS], blocks)
         got = mm_nt(thirds(values), ones_where(places == owners))
@@ -429,7 +456,7 @@
 def crossed(values, step):
     dp, space = lax.axis_size("dp"), lax.axis_size("space")
     dp_moves = [(bit, 0) for bit in bits_of(dp, 1)]
-    space_moves = [(0, bit) for bit in bits_of(space, 2)]
+    space_moves = [(0, bit) for bit in bits_of(space, 2)[::-1]]
     orders = (dp_moves + space_moves, space_moves + dp_moves)
     pairs = []
     for d in range(dp):
@@ -500,29 +527,21 @@
         ],
         name="pack_edges",
     )(fields, jnp.swapaxes(targets, 0, 1))
-    payload, gots = sent, []
-    for at, mask in enumerate(masks):
-        if mask == 1:
-            payload = jnp.concatenate([held, inner], axis=0)
-        elif at > 0:
-            mine = apart == (mask if mask == 3 else 2 * mask - 1)
-            payload = jnp.concatenate([held, jnp.where(mine, outer, passing)], axis=0)
-        got = swapped(payload, "space", mask)
-        gots.append(got)
-        had = payload.shape[0] - channels
-        held = jnp.concatenate([payload[:had], got[:had]], axis=0)
-        passing = got[had:]
     later, _ = lax.optimization_barrier((fields, sent))
     by_row = jnp.swapaxes(later[0], 0, 1)
-    by_row, _ = lax.optimization_barrier((by_row, gots[0]))
+    got = swapped(sent, "space", masks[0])
+    by_row, got = lax.optimization_barrier((by_row, got))
 
     conv_rows = 9 * channels
     half = conv_rows + width + 2 * POOL_ROWS
     half = (half + 31) // 32 * 16
     cells = SIDE * cols // 2
     f32, bf16 = F32, BF16
+    held_masks = [0]
+    for mask in masks:
+        held_masks = held_masks + [mask ^ other for other in held_masks]
     prepared = pl.pallas_call(
-        prepare_kernel,
+        functools.partial(prepare_kernel, held_masks),
         out_shape=[
             pltpu.VMEM((rows * 3 * channels, cols), bf16),
             pltpu.VMEM((rows, cols), f32),
@@ -533,9 +552,12 @@
             pltpu.VMEM((2 * POOL_ROWS, 2 * width), bf16),
             pltpu.VMEM((4 * width, 4 * POOL_ROWS), bf16),
             pltpu.VMEM((2 * POOL_ROWS, cols), f32),
+            pltpu.VMEM((min(peers, MOST_PICKS) * blocks, blocks), bf16),
+            pltpu.VMEM((blocks, tiles * cols), bf16),
+            pltpu.VMEM((tiles * cols, blocks), bf16),
         ],
         in_specs=[pl.BlockSpec(memory_space=pltpu.VMEM)] * 10,
-        out_specs=[pl.BlockSpec(memory_space=pltpu.VMEM)] * 9,
+        out_specs=[pl.BlockSpec(memory_space=pltpu.VMEM)] * 12,
         compiler_params=pltpu.CompilerParams(vmem_limit_bytes=PREPARE_VMEM),
         cost_estimate=pl.CostEstimate(flops=10**9, bytes_accessed=4 * 10**6, transcendentals=0),
         name="prepare",
@@ -551,6 +573,21 @@
         out_bias.reshape(1, pools),
         owners,
     )
+    payload, gots = sent, []
+    for at, mask in enumerate(masks):
+        if mask == 1:
+            payload = jnp.concatenate([held, inner], axis=0)
+        elif at > 0:
+            mine = apart == (mask if mask == 3 else 2 * mask - 1)
+            payload = jnp.concatenate([held, jnp.where(mine, outer, passing)], axis=0)
+        if at > 0:
+            got = swapped(payload, "space", mask)
+        if at == 1:
+            prepared, got = lax.optimization_barrier((prepared, got))
+        gots.append(got)
+        had = payload.shape[0] - channels
+        held = jnp.concatenate([payload[:had], got[:had]], axis=0)
+        passing = got[had:]
     owners = prepared[2]
     keep, send, coarse = pl.pallas_call(
         functools.partial(step_kernel, count_all, masks, pools),
@@ -559,7 +596,7 @@
             jax.ShapeDtypeStruct((half + PACK_ROWS, width), f32),
             jax.ShapeDtypeStruct((PACK_ROWS, width), f32),
         ],
-        in_specs=[pl.BlockSpec(memory_space=pltpu.VMEM)] * (len(masks) + 10),
+        in_specs=[pl.BlockSpec(memory_space=pltpu.VMEM)] * (len(masks) + 13),
         out_specs=[pl.BlockSpec(memory_space=pltpu.VMEM)] * 3,
         scratch_shapes=[
             pltpu.VMEM((12 * channels, cols), bf16),
@@ -586,7 +623,7 @@
     )
     mine, other = reduce_all(keep, send, coarse)
     outs = pl.pallas_call(
-        functools.partial(finish_kernel, count_all),
+        functools.partial(finish_kernel, count_all, [1] + bits_of(peers, 2)[::-1]),
         out_shape=[
             jax.ShapeDtypeStruct((pools, 1, blocks), f32),
             jax.ShapeDtypeStruct((conv_rows, width), f32),

time: 51.2 us -> 50.8 us (level)
  starting transfers between devices: 14 us -> 13.4 us
    ppermute x4, starting transfers between devices: 8.86 us -> 8.09 us  [crossed(): return lax.ppermute(values, ('dp', 'space'), pairs)]
    ppermute x4, waiting for transfers between devices: 13.9 us -> 14.6 us  [crossed(): return lax.ppermute(values, ('dp', 'space'), pairs)]
    ppermute x5, waiting for transfers between devices: 6.35 us -> 5.68 us  [swapped(): lax.ppermute(values, axis, [(i, i ^ bit) for i in range(lax.axis_size(axi...]
    pallas_call x2, Pallas kernels: 1.7 us -> 2.26 us  [the longest x1 1.21 us: on_device(): pl.pallas_call(functools.partial(prepare_kernel, held_masks), out_shape=[...]
  transfers between devices with their start and end apart: 9 -> 9, of which waited for: 9 -> 9; matrix products, arithmetic and copies ran while one was open for 3% -> 3% of each run, Pallas kernels for 1% -> 2%
where the time goes in v7:
time: 50.8 us; the launch traced here: 50.6 us
  waiting for transfers between devices  20.3 us (40%)
  Pallas kernels  14.4 us (28%)
  starting transfers between devices  13.4 us (26%)
  local copies, waits for them, and re-layouts  1.51 us (3%)
  between operations  0.88 us (2%)
    ppermute x4, waiting for transfers between devices, crossed(): return lax.ppermute(values, ('dp', 'space'), pairs)  14.6 us
    pallas_call x1, Pallas kernels, on_device(): pl.pallas_call(functools.partial(step_kernel, count_all, masks, pools), o...  11 us
    ppermute x4, starting transfers between devices, crossed(): return lax.ppermute(values, ('dp', 'space'), pairs)  8.09 us
    ppermute x5, waiting for transfers between devices, swapped(): lax.ppermute(values, axis, [(i, i ^ bit) for i in range(lax.axis_size(axi...  5.68 us
    ppermute x5, starting transfers between devices, swapped(): lax.ppermute(values, axis, [(i, i ^ bit) for i in range(lax.axis_size(axi...  5.28 us
    optimization_barrier x1, local copies, waits for them, and re-layouts, on_device(): later, _ = lax.optimization_barrier((fields, sent))  1.44 us
    pallas_call x1, Pallas kernels, on_device(): pl.pallas_call(functools.partial(prepare_kernel, held_masks), out_shape=[...  1.21 us
    pallas_call x1, Pallas kernels, on_device(): pl.pallas_call(pack_kernel, out_shape=[pltpu.VMEM((PACK_ROWS + channels,...  1.17 us
  transfers between devices with their start and end apart: 9, of which 9 were waited for; matrix products, arithmetic and copies ran while one was open for 3% of the time, Pallas kernels for 2%

profile of v7, /device:TPU:0, one launch (start us, length us, event | category | flops | bytes accessed | tf_op | source)
XLA Modules:
  0.0 50.6 jit_solution(957533892484622269)
XLA Ops:
  0.6 0.0 copy-start.1
  0.6 0.0 copy-start.2
  0.7 0.0 copy-start
  0.7 1.2 %pack_edges.1 = (f32[56,128]{1,0:T(8,128)S(1)}, f32[32,128]{1,0:T(8,128)S(1)}, f32[32,128]{1,0:T(8,128)S(1)}) custom-call(bf16[1,32,96,128]{3,2,1,0:T(8,128)(2,1)} %fields_ref.1, f32[14,1,192]{2,1,0:T(1,128)} %bitcast.26), custom_call_target="tpu_custom_call" | custom-call | tf_op jit(solution)/shard_map/pack_edges/pallas_call | solution.py:512
  1.9 4.1 %collective-permute-start = (f32[56,128]{1,0:T(8,128)S(1)}, f32[56,128]{1,0:T(8,128)S(1)}, u32[]{:S(2)}, u32[]{:S(2)}) collective-permute-start(f32[56,128]{1,0:T(8,128)S(1)} %get-tuple-element.50.refs_0_), channel_id=1, source_target_pairs={{0,4},{1,5},{2,6},{3,7},{4,0},{5,1},{6,2},{7,3},{8,12},{9,13},{10,... | collective-permute-start | bytes 86024 | tf_op jit(solution)/shard_map/ppermute | solution.py:453
  6.0 1.4 %copy.21 = bf16[1,32,96,128]{3,1,2,0:T(8,128)(2,1)S(1)} copy(bf16[1,32,96,128]{3,2,1,0:T(8,128)(2,1)} %fields_ref.1) | data formatting | bytes 1572864 | tf_op jit(solution)/shard_map/optimization_barrier | solution.py:530
  7.5 0.4 collective-permute-done.refs_1_
  7.9 0.4 collective-permute-start.1
  8.3 0.0 copy-done.6
  8.3 0.0 copy-done.3
  8.3 0.0 copy-done.7
  8.4 0.0 copy-done.5
  8.4 0.0 copy-done.8
  8.4 0.0 copy-done.4
  8.4 1.2 %prepare.1 = (bf16[9216,128]{1,0:T(8,128)(2,1)S(1)}, f32[96,128]{1,0:T(8,128)S(1)}, s32[12,128]{1,0:T(8,128)S(1)}, bf16[256,400]{1,0:T(8,128)(2,1)S(1)}, bf16[25...) custom-call(bf16[96,32,128]{2,1,0:T(8,128)(2,1)S(1)} %bitcast.19, ...), custom_call_target="tpu_custom_call" | custom-call | flops 1000000000 | bytes 4000000 | tf_op jit(solution)/shard_map/prepare/pallas_call | solution.py:543
  9.6 1.8 %collective-permute-done.1.refs_2_ = f32[80,128]{1,0:T(8,128)S(1)} collective-permute-done((f32[80,128]{1,0:T(8,128)S(1)}, f32[80,128]{1,0:T(8,128)S(1)}, u32[]{:S(2)}, u32[]{:S(2)}) %collective-permute-start.1) | collective-permute-done | bytes 40992 | tf_op jit(solution)/shard_map/ppermute | solution.py:453
  11.4 0.3 collective-permute-start.2
  11.7 1.0 %collective-permute-done.2.refs_3_ = f32[128,128]{1,0:T(8,128)S(1)} collective-permute-done((f32[128,128]{1,0:T(8,128)S(1)}, f32[128,128]{1,0:T(8,128)S(1)}, u32[]{:S(2)}, u32[]{:S(2)}) %collective-permute-start.2) | collective-permute-done | bytes 65568 | tf_op jit(solution)/shard_map/ppermute | solution.py:453
  12.7 11.0 %train_step.1 = (f32[224,128]{1,0:T(8,128)S(1)}, f32[248,128]{1,0:T(8,128)S(1)}, f32[24,128]{1,0:T(8,128)S(1)}) custom-call(f32[56,128]{1,0:T(8,128)S(1)} %get-tuple-element.50.refs_0_, f32[56,128]{1,0:T(8,128)S(1)} %collective-permute-done.refs_1_, f32[80,128]{1,0:T(8,128)S(1)} %collective-permute-done.1.refs_2_, ...), custom_call_target="tpu_custom_call" | custom-call | tf_op jit(solution)/shard_map/train_step/pallas_call | solution.py:592
  23.7 0.3 collective-permute-start.3
  24.1 1.1 %collective-permute-done.3 = f32[248,128]{1,0:T(8,128)S(1)} collective-permute-done((f32[248,128]{1,0:T(8,128)S(1)}, f32[248,128]{1,0:T(8,128)S(1)}, u32[]{:S(2)}, u32[]{:S(2)}) %collective-permute-start.3) | collective-permute-done | bytes 127008 | tf_op jit(solution)/shard_map/ppermute | solution.py:453
  25.2 2.4 %collective-permute-start.4 = (f32[272,128]{1,0:T(8,128)S(1)}, f32[272,128]{1,0:T(8,128)S(1)}, u32[]{:S(2)}, u32[]{:S(2)}) collective-permute-start(f32[272,128]{1,0:T(8,128)S(1)} %pad_maximum_fusion.1), channel_id=1, source_target_pairs={{0,8},{1,5},{2,10},{3,7},{4,12},{5,1},{6,14},{7,3},{8,0},{9,13},{1... | collective-permute-start | bytes 417800 | tf_op jit(solution)/shard_map/ppermute | solution.py:466
  27.6 3.0 %collective-permute-done.4 = f32[272,128]{1,0:T(8,128)S(1)} collective-permute-done((f32[272,128]{1,0:T(8,128)S(1)}, f32[272,128]{1,0:T(8,128)S(1)}, u32[]{:S(2)}, u32[]{:S(2)}) %collective-permute-start.4) | collective-permute-done | bytes 139296 | tf_op jit(solution)/shard_map/ppermute | solution.py:466
  30.7 2.1 %collective-permute-start.5 = (f32[320,128]{1,0:T(8,128)S(1)}, f32[320,128]{1,0:T(8,128)S(1)}, u32[]{:S(2)}, u32[]{:S(2)}) collective-permute-start(f32[320,128]{1,0:T(8,128)S(1)} %pad_maximum_fusion), channel_id=1, source_target_pairs={{0,16},{1,3},{2,18},{3,1},{4,20},{5,7},{6,22},{7,5},{8,24},{9,11},... | collective-permute-start | bytes 491528 | tf_op jit(solution)/shard_map/ppermute | solution.py:466
  32.8 3.3 %collective-permute-done.5 = f32[320,128]{1,0:T(8,128)S(1)} collective-permute-done((f32[320,128]{1,0:T(8,128)S(1)}, f32[320,128]{1,0:T(8,128)S(1)}, u32[]{:S(2)}, u32[]{:S(2)}) %collective-permute-start.5) | collective-permute-done | bytes 163872 | tf_op jit(solution)/shard_map/ppermute | solution.py:466
  36.1 2.7 %collective-permute-start.6 = (f32[224,128]{1,0:T(8,128)S(1)}, f32[224,128]{1,0:T(8,128)S(1)}, u32[]{:S(2)}, u32[]{:S(2)}) collective-permute-start(f32[224,128]{1,0:T(8,128)S(1)} %slice_add_fusion), channel_id=1, source_target_pairs={{0,4},{1,9},{2,6},{3,11},{4,0},{5,13},{6,2},{7,15},{8,12},{9,1},{1... | collective-permute-start | bytes 344072 | tf_op jit(solution)/shard_map/ppermute | solution.py:466
  38.9 4.3 %collective-permute-done.6 = f32[224,128]{1,0:T(8,128)S(1)} collective-permute-done((f32[224,128]{1,0:T(8,128)S(1)}, f32[224,128]{1,0:T(8,128)S(1)}, u32[]{:S(2)}, u32[]{:S(2)}) %collective-permute-start.6) | collective-permute-done | bytes 114720 | tf_op jit(solution)/shard_map/ppermute | solution.py:466
  43.1 0.8 %collective-permute-start.7 = (f32[224,128]{1,0:T(8,128)S(1)}, f32[224,128]{1,0:T(8,128)S(1)}, u32[]{:S(2)}, u32[]{:S(2)}) collective-permute-start(f32[224,128]{1,0:T(8,128)S(1)} %add.28), channel_id=1, source_target_pairs={{0,2},{1,17},{2,0},{3,19},{4,6},{5,21},{6,4},{7,23},{8,10},{9,25},... | collective-permute-start | bytes 344072 | tf_op jit(solution)/shard_map/ppermute | solution.py:466
  44.0 4.0 %collective-permute-done.7 = f32[224,128]{1,0:T(8,128)S(1)} collective-permute-done((f32[224,128]{1,0:T(8,128)S(1)}, f32[224,128]{1,0:T(8,128)S(1)}, u32[]{:S(2)}, u32[]{:S(2)}) %collective-permute-start.7) | collective-permute-done | bytes 114720 | tf_op jit(solution)/shard_map/ppermute | solution.py:466
  48.1 0.1 collective-permute-start.8
  48.1 1.5 %collective-permute-done.8.other_ref = f32[416,128]{1,0:T(8,128)S(1)} collective-permute-done((f32[416,128]{1,0:T(8,128)S(1)}, f32[416,128]{1,0:T(8,128)S(1)}, u32[]{:S(2)}, u32[]{:S(2)}) %collective-permute-start.8) | collective-permute-done | bytes 213024 | tf_op jit(solution)/shard_map/ppermute | solution.py:453
  49.6 1.0 %finish.1 = (f32[14,1,192]{2,1,0:T(1,128)}, f32[288,128]{1,0:T(8,128)}, f32[1,128]{1,0:T(1,128)}, f32[128,128]{1,0:T(8,128)}, f32[1,128]{1,0:T(1,128)}, /*index=...) custom-call(f32[416,128]{1,0:T(8,128)S(1)} %slice_dynamic-update-slice_fusion.mine_ref, ...), custom_call_target="tpu_custom_call" | custom-call | tf_op jit(solution)/shard_map/finish/pallas_call | solution.py:625
  (28 shorter events, 0.2 us)
Async XLA Ops:
  0.6 7.7 %copy-start.1 = (f32[96,128]{1,0:T(8,128)S(1)}, f32[96,128]{1,0:T(8,128)}, u32[]{:S(2)}) copy-start(f32[96,128]{1,0:T(8,128)} %frac_ref.1) | copy-start | bytes 147460
  0.6 7.7 %copy-start.2 = (s32[96,128]{1,0:T(8,128)S(1)}, s32[96,128]{1,0:T(8,128)}, u32[]{:S(2)}) copy-start(s32[96,128]{1,0:T(8,128)} %mask_ref.1) | copy-start | bytes 147460
  0.7 7.7 %copy-start = (bf16[3,3,32,128]{3,2,1,0:T(8,128)(2,1)S(1)}, bf16[3,3,32,128]{3,2,1,0:T(8,128)(2,1)}, u32[]{:S(2)}) copy-start(bf16[3,3,32,128]{3,2,1,0:T(8,128)(2,1)} %param.16) | copy-start | bytes 221188
  0.7 7.7 %copy-start.6 = (f32[128]{0:T(128)S(1)}, f32[128]{0:T(128)}, u32[]{:S(2)}) copy-start(f32[128]{0:T(128)} %param.17) | copy-start | bytes 1540
  0.7 7.7 %copy-start.3 = (bf16[128,128]{1,0:T(8,128)(2,1)S(1)}, bf16[128,128]{1,0:T(8,128)(2,1)}, u32[]{:S(2)}) copy-start(bf16[128,128]{1,0:T(8,128)(2,1)} %w2_ref.1) | copy-start | bytes 98308
  0.7 7.7 %copy-start.7 = (f32[128]{0:T(128)S(1)}, f32[128]{0:T(128)}, u32[]{:S(2)}) copy-start(f32[128]{0:T(128)} %param.19) | copy-start | bytes 1540
  0.7 7.7 %copy-start.5 = (bf16[128,14]{0,1:T(8,128)(2,1)S(1)}, bf16[128,14]{0,1:T(8,128)(2,1)}, u32[]{:S(2)}) copy-start(bf16[128,14]{0,1:T(8,128)(2,1)} %param.20) | copy-start | bytes 10756
  0.7 7.7 %copy-start.8 = (f32[14]{0:T(128)S(1)}, f32[14]{0:T(128)}, u32[]{:S(2)}) copy-start(f32[14]{0:T(128)} %param.21) | copy-start | bytes 172
  0.7 7.7 %copy-start.4 = (s32[1536]{0:T(1024)S(1)}, s32[1536]{0:T(1024)}, u32[]{:S(2)}) copy-start(s32[1536]{0:T(1024)} %param.14) | copy-start | bytes 18436
  1.9 6.0 %collective-permute-start = (f32[56,128]{1,0:T(8,128)S(1)}, f32[56,128]{1,0:T(8,128)S(1)}, u32[]{:S(2)}, u32[]{:S(2)}) collective-permute-start(f32[56,128]{1,0:T(8,128)S(1)} %get-tuple-element.50.refs_0_), channel_id=1, source_target_pairs={{0,4},{1,5},{2,6},{3,7},{4,0},{5,1},{6,2},{7,3},{8,12},{9,13},{10,... | collective-permute-start | bytes 86024 | tf_op jit(solution)/shard_map/ppermute | solution.py:453
  7.9 3.5 %collective-permute-start.1 = (f32[80,128]{1,0:T(8,128)S(1)}, f32[80,128]{1,0:T(8,128)S(1)}, u32[]{:S(2)}, u32[]{:S(2)}) collective-permute-start(f32[80,128]{1,0:T(8,128)S(1)} %pad_maximum_fusion.3), channel_id=1, source_target_pairs={{0,3},{1,2},{2,1},{3,0},{4,7},{5,6},{6,5},{7,4},{8,11},{9,10},{10,... | collective-permute-start | bytes 122888 | tf_op jit(solution)/shard_map/ppermute | solution.py:453
  11.4 1.3 %collective-permute-start.2 = (f32[128,128]{1,0:T(8,128)S(1)}, f32[128,128]{1,0:T(8,128)S(1)}, u32[]{:S(2)}, u32[]{:S(2)}) collective-permute-start(f32[128,128]{1,0:T(8,128)S(1)} %pad_maximum_fusion.2), channel_id=1, source_target_pairs={{0,1},{1,0},{2,3},{3,2},{4,5},{5,4},{6,7},{7,6},{8,9},{9,8},{10,11... | collective-permute-start | bytes 196616 | tf_op jit(solution)/shard_map/ppermute | solution.py:453
  23.7 1.4 %collective-permute-start.3 = (f32[248,128]{1,0:T(8,128)S(1)}, f32[248,128]{1,0:T(8,128)S(1)}, u32[]{:S(2)}, u32[]{:S(2)}) collective-permute-start(f32[248,128]{1,0:T(8,128)S(1)} %get-tuple-element.82), channel_id=1, source_target_pairs={{0,1},{1,0},{2,3},{3,2},{4,5},{5,4},{6,7},{7,6},{8,9},{9,8},{10,11... | collective-permute-start | bytes 380936 | tf_op jit(solution)/shard_map/ppermute | solution.py:453
  25.2 5.5 %collective-permute-start.4 = (f32[272,128]{1,0:T(8,128)S(1)}, f32[272,128]{1,0:T(8,128)S(1)}, u32[]{:S(2)}, u32[]{:S(2)}) collective-permute-start(f32[272,128]{1,0:T(8,128)S(1)} %pad_maximum_fusion.1), channel_id=1, source_target_pairs={{0,8},{1,5},{2,10},{3,7},{4,12},{5,1},{6,14},{7,3},{8,0},{9,13},{1... | collective-permute-start | bytes 417800 | tf_op jit(solution)/shard_map/ppermute | solution.py:466
  30.7 5.4 %collective-permute-start.5 = (f32[320,128]{1,0:T(8,128)S(1)}, f32[320,128]{1,0:T(8,128)S(1)}, u32[]{:S(2)}, u32[]{:S(2)}) collective-permute-start(f32[320,128]{1,0:T(8,128)S(1)} %pad_maximum_fusion), channel_id=1, source_target_pairs={{0,16},{1,3},{2,18},{3,1},{4,20},{5,7},{6,22},{7,5},{8,24},{9,11},... | collective-permute-start | bytes 491528 | tf_op jit(solution)/shard_map/ppermute | solution.py:466
  36.1 7.0 %collective-permute-start.6 = (f32[224,128]{1,0:T(8,128)S(1)}, f32[224,128]{1,0:T(8,128)S(1)}, u32[]{:S(2)}, u32[]{:S(2)}) collective-permute-start(f32[224,128]{1,0:T(8,128)S(1)} %slice_add_fusion), channel_id=1, source_target_pairs={{0,4},{1,9},{2,6},{3,11},{4,0},{5,13},{6,2},{7,15},{8,12},{9,1},{1... | collective-permute-start | bytes 344072 | tf_op jit(solution)/shard_map/ppermute | solution.py:466
  43.1 4.9 %collective-permute-start.7 = (f32[224,128]{1,0:T(8,128)S(1)}, f32[224,128]{1,0:T(8,128)S(1)}, u32[]{:S(2)}, u32[]{:S(2)}) collective-permute-start(f32[224,128]{1,0:T(8,128)S(1)} %add.28), channel_id=1, source_target_pairs={{0,2},{1,17},{2,0},{3,19},{4,6},{5,21},{6,4},{7,23},{8,10},{9,25},... | collective-permute-start | bytes 344072 | tf_op jit(solution)/shard_map/ppermute | solution.py:466
  48.1 1.5 %collective-permute-start.8 = (f32[416,128]{1,0:T(8,128)S(1)}, f32[416,128]{1,0:T(8,128)S(1)}, u32[]{:S(2)}, u32[]{:S(2)}) collective-permute-start(f32[416,128]{1,0:T(8,128)S(1)} %slice_dynamic-update-slice_fusion.mine_ref), channel_id=1, source_target_pairs={{0,1},{1,0},{2,3},{3,2},{4,5},{5,4},{6,7},{7,6},{8,9},{9,8},{10,11... | collective-permute-start | bytes 638984 | tf_op jit(solution)/shard_map/ppermute | solution.py:453
